TPU v7x, 512 devices: a whole 4x8x8 slice. The times are simulated.
512 devices in a mesh: batch: 32 (over z, x), blk: 16 (over y, core).
Axes of the slice: x: 4, y: 8, z: 8, core: 2. Of those that a mesh axis runs over, the one named last changes fastest.
Arguments:
- points: float32 [1024, 16, 3, 256], P('batch', 'blk'), may hold values from -6 to 6
- centers: float32 [1024, 16, 3, 384], P('batch', 'blk'), may hold values from -6 to 6
- exponents: float32 [1024, 16, 384], P('batch', 'blk'), may hold values from 0.1 to 1
- angular: float32 [1024, 16, 3, 384], P('batch', 'blk'), may hold values from -3 to 3
- grid_weights: float32 [1024, 16, 256], P('batch', 'blk'), may hold values from 0.001 to 0.01
- hartree: float32 [1024, 16, 256], P('batch', 'blk'), may hold values from 0 to 1.7
- load_plan: int32 [16, 1024], P('blk'), may hold values from 0 to 1023, each once within a row
- density_blocks: bfloat16 [256, 128, 128], P('blk'), may hold values from -0.046875 to 0.046875
- pair_lists: int32 [32, 16, 16, 2], P('batch', 'blk'), may hold values from 0 to 15
- batch_pairs: int32 [1024, 16, 9], P('batch', 'blk'), may hold values from 0 to 31, as said below
Outputs:
- hamiltonian: float32 [256, 128, 128], P('blk')
- density: float32 [1024, 16, 256], P('batch', 'blk')
Inputs may be any that keep to these rules, and one draw needn't show every extreme that they name: Each row of load_plan names every storage row of its column once. `pair_lists`: local index of a block pair within the 16 pairs held by one index of blk. `batch_pairs`: entry e of a device's table is the (e % 2)-th block it reads from index e // 2 of blk; every entry of a device's table is named by some pair of its batches.
All inputs are finite; a program needn't handle non-finite values.
Results may differ from a plain program's by a relative error of at most 0.0065.
Values may be sent and summed in bfloat16 or wider, within the bound.
No kernel may reach another device: no remote copies, remote signals or barrier semaphores. Data moves between devices by JAX's collectives and lax.ppermute only.
A program may use at most 64 MiB of HBM per device.

v0:
```python
import jax
import jax.numpy as jnp
from jax import lax
from jax.sharding import PartitionSpec as P

LIST = 3


xc_scale = 0.98474502
soft_square = 0.01


def exchange_potential(grid_rho):
    return -xc_scale * jnp.power(grid_rho * grid_rho + soft_square, 1.0 / 6.0)


def evaluate(points, centers, exponents, angular):
    distance = jnp.zeros(points.shape[:-2] + (points.shape[-1], centers.shape[-1]), jnp.float32)
    angular_part = jnp.ones_like(distance)
    for component in range(3):
        delta = points[..., component, :, None] - centers[..., component, None, :]
        distance = distance + delta * delta
        angular_part = angular_part + angular[..., component, None, :] * delta
    return (jnp.exp(-exponents[..., None, :] * distance) * angular_part).astype(jnp.bfloat16)


def on_device(
    points,
    centers,
    exponents,
    angular,
    grid_weights,
    hartree,
    load_plan,
    density_blocks,
    pair_lists,
    batch_pairs,
):
    slot_count = points.shape[0]
    grid_size = points.shape[3]
    columns = lax.axis_size("blk")
    per_owner = pair_lists.shape[3]
    held_pairs = density_blocks.shape[0]
    block_size = density_blocks.shape[1]
    entries = columns * per_owner
    list_size = LIST
    basis_width = list_size * block_size
    batch_rank = lax.axis_index("batch")
    plan_rows = lax.dynamic_slice_in_dim(load_plan[0], batch_rank * slot_count, slot_count)
    stored = lax.all_gather(hartree[:, 0, :], "batch", axis=0, tiled=True)
    potential = stored[plan_rows]
    wanted = pair_lists[0, 0]
    asked_slots = lax.all_to_all(wanted, "blk", split_axis=0, concat_axis=0, tiled=True)
    owner_base = jnp.arange(entries, dtype=jnp.int32) // per_owner * held_pairs
    global_ids = owner_base + wanted.reshape(entries)
    blank_table = jnp.zeros((entries, block_size, block_size), jnp.bfloat16)
    piece = lax.all_gather(density_blocks, "blk", axis=0, tiled=True)
    inside = (global_ids >= 0) & (global_ids < piece.shape[0])
    chosen = piece[jnp.clip(global_ids, 0, piece.shape[0] - 1)]
    fetched = jnp.where(inside[:, None, None], chosen, blank_table)
    group_size = 4
    loop_turns = slot_count // group_size

    def take_rows(value, turn_index):
        return lax.dynamic_slice_in_dim(value, turn_index * group_size, group_size, 0)

    def integrate(partial_table, turn_index):
        basis = evaluate(
            take_rows(points, turn_index)[:, 0],
            take_rows(centers, turn_index)[:, 0],
            take_rows(exponents, turn_index)[:, 0],
            take_rows(angular, turn_index)[:, 0],
        )
        slot_refs = take_rows(batch_pairs, turn_index)[:, 0]
        blocks = fetched[slot_refs]
        sub_density = (
            blocks.reshape(group_size, list_size, list_size, block_size, block_size)
            .transpose(0, 1, 3, 2, 4)
            .reshape(group_size, basis_width, basis_width)
        )
        inner = jnp.einsum("gpm,gmn->gpn", basis, sub_density, preferred_element_type=jnp.float32)
        grid_rho = jnp.sum(inner * basis.astype(jnp.float32), axis=-1)
        effective = take_rows(potential, turn_index) + exchange_potential(grid_rho)
        weight_rows = take_rows(grid_weights, turn_index)[:, 0]
        scaled = ((weight_rows * effective)[..., None] * basis.astype(jnp.float32)).astype(
            jnp.bfloat16
        )
        full_blocks = jnp.einsum("gpm,gpn->gmn", basis, scaled, preferred_element_type=jnp.float32)
        contributions = (
            full_blocks.reshape(group_size, list_size, block_size, list_size, block_size)
            .transpose(0, 1, 3, 2, 4)
            .reshape(group_size * list_size * list_size, block_size, block_size)
        )
        partial_table = partial_table.at[slot_refs.reshape(-1)].add(contributions)
        return (partial_table, grid_rho)

    zero_table = jnp.zeros((entries, block_size, block_size), jnp.float32)
    partial_table, rho_groups = lax.scan(integrate, zero_table, jnp.arange(loop_turns))
    grid_rho = rho_groups.reshape(slot_count, grid_size)
    received = lax.all_to_all(
        partial_table.reshape(columns, per_owner, block_size, block_size),
        "blk",
        split_axis=0,
        concat_axis=0,
        tiled=True,
    )
    owned_sums = (
        jnp.zeros((held_pairs, block_size, block_size), jnp.float32)
        .at[asked_slots.reshape(entries)]
        .add(received.reshape(entries, block_size, block_size))
    )
    hamiltonian = lax.psum(owned_sums, "batch")
    batch_total = load_plan.shape[1]
    placement = (plan_rows[None, :] == jnp.arange(batch_total, dtype=jnp.int32)[:, None]).astype(
        jnp.float32
    )
    spread_rows = jnp.dot(
        placement, grid_rho, precision=lax.Precision.HIGHEST, preferred_element_type=jnp.float32
    )
    density = lax.psum_scatter(spread_rows, "batch", scatter_dimension=0, tiled=True)
    return (hamiltonian, density[:, None, :])


def solution(mesh):
    return jax.shard_map(
        on_device,
        mesh=mesh,
        in_specs=(
            P("batch", "blk", None, None),
            P("batch", "blk", None, None),
            P("batch", "blk", None),
            P("batch", "blk", None, None),
            P("batch", "blk", None),
            P("batch", "blk", None),
            P("blk", None),
            P("blk", None, None),
            P("batch", "blk", None, None),
            P("batch", "blk", None),
        ),
        out_specs=(P("blk", None, None), P("batch", "blk", None)),
        check_vma=False,
    )
```

profile of v0, /device:TPU:24, one launch (start us, length us, event | category | flops | bytes accessed | tf_op | source)
XLA Modules:
  0.0 800.7 jit_solution(2311108223574678586)
XLA Ops:
  10.7 8.9 %all-to-all-start = ((s32[16,1,2]{2,1,0:T(1,128)}), s32[16,1,2]{2,1,0:T(1,128)S(1)}, u32[]{:S(2)}, u32[]{:S(2)}) async-start(s32[16,1,2]{2,1,0:T(1,128)} %copy.56), calls=%async_computation | async-start | bytes 16384 | tf_op jit(solution)/shard_map/all_to_all | solution.py:53
  22.1 76.3 %all-gather.6.cloned.1.call-done = f32[1024,1,256]{2,0,1:T(8,128)} async-done(((f32[32,1,256]{2,0,1:T(8,128)}), f32[1024,1,256]{2,0,1:T(8,128)}) %all-gather.6.cloned.1.call-update) | async-done | bytes 1048592 | tf_op jit(solution)/shard_map/all_gather | solution.py:50
  100.2 55.6 %all-gather.4.cloned.1.call-done = bf16[256,128,128]{2,1,0:T(8,128)(2,1)} async-done(((bf16[16,128,128]{2,1,0:T(8,128)(2,1)}), bf16[256,128,128]{2,1,0:T(8,128)(2,1)}) %all-gather.4.cloned.1.call-update) | async-done | bytes 8388624 | tf_op jit(solution)/shard_map/all_gather | solution.py:57
  155.8 4.1 gather_fusion.2
  161.7 235.0 %while.12 = (s32[]{:T(128)}, f32[32,128,128]{2,1,0:T(8,128)}, f32[8,4,256]{2,1,0:T(4,128)S(1)}, s32[8]{0:T(128)S(1)}, s32[32,1,9]{2,0,1:T(8,128)S(1)}, /*index=5...) while((s32[]{:T(128)}, f32[32,128,128]{2,1,0:T(8,128)}, ...), condition=%wide.region_3.4_spmd, body=%wide.region_0.3_spmd.sunk | while | flops 633674496 | bytes 35997664 | solution.py:98
  171.9 4.2 fusion.51
  176.1 3.5 reshape.302
  181.4 9.7 %scatter_fusion = f32[32,128,128]{2,1,0:T(8,128)} fusion(f32[32,128,128]{2,1,0:T(8,128)} %get-tuple-element.276, s32[36]{0:T(128)S(1)} %fusion.47, f32[36,128,128]{2,1,0:T(8,128)} %bitcast.106), kind=kCustom, calls=%fused_computation.3.clone.1 | custom fusion | flops 589824 | bytes 7078032 | tf_op jit(solution)/shard_map/while/body/eval_jaxpr/scatter-add | solution.py:94
  201.2 4.2 fusion.51
  205.5 3.5 reshape.302
  210.7 9.7 %scatter_fusion = f32[32,128,128]{2,1,0:T(8,128)} fusion(f32[32,128,128]{2,1,0:T(8,128)} %get-tuple-element.276, s32[36]{0:T(128)S(1)} %fusion.47, f32[36,128,128]{2,1,0:T(8,128)} %bitcast.106), kind=kCustom, calls=%fused_computation.3.clone.1 | custom fusion | flops 589824 | bytes 7078032 | tf_op jit(solution)/shard_map/while/body/eval_jaxpr/scatter-add | solution.py:94
  230.6 4.2 fusion.51
  234.8 3.5 reshape.302
  240.1 9.7 %scatter_fusion = f32[32,128,128]{2,1,0:T(8,128)} fusion(f32[32,128,128]{2,1,0:T(8,128)} %get-tuple-element.276, s32[36]{0:T(128)S(1)} %fusion.47, f32[36,128,128]{2,1,0:T(8,128)} %bitcast.106), kind=kCustom, calls=%fused_computation.3.clone.1 | custom fusion | flops 589824 | bytes 7078032 | tf_op jit(solution)/shard_map/while/body/eval_jaxpr/scatter-add | solution.py:94
  260.1 4.2 fusion.51
  264.3 3.5 reshape.302
  269.6 9.6 %scatter_fusion = f32[32,128,128]{2,1,0:T(8,128)} fusion(f32[32,128,128]{2,1,0:T(8,128)} %get-tuple-element.276, s32[36]{0:T(128)S(1)} %fusion.47, f32[36,128,128]{2,1,0:T(8,128)} %bitcast.106), kind=kCustom, calls=%fused_computation.3.clone.1 | custom fusion | flops 589824 | bytes 7078032 | tf_op jit(solution)/shard_map/while/body/eval_jaxpr/scatter-add | solution.py:94
  289.4 4.2 fusion.51
  293.7 3.5 reshape.302
  298.9 9.7 %scatter_fusion = f32[32,128,128]{2,1,0:T(8,128)} fusion(f32[32,128,128]{2,1,0:T(8,128)} %get-tuple-element.276, s32[36]{0:T(128)S(1)} %fusion.47, f32[36,128,128]{2,1,0:T(8,128)} %bitcast.106), kind=kCustom, calls=%fused_computation.3.clone.1 | custom fusion | flops 589824 | bytes 7078032 | tf_op jit(solution)/shard_map/while/body/eval_jaxpr/scatter-add | solution.py:94
  318.8 4.2 fusion.51
  323.0 3.5 reshape.302
  328.3 9.6 %scatter_fusion = f32[32,128,128]{2,1,0:T(8,128)} fusion(f32[32,128,128]{2,1,0:T(8,128)} %get-tuple-element.276, s32[36]{0:T(128)S(1)} %fusion.47, f32[36,128,128]{2,1,0:T(8,128)} %bitcast.106), kind=kCustom, calls=%fused_computation.3.clone.1 | custom fusion | flops 589824 | bytes 7078032 | tf_op jit(solution)/shard_map/while/body/eval_jaxpr/scatter-add | solution.py:94
  348.2 4.2 fusion.51
  352.4 3.5 reshape.302
  357.7 9.7 %scatter_fusion = f32[32,128,128]{2,1,0:T(8,128)} fusion(f32[32,128,128]{2,1,0:T(8,128)} %get-tuple-element.276, s32[36]{0:T(128)S(1)} %fusion.47, f32[36,128,128]{2,1,0:T(8,128)} %bitcast.106), kind=kCustom, calls=%fused_computation.3.clone.1 | custom fusion | flops 589824 | bytes 7078032 | tf_op jit(solution)/shard_map/while/body/eval_jaxpr/scatter-add | solution.py:94
  377.6 4.2 fusion.51
  387.0 9.7 %scatter_fusion = f32[32,128,128]{2,1,0:T(8,128)} fusion(f32[32,128,128]{2,1,0:T(8,128)} %get-tuple-element.276, s32[36]{0:T(128)S(1)} %fusion.47, f32[36,128,128]{2,1,0:T(8,128)} %bitcast.106), kind=kCustom, calls=%fused_computation.3.clone.1 | custom fusion | flops 589824 | bytes 7078032 | tf_op jit(solution)/shard_map/while/body/eval_jaxpr/scatter-add | solution.py:94
  396.7 5.4 all-to-all-start.1
  405.8 45.0 %all-to-all-done.1 = f32[16,2,128,128]{3,2,1,0:T(8,128)S(1)} async-done(((f32[16,2,128,128]{3,2,1,0:T(8,128)}), f32[16,2,128,128]{3,2,1,0:T(8,128)S(1)}, u32[]{:S(2)}, u32[]{:S(2)}) %all-to-all-start.1) | async-done | bytes 2097184 | tf_op jit(solution)/shard_map/all_to_all | solution.py:100
  454.6 174.8 %reduce-scatter.2.cloned.1.call-done = f32[32,256]{1,0:T(8,128)} async-done(((f32[1024,256]{1,0:T(8,128)}), f32[32,256]{1,0:T(8,128)}) %reduce-scatter.2.cloned.1.call-update) | async-done | bytes 32784 | tf_op jit(solution)/shard_map/reduce_scatter | solution.py:120
  630.8 161.1 %all-reduce.2.cloned.1.call-done = f32[16,128,128]{2,1,0:T(8,128)} async-done(((f32[16,128,128]{2,1,0:T(8,128)}), f32[16,128,128]{2,1,0:T(8,128)}) %all-reduce.2.cloned.1.call-update) | async-done | bytes 1048592 | tf_op jit(solution)/shard_map/psum | solution.py:112
  (263 shorter events, 114.2 us)
Async XLA Ops:
  7.2 91.2 %all-gather.6.cloned.1.call-start = ((), (), s32[]{:S(2)}) async-start(), calls=%async_computation.6 | async-start | bytes 1081344 | tf_op jit(solution)/shard_map/all_gather | solution.py:50
  8.6 147.2 %all-gather.4.cloned.1.call-start = ((), (), s32[]{:S(2)}) async-start(), calls=%async_computation.3 | async-start | bytes 8912896 | tf_op jit(solution)/shard_map/all_gather | solution.py:57
  10.7 386.0 %all-to-all-start = ((s32[16,1,2]{2,1,0:T(1,128)}), s32[16,1,2]{2,1,0:T(1,128)S(1)}, u32[]{:S(2)}, u32[]{:S(2)}) async-start(s32[16,1,2]{2,1,0:T(1,128)} %copy.56), calls=%async_computation | async-start | bytes 16384 | tf_op jit(solution)/shard_map/all_to_all | solution.py:53
  161.7 3.8 copy-start
  181.4 9.7 %copy-start.1 = (bf16[32,128,128]{2,1,0:T(8,128)(2,1)S(1)}, bf16[32,128,128]{2,1,0:T(8,128)(2,1)}, u32[]{:S(2)}) copy-start(bf16[32,128,128]{2,1,0:T(8,128)(2,1)} %copy-done) | copy-start | bytes 3145732 | tf_op jit(solution)/shard_map/while
  191.0 3.8 copy-start
  210.7 9.7 %copy-start.1 = (bf16[32,128,128]{2,1,0:T(8,128)(2,1)S(1)}, bf16[32,128,128]{2,1,0:T(8,128)(2,1)}, u32[]{:S(2)}) copy-start(bf16[32,128,128]{2,1,0:T(8,128)(2,1)} %copy-done) | copy-start | bytes 3145732 | tf_op jit(solution)/shard_map/while
  220.4 3.8 copy-start
  240.1 9.8 %copy-start.1 = (bf16[32,128,128]{2,1,0:T(8,128)(2,1)S(1)}, bf16[32,128,128]{2,1,0:T(8,128)(2,1)}, u32[]{:S(2)}) copy-start(bf16[32,128,128]{2,1,0:T(8,128)(2,1)} %copy-done) | copy-start | bytes 3145732 | tf_op jit(solution)/shard_map/while
  249.9 3.8 copy-start
  269.6 9.7 %copy-start.1 = (bf16[32,128,128]{2,1,0:T(8,128)(2,1)S(1)}, bf16[32,128,128]{2,1,0:T(8,128)(2,1)}, u32[]{:S(2)}) copy-start(bf16[32,128,128]{2,1,0:T(8,128)(2,1)} %copy-done) | copy-start | bytes 3145732 | tf_op jit(solution)/shard_map/while
  279.2 3.8 copy-start
  298.9 9.7 %copy-start.1 = (bf16[32,128,128]{2,1,0:T(8,128)(2,1)S(1)}, bf16[32,128,128]{2,1,0:T(8,128)(2,1)}, u32[]{:S(2)}) copy-start(bf16[32,128,128]{2,1,0:T(8,128)(2,1)} %copy-done) | copy-start | bytes 3145732 | tf_op jit(solution)/shard_map/while
  308.6 3.8 copy-start
  328.3 9.6 %copy-start.1 = (bf16[32,128,128]{2,1,0:T(8,128)(2,1)S(1)}, bf16[32,128,128]{2,1,0:T(8,128)(2,1)}, u32[]{:S(2)}) copy-start(bf16[32,128,128]{2,1,0:T(8,128)(2,1)} %copy-done) | copy-start | bytes 3145732 | tf_op jit(solution)/shard_map/while
  338.0 3.8 copy-start
  357.7 9.7 %copy-start.1 = (bf16[32,128,128]{2,1,0:T(8,128)(2,1)S(1)}, bf16[32,128,128]{2,1,0:T(8,128)(2,1)}, u32[]{:S(2)}) copy-start(bf16[32,128,128]{2,1,0:T(8,128)(2,1)} %copy-done) | copy-start | bytes 3145732 | tf_op jit(solution)/shard_map/while
  367.3 3.8 copy-start
  387.0 9.7 %copy-start.1 = (bf16[32,128,128]{2,1,0:T(8,128)(2,1)S(1)}, bf16[32,128,128]{2,1,0:T(8,128)(2,1)}, u32[]{:S(2)}) copy-start(bf16[32,128,128]{2,1,0:T(8,128)(2,1)} %copy-done) | copy-start | bytes 3145732 | tf_op jit(solution)/shard_map/while
  396.7 54.1 %all-to-all-start.1 = ((f32[16,2,128,128]{3,2,1,0:T(8,128)}), f32[16,2,128,128]{3,2,1,0:T(8,128)S(1)}, u32[]{:S(2)}, u32[]{:S(2)}) async-start(f32[16,2,128,128]{3,2,1,0:T(8,128)} %bitcast.108), calls=%async_computation.1 | async-start | bytes 4194304 | tf_op jit(solution)/shard_map/all_to_all | solution.py:100
  402.1 227.3 %reduce-scatter.2.cloned.1.call-start = ((), (), s32[]{:S(2)}) async-start(), calls=%async_computation.5 | async-start | bytes 1081344 | tf_op jit(solution)/shard_map/reduce_scatter | solution.py:120
  404.4 387.4 %all-reduce.2.cloned.1.call-start = ((), (), s32[]{:S(2)}) async-start(), calls=%async_computation.4 | async-start | bytes 2097152 | tf_op jit(solution)/shard_map/psum | solution.py:112
  453.6 1.0 copy-start.2
Sparse Core Ops, SparseCore 0:
  11.7 86.6 all-gather.5
  100.5 55.2 all-gather.3
  407.3 222.0 reduce-scatter.1
  633.2 158.5 all-reduce.1
where the time goes:
time: 804 us; the launch traced here: 801 us
  waiting for transfers between devices  514 us (64%)
  local copies, waits for them, and re-layouts  112 us (14%)
  other arithmetic  82 us (10%)
  matrix products  58.4 us (7%)
  starting transfers between devices  14.4 us (2%)
  between operations  13.9 us (2%)
    reduce_scatter x1, waiting for transfers between devices, on_device(): lax.psum_scatter(spread_rows, 'batch', scatter_dimension=0, tiled=True)  175 us
    psum x1, waiting for transfers between devices, on_device(): hamiltonian = lax.psum(owned_sums, 'batch')  161 us
    scatter-add x8, other arithmetic, integrate(): partial_table = partial_table.at[slot_refs.reshape(-1)].add(contributions)  77.4 us
    all_gather x1, waiting for transfers between devices, on_device(): stored = lax.all_gather(hartree[:, 0, :], 'batch', axis=0, tiled=True)  76.3 us
    all_gather x1, waiting for transfers between devices, on_device(): piece = lax.all_gather(density_blocks, 'blk', axis=0, tiled=True)  55.6 us
    all_to_all x1, waiting for transfers between devices, on_device(): lax.all_to_all(partial_table.reshape(columns, per_owner, block_size, bloc...  45 us
    dot_general x8, matrix products, integrate(): jnp.einsum('gpm,gpn->gmn', basis, scaled, preferred_element_type=jnp.floa...  33.7 us
    reshape x8, local copies, waits for them, and re-layouts, integrate(): full_blocks.reshape(group_size, list_size, block_size, list_size, block_s...  27.7 us
  transfers between devices with their start and end apart: 6, of which 5 were waited for; matrix products, arithmetic and copies ran while one was open for 31% of the time, Pallas kernels for 0%

commit v1 on v0

v1 whole, which is shorter than its diff:
```python
import jax
import jax.numpy as jnp
from jax import lax
from jax.experimental import pallas as pl
from jax.experimental.pallas import tpu as pltpu
from jax.sharding import PartitionSpec as P

LIST = 3
xc_scale = 0.98474502
soft_square = 0.01
log2_e = 1.4426950408889634

bf16 = jnp.bfloat16
f32 = jnp.float32
VMEM = pl.BlockSpec(memory_space=pltpu.VMEM)
SMEM = pl.BlockSpec(memory_space=pltpu.SMEM)


def call(body, outs, ins, scratch=(), flops=0, moved=0, limit=24):
    return pl.pallas_call(
        body,
        out_shape=outs,
        in_specs=ins,
        out_specs=jax.tree.map(lambda _: VMEM, outs),
        scratch_shapes=list(scratch),
        compiler_params=pltpu.CompilerParams(vmem_limit_bytes=limit * 2**20),
        cost_estimate=pl.CostEstimate(flops=flops, bytes_accessed=moved, transcendentals=0),
    )


def basis_kernel(points_ref, params_ref, out_ref):
    slots, width, _ = out_ref.shape
    step = 32

    def one(s, carry):
        columns = jnp.transpose(params_ref[s])
        for at in range(0, width, step):
            own = columns[at : at + step]
            distance = None
            angular = None
            for a in range(3):
                delta = points_ref[s, a : a + 1, :] - own[:, a : a + 1]
                square = delta * delta
                slope = own[:, 4 + a : 5 + a] * delta
                distance = square if a == 0 else distance + square
                angular = slope + 1.0 if a == 0 else angular + slope
            value = jnp.exp2((own[:, 3:4] * -log2_e) * distance) * angular
            out_ref[s, at : at + step, :] = value.astype(bf16)
        return carry

    lax.fori_loop(0, slots, one, 0)


def pick_kernel(asked_ref, blocks_ref, out_ref):
    for e in range(out_ref.shape[0]):
        out_ref[e] = blocks_ref[asked_ref[e]]


def integrate_kernel(
    pairs_ref, plan_ref, basis_ref, table_ref, hartree_ref, weights_ref,
    out_ref, rho_ref, sub_ref, sums_ref,
):
    slots = basis_ref.shape[0]
    entries, block, _ = table_ref.shape
    unroll = sub_ref.shape[0]

    def clear(e, carry):
        sums_ref[e] = jnp.zeros((block, block), f32)
        return carry

    lax.fori_loop(0, entries, clear, 0)

    def group(turn, carry):
        for u in range(unroll):
            s = turn * unroll + u
            for k in range(LIST):
                for l in range(LIST):
                    sub_ref[u, k * block : (k + 1) * block, l * block : (l + 1) * block] = table_ref[
                        pairs_ref[s * LIST * LIST + k * LIST + l]
                    ]
        for u in range(unroll):
            s = turn * unroll + u
            basis = basis_ref[s]
            inner = jnp.dot(sub_ref[u], basis, preferred_element_type=f32)
            wide = basis.astype(f32)
            rho = jnp.sum(inner * wide, axis=0, keepdims=True)
            rho_ref[pl.ds(s, 1), :] = rho
            root = jnp.exp2(jnp.log2(rho * rho + soft_square) * (1.0 / 6.0))
            effective = hartree_ref[pl.ds(plan_ref[s], 1), :] - xc_scale * root
            scaled = (wide * (weights_ref[pl.ds(s, 1), :] * effective)).astype(bf16)
            full = lax.dot_general(
                basis, scaled, (((1,), (1,)), ((), ())), preferred_element_type=f32
            )
            for k in range(LIST):
                for l in range(LIST):
                    e = pairs_ref[s * LIST * LIST + k * LIST + l]
                    sums_ref[e] += full[
                        k * block : (k + 1) * block, l * block : (l + 1) * block
                    ]
        return carry

    lax.fori_loop(0, slots // unroll, group, 0)

    low = lax.broadcasted_iota(jnp.int32, (1, 8, block), 1) < 4
    for c in range(out_ref.shape[2]):
        first = sums_ref[2 * c].reshape(block // 8, 8, block)
        second = sums_ref[2 * c + 1].reshape(block // 8, 8, block)
        out_ref[:, 0, c] = jnp.where(low, first, pltpu.roll(second, 4, 1)).astype(bf16)
        out_ref[:, 1, c] = jnp.where(low, pltpu.roll(first, 4, 1), second).astype(bf16)


def add_kernel(target_ref, received_ref, out_ref):
    rows = out_ref.shape[1]
    length = target_ref.shape[1]
    chosen = lax.broadcasted_iota(jnp.int32, (rows, length), 0) == target_ref[...]
    total = jnp.dot(
        chosen.astype(f32).astype(bf16), received_ref[...], preferred_element_type=f32
    ).astype(bf16)
    for h in range(out_ref.shape[0]):
        out_ref[h] = total


def merge_kernel(received_ref, out_ref):
    half, _, rows, block = received_ref.shape
    low = lax.broadcasted_iota(jnp.int32, (1, 8, block), 1) < 4
    for at in range(0, rows, 16):
        even = received_ref[:, 0, at : at + 16, :].astype(f32)
        odd = received_ref[:, 1, at : at + 16, :].astype(f32)
        for q in range(2):
            first = even[:, 8 * q : 8 * q + 8]
            second = odd[:, 8 * q : 8 * q + 8]
            place = at // 4 + 2 * q
            out_ref[place] = jnp.where(low, first, pltpu.roll(second, 4, 1)).reshape(8 * half, block)
            out_ref[place + 1] = jnp.where(low, pltpu.roll(first, 4, 1), second).reshape(
                8 * half, block
            )


def to_all(value, axis):
    copies = jnp.broadcast_to(value[None], (lax.axis_size(axis),) + value.shape)
    return lax.all_to_all(copies, axis, split_axis=0, concat_axis=0, tiled=True)


def on_device(
    points,
    centers,
    exponents,
    angular,
    grid_weights,
    hartree,
    load_plan,
    density_blocks,
    pair_lists,
    batch_pairs,
):
    slots, _, _, grid = points.shape
    ranks = lax.axis_size("batch")
    columns = lax.axis_size("blk")
    per_owner = pair_lists.shape[3]
    held, block, _ = density_blocks.shape
    entries = columns * per_owner
    width = LIST * block
    piece = block // ranks
    rank = lax.axis_index("batch")
    plan_rows = lax.dynamic_slice_in_dim(load_plan[0], rank * slots, slots)

    wanted = pair_lists[0, 0]
    asked = lax.all_to_all(wanted, "blk", split_axis=0, concat_axis=0, tiled=True)
    stored = to_all(hartree[:, 0, :], "batch").reshape(ranks * slots, grid)

    params = jnp.concatenate(
        [centers[:, 0], exponents, angular[:, 0], jnp.zeros((slots, 1, width), f32)], axis=1
    )
    basis = call(
        basis_kernel,
        jax.ShapeDtypeStruct((slots, width, grid), bf16),
        [VMEM, VMEM],
        flops=slots * width * grid * 400,
        moved=slots * width * grid * 2,
    )(points[:, 0], params)

    sent = call(
        pick_kernel,
        jax.ShapeDtypeStruct((entries, block, block), bf16),
        [SMEM, VMEM],
        moved=entries * block * block * 4,
    )(asked.reshape(entries), density_blocks)
    table = lax.all_to_all(
        sent.reshape(columns, per_owner * block, block), "blk", split_axis=0, concat_axis=0, tiled=True
    ).reshape(entries, block, block)

    everyone = to_all(asked, "batch").reshape(ranks * entries, 1)
    targets = (everyone * piece + jnp.arange(piece, dtype=jnp.int32)[None]).reshape(
        1, ranks * entries * piece
    )

    unroll = 2
    partial, rho = call(
        integrate_kernel,
        (
            jax.ShapeDtypeStruct((ranks // 2, 2, columns, per_owner * piece, block), bf16),
            jax.ShapeDtypeStruct((slots, grid), f32),
        ),
        [SMEM, SMEM, VMEM, VMEM, VMEM, VMEM],
        [pltpu.VMEM((unroll, width, width), bf16), pltpu.VMEM((entries, block, block), f32)],
        flops=slots * width * width * grid * 4,
        moved=slots * width * grid * 2,
    )(
        batch_pairs.reshape(slots * LIST * LIST), plan_rows, basis, table, stored, grid_weights[:, 0]
    )

    rows = per_owner * piece
    received = lax.all_to_all(
        partial.reshape(ranks * columns, rows, block),
        ("batch", "blk"),
        split_axis=0,
        concat_axis=0,
        tiled=True,
    ).reshape(ranks * columns * rows, block)
    spread = to_all(rho.astype(bf16), "batch").reshape(ranks * slots, grid)

    totals = call(
        add_kernel,
        jax.ShapeDtypeStruct((ranks, held * piece, block), bf16),
        [VMEM, VMEM],
        moved=ranks * columns * rows * block * 2,
    )(targets, received)
    gathered = lax.all_to_all(totals, "batch", split_axis=0, concat_axis=0, tiled=True)
    hamiltonian = call(
        merge_kernel,
        jax.ShapeDtypeStruct((held, block, block), f32),
        [VMEM],
        moved=held * block * block * 6,
    )(gathered.reshape(ranks // 2, 2, held * piece, block))

    own_rows = rank * slots + jnp.arange(slots, dtype=jnp.int32)
    placement = (own_rows[:, None] == load_plan).astype(bf16)
    density = jnp.dot(placement, spread, preferred_element_type=f32)
    return (hamiltonian, density[:, None, :])


def solution(mesh):
    return jax.shard_map(
        on_device,
        mesh=mesh,
        in_specs=(
            P("batch", "blk", None, None),
            P("batch", "blk", None, None),
            P("batch", "blk", None),
            P("batch", "blk", None, None),
            P("batch", "blk", None),
            P("batch", "blk", None),
            P("blk", None),
            P("blk", None, None),
            P("batch", "blk", None, None),
            P("batch", "blk", None),
        ),
        out_specs=(P("blk", None, None), P("batch", "blk", None)),
        check_vma=False,
    )
```

time: 804 us -> 216 us (0.27)
  the two profiles are of different devices: /device:TPU:24 before, /device:TPU:8 now
where the time goes in v1:
time: 216 us; the launch traced here: 215 us
  waiting for transfers between devices  91.8 us (42%)
  starting transfers between devices  50.4 us (23%)
  Pallas kernels  43.4 us (20%)
  blocking collectives  14.5 us (7%)
  local copies, waits for them, and re-layouts  13.4 us (6%)
    all_to_all x1, waiting for transfers between devices, on_device(): lax.all_to_all(partial.reshape(ranks * columns, rows, block), ('batch', '...  32.6 us
    all_to_all x1, waiting for transfers between devices, on_device(): lax.all_to_all(sent.reshape(columns, per_owner * block, block), 'blk', sp...  24 us
    all_to_all x3, starting transfers between devices, to_all(): return lax.all_to_all(copies, axis, split_axis=0, concat_axis=0, tiled=True)  24 us
    pallas_call x1, Pallas kernels, on_device(): call(basis_kernel, jax.ShapeDtypeStruct((slots, width, grid), bf16), [VME...  21.8 us
    all_to_all x3, waiting for transfers between devices, to_all(): return lax.all_to_all(copies, axis, split_axis=0, concat_axis=0, tiled=True)  19 us
    pallas_call x1, Pallas kernels, on_device(): call(integrate_kernel, (jax.ShapeDtypeStruct((ranks // 2, 2, columns, per...  17.7 us
    all_to_all x1, starting transfers between devices, on_device(): lax.all_to_all(partial.reshape(ranks * columns, rows, block), ('batch', '...  16.9 us
    all_to_all x1, waiting for transfers between devices, on_device(): lax.all_to_all(totals, 'batch', split_axis=0, concat_axis=0, tiled=True)  16.2 us
  transfers between devices with their start and end apart: 6, of which 5 were waited for; matrix products, arithmetic and copies ran while one was open for 2% of the time, Pallas kernels for 19%

profile of v1, /device:TPU:8, one launch (start us, length us, event | category | flops | bytes accessed | tf_op | source)
XLA Modules:
  0.0 215.5 jit_solution(11865818055209224748)
XLA Ops:
  0.7 0.8 copy.36
  1.4 14.5 %all_to_all.39 = s32[16,1,2]{2,1,0:T(1,128)S(1)} all-to-all(s32[16,1,2]{2,1,0:T(1,128)S(1)} %copy.36), channel_id=1, replica_groups=mesh['batch'=32,'blk'=16] {'blk'}, dimensions={0} | all-to-all | bytes 256 | tf_op jit(solution)/shard_map/all_to_all | solution.py:168
  15.9 0.5 broadcast.21
  16.4 0.7 reduce.3
  17.2 1.0 copy-done.2
  18.2 1.6 shard_map.114
  19.8 4.9 %all-to-all-start.2 = ((bf16[16,256,128]{2,1,0:T(8,128)(2,1)}), bf16[16,256,128]{2,1,0:T(8,128)(2,1)S(1)}, u32[]{:S(2)}, u32[]{:S(2)}) async-start(bf16[16,256,128]{2,1,0:T(8,128)(2,1)} %bitcast.6), calls=%async_computation.2 | async-start | bytes 2097152 | tf_op jit(solution)/shard_map/all_to_all | solution.py:188
  24.7 0.8 copy.59
  25.5 24.0 %all-to-all-done.2 = bf16[16,256,128]{2,1,0:T(8,128)(2,1)S(1)} async-done(((bf16[16,256,128]{2,1,0:T(8,128)(2,1)}), bf16[16,256,128]{2,1,0:T(8,128)(2,1)S(1)}, u32[]{:S(2)}, u32[]{:S(2)}) %all-to-all-start.2) | async-done | bytes 1048608 | tf_op jit(solution)/shard_map/all_to_all | solution.py:188
  49.5 1.1 broadcast_in_dim.33
  50.6 12.3 %all-to-all-start.3 = ((f32[32,32,256]{2,1,0:T(8,128)}), f32[32,32,256]{2,1,0:T(8,128)S(1)}, u32[]{:S(2)}, u32[]{:S(2)}) async-start(f32[32,32,256]{2,1,0:T(8,128)} %broadcast_in_dim.33), calls=%async_computation.3 | async-start | bytes 2097152 | tf_op jit(solution)/shard_map/all_to_all | solution.py:141
  63.8 21.8 %shard_map.113.basis_ref = bf16[32,384,256]{2,1,0:T(8,128)(2,1)S(1)} custom-call(f32[32,3,256]{2,1,0:T(4,128)S(1)} %copy.46.points_ref, f32[32,8,384]{2,1,0:T(8,128)S(1)} %maximum_maximum_fusion.params_ref), custom_call_target="tpu_custom_call" | custom-call | flops 1258291200 | bytes 6291456 | tf_op jit(solution)/shard_map/pallas_call | solution.py:174
  85.6 2.7 %copy-done = bf16[32,384,256]{2,1,0:T(8,128)(2,1)} copy-done((bf16[32,384,256]{2,1,0:T(8,128)(2,1)}, bf16[32,384,256]{2,1,0:T(8,128)(2,1)S(1)}, u32[]{:S(2)}) %copy-start) | copy-done | bytes 6291480
  88.3 3.0 %all-to-all-done.3 = f32[32,32,256]{2,1,0:T(8,128)S(1)} async-done(((f32[32,32,256]{2,1,0:T(8,128)}), f32[32,32,256]{2,1,0:T(8,128)S(1)}, u32[]{:S(2)}, u32[]{:S(2)}) %all-to-all-start.3) | async-done | bytes 1048608 | tf_op jit(solution)/shard_map/all_to_all | solution.py:141
  91.4 0.6 broadcast_in_dim.30
  92.0 6.7 %all-to-all-start.1 = ((s32[32,16,2]{1,2,0:T(2,128)}), s32[32,16,2]{1,2,0:T(2,128)S(1)}, u32[]{:S(2)}, u32[]{:S(2)}) async-start(s32[32,16,2]{1,2,0:T(2,128)} %broadcast_in_dim.30), calls=%async_computation.1 | async-start | bytes 65536 | tf_op jit(solution)/shard_map/all_to_all | solution.py:141
  98.7 2.8 %copy-done.1 = bf16[32,384,256]{2,1,0:T(8,128)(2,1)S(1)} copy-done((bf16[32,384,256]{2,1,0:T(8,128)(2,1)S(1)}, bf16[32,384,256]{2,1,0:T(8,128)(2,1)}, u32[]{:S(2)}) %copy-start.1) | copy-done | bytes 6291480
  101.5 17.7 %shard_map.115 = (bf16[16,2,16,8,128]{4,3,2,1,0:T(8,128)(2,1)}, f32[32,256]{1,0:T(8,128)S(1)}) custom-call(s32[288]{0:T(512)S(1)} %reshape.77.pairs_ref, s32[32]{0:T(128)S(1)} %dynamic-slice_bitcast_fusion.plan_ref, bf16[32,384,256]{2,1,0:T(8,128)(2,1)S(1)} %copy-done.1, bf16[32,128,128]{2,1,0:T(8,128)(2,1)S(1)} %bitcast.35, f32[1024,256]{1,0:T(8,128)S(1)} %bitcast.36, ...), custom_call_target="tpu_custom_call" | custom-call | flops 4831838208 | bytes 6291456 | tf_op jit(solution)/shard_map/pallas_call | solution.py:198
  119.2 16.9 %all-to-all-start.4 = ((bf16[512,8,128]{2,1,0:T(8,128)(2,1)}), bf16[512,8,128]{2,1,0:T(8,128)(2,1)S(1)}, u32[]{:S(2)}, u32[]{:S(2)}) async-start(bf16[512,8,128]{2,1,0:T(8,128)(2,1)} %bitcast.9), calls=%async_computation.4 | async-start | bytes 2097152 | tf_op jit(solution)/shard_map/all_to_all | solution.py:213
  136.1 32.6 %all-to-all-done.4 = bf16[512,8,128]{2,1,0:T(8,128)(2,1)S(1)} async-done(((bf16[512,8,128]{2,1,0:T(8,128)(2,1)}), bf16[512,8,128]{2,1,0:T(8,128)(2,1)S(1)}, u32[]{:S(2)}, u32[]{:S(2)}) %all-to-all-start.4) | async-done | bytes 1048608 | tf_op jit(solution)/shard_map/all_to_all | solution.py:213
  168.8 0.9 broadcast_in_dim.34
  169.6 5.0 %all-to-all-start.6 = ((bf16[32,32,256]{2,1,0:T(8,128)(2,1)}), bf16[32,32,256]{2,1,0:T(8,128)(2,1)S(1)}, u32[]{:S(2)}, u32[]{:S(2)}) async-start(bf16[32,32,256]{2,1,0:T(8,128)(2,1)} %broadcast_in_dim.34), calls=%async_computation.6 | async-start | bytes 1048576 | tf_op jit(solution)/shard_map/all_to_all | solution.py:141
  174.7 0.2 copy.39
  175.0 0.2 iota_add_fusion
  175.3 0.3 add.39.target_ref
  175.6 1.2 shard_map.116
  176.8 16.0 %all-to-all-done.6 = bf16[32,32,256]{2,1,0:T(8,128)(2,1)S(1)} async-done(((bf16[32,32,256]{2,1,0:T(8,128)(2,1)}), bf16[32,32,256]{2,1,0:T(8,128)(2,1)S(1)}, u32[]{:S(2)}, u32[]{:S(2)}) %all-to-all-start.6) | async-done | bytes 524320 | tf_op jit(solution)/shard_map/all_to_all | solution.py:141
  192.7 4.6 %all-to-all-start.5 = ((bf16[32,64,128]{2,1,0:T(8,128)(2,1)}), bf16[32,64,128]{2,1,0:T(8,128)(2,1)S(1)}, u32[]{:S(2)}, u32[]{:S(2)}) async-start(bf16[32,64,128]{2,1,0:T(8,128)(2,1)} %shard_map.116), calls=%async_computation.5 | async-start | bytes 1048576 | tf_op jit(solution)/shard_map/all_to_all | solution.py:228
  197.3 0.2 convolution_bitcast_fusion
  197.6 0.7 copy.47
  198.2 16.2 %all-to-all-done.5 = bf16[32,64,128]{2,1,0:T(8,128)(2,1)S(1)} async-done(((bf16[32,64,128]{2,1,0:T(8,128)(2,1)}), bf16[32,64,128]{2,1,0:T(8,128)(2,1)S(1)}, u32[]{:S(2)}, u32[]{:S(2)}) %all-to-all-start.5) | async-done | bytes 524320 | tf_op jit(solution)/shard_map/all_to_all | solution.py:228
  214.4 1.1 shard_map.117
  (37 shorter events, 1.2 us)
Async XLA Ops:
  0.6 62.6 %copy-start.8 = (s32[32,1,9]{0,1,2:T(1,128)S(1)}, s32[32,1,9]{0,1,2:T(1,128)}, u32[]{:S(2)}) copy-start(s32[32,1,9]{0,1,2:T(1,128)} %param.19) | copy-start | bytes 3460
  0.6 63.0 %copy-start.6 = (f32[32,1,384]{2,1,0:T(1,128)S(1)}, f32[32,1,384]{2,1,0:T(1,128)}, u32[]{:S(2)}) copy-start(f32[32,1,384]{2,1,0:T(1,128)} %param.12) | copy-start | bytes 147460
  17.2 1.0 copy-start.2
  18.2 44.7 %copy-start.3 = (f32[32,1,3,384]{3,1,2,0:T(1,128)S(1)}, f32[32,1,3,384]{3,1,2,0:T(1,128)}, u32[]{:S(2)}) copy-start(f32[32,1,3,384]{3,1,2,0:T(1,128)} %param.11) | copy-start | bytes 442372
  18.2 44.8 %copy-start.4 = (f32[32,1,3,384]{3,1,2,0:T(1,128)S(1)}, f32[32,1,3,384]{3,1,2,0:T(1,128)}, u32[]{:S(2)}) copy-start(f32[32,1,3,384]{3,1,2,0:T(1,128)} %param.13) | copy-start | bytes 442372
  18.2 44.9 %copy-start.5 = (f32[32,1,3,256]{3,1,2,0:T(1,128)S(1)}, f32[32,1,3,256]{3,1,2,0:T(1,128)}, u32[]{:S(2)}) copy-start(f32[32,1,3,256]{3,1,2,0:T(1,128)} %param.10) | copy-start | bytes 294916
  18.2 45.0 %copy-start.7 = (f32[32,1,256]{2,1,0:T(1,128)S(1)}, f32[32,1,256]{2,1,0:T(1,128)}, u32[]{:S(2)}) copy-start(f32[32,1,256]{2,1,0:T(1,128)} %param.14) | copy-start | bytes 98308
  18.2 45.3 %copy-start.9 = (s32[1,1024]{1,0:T(1,128)S(1)}, s32[1,1024]{1,0:T(1,128)}, u32[]{:S(2)}) copy-start(s32[1,1024]{1,0:T(1,128)} %param.16) | copy-start | bytes 12292
  19.8 29.7 %all-to-all-start.2 = ((bf16[16,256,128]{2,1,0:T(8,128)(2,1)}), bf16[16,256,128]{2,1,0:T(8,128)(2,1)S(1)}, u32[]{:S(2)}, u32[]{:S(2)}) async-start(bf16[16,256,128]{2,1,0:T(8,128)(2,1)} %bitcast.6), calls=%async_computation.2 | async-start | bytes 2097152 | tf_op jit(solution)/shard_map/all_to_all | solution.py:188
  50.6 40.8 %all-to-all-start.3 = ((f32[32,32,256]{2,1,0:T(8,128)}), f32[32,32,256]{2,1,0:T(8,128)S(1)}, u32[]{:S(2)}, u32[]{:S(2)}) async-start(f32[32,32,256]{2,1,0:T(8,128)} %broadcast_in_dim.33), calls=%async_computation.3 | async-start | bytes 2097152 | tf_op jit(solution)/shard_map/all_to_all | solution.py:141
  85.6 2.7 %copy-start = (bf16[32,384,256]{2,1,0:T(8,128)(2,1)}, bf16[32,384,256]{2,1,0:T(8,128)(2,1)S(1)}, u32[]{:S(2)}) copy-start(bf16[32,384,256]{2,1,0:T(8,128)(2,1)S(1)} %shard_map.113.basis_ref) | copy-start | bytes 18874372
  92.0 27.3 %all-to-all-start.1 = ((s32[32,16,2]{1,2,0:T(2,128)}), s32[32,16,2]{1,2,0:T(2,128)S(1)}, u32[]{:S(2)}, u32[]{:S(2)}) async-start(s32[32,16,2]{1,2,0:T(2,128)} %broadcast_in_dim.30), calls=%async_computation.1 | async-start | bytes 65536 | tf_op jit(solution)/shard_map/all_to_all | solution.py:141
  98.7 2.8 %copy-start.1 = (bf16[32,384,256]{2,1,0:T(8,128)(2,1)S(1)}, bf16[32,384,256]{2,1,0:T(8,128)(2,1)}, u32[]{:S(2)}) copy-start(bf16[32,384,256]{2,1,0:T(8,128)(2,1)} %copy-done) | copy-start | bytes 18874372
  119.2 49.5 %all-to-all-start.4 = ((bf16[512,8,128]{2,1,0:T(8,128)(2,1)}), bf16[512,8,128]{2,1,0:T(8,128)(2,1)S(1)}, u32[]{:S(2)}, u32[]{:S(2)}) async-start(bf16[512,8,128]{2,1,0:T(8,128)(2,1)} %bitcast.9), calls=%async_computation.4 | async-start | bytes 2097152 | tf_op jit(solution)/shard_map/all_to_all | solution.py:213
  169.6 23.1 %all-to-all-start.6 = ((bf16[32,32,256]{2,1,0:T(8,128)(2,1)}), bf16[32,32,256]{2,1,0:T(8,128)(2,1)S(1)}, u32[]{:S(2)}, u32[]{:S(2)}) async-start(bf16[32,32,256]{2,1,0:T(8,128)(2,1)} %broadcast_in_dim.34), calls=%async_computation.6 | async-start | bytes 1048576 | tf_op jit(solution)/shard_map/all_to_all | solution.py:141
  192.7 21.6 %all-to-all-start.5 = ((bf16[32,64,128]{2,1,0:T(8,128)(2,1)}), bf16[32,64,128]{2,1,0:T(8,128)(2,1)S(1)}, u32[]{:S(2)}, u32[]{:S(2)}) async-start(bf16[32,64,128]{2,1,0:T(8,128)(2,1)} %shard_map.116), calls=%async_computation.5 | async-start | bytes 1048576 | tf_op jit(solution)/shard_map/all_to_all | solution.py:228

commit v2 on v1

v2 whole, which is shorter than its diff:
```python
import jax
import jax.numpy as jnp
from jax import lax
from jax.experimental import pallas as pl
from jax.experimental.pallas import tpu as pltpu
from jax.sharding import PartitionSpec as P

LIST = 3
BLK = ("y", "core")
xc_scale = 0.98474502
soft_square = 0.01
log2_e = 1.4426950408889634

bf16 = jnp.bfloat16
f32 = jnp.float32
VMEM = pl.BlockSpec(memory_space=pltpu.VMEM)
HBM = pl.BlockSpec(memory_space=pltpu.HBM)
SMEM = pl.BlockSpec(memory_space=pltpu.SMEM)


def rows_of(*block):
    return pl.BlockSpec(block, lambda n: (n,) + (0,) * (len(block) - 1))


def call(body, outs, ins, scratch=(), flops=0, moved=0, limit=24, grid=(), out_specs=None):
    return pl.pallas_call(
        body,
        out_shape=outs,
        grid=grid,
        in_specs=ins,
        out_specs=out_specs or jax.tree.map(lambda _: VMEM, outs),
        scratch_shapes=list(scratch),
        compiler_params=pltpu.CompilerParams(vmem_limit_bytes=limit * 2**20),
        cost_estimate=pl.CostEstimate(flops=flops, bytes_accessed=moved, transcendentals=0),
    )


def basis_kernel(points_ref, params_ref, out_ref, done_ref):
    slots, width, _ = out_ref.shape
    step = 32
    done_ref[...] = jnp.zeros_like(done_ref)

    def one(s, carry):
        columns = jnp.transpose(params_ref[s])
        for at in range(0, width, step):
            own = columns[at : at + step]
            distance = None
            angular = None
            for a in range(3):
                delta = points_ref[s, a : a + 1, :] - own[:, a : a + 1]
                square = delta * delta
                slope = own[:, 4 + a : 5 + a] * delta
                distance = square if a == 0 else distance + square
                angular = slope + 1.0 if a == 0 else angular + slope
            value = jnp.exp2((own[:, 3:4] * -log2_e) * distance) * angular
            out_ref[s, at : at + step, :] = value.astype(bf16)
        return carry

    lax.fori_loop(0, slots, one, 0)


def pick_kernel(places_ref, blocks_ref, done_ref, own_ref, other_ref, sems):
    del done_ref
    half = own_ref.shape[0]
    copies = []
    for n in range(2 * half):
        to = other_ref.at[n] if n < half else own_ref.at[n - half]
        copies.append(pltpu.make_async_copy(blocks_ref.at[places_ref[n]], to, sems.at[n]))
    for copy in copies:
        copy.start()
    for copy in copies:
        copy.wait()


def density_kernel(pairs_ref, core_ref, basis_ref, own_ref, other_ref, rho_ref, table_ref, sub_ref):
    slots = basis_ref.shape[0]
    half, block, _ = own_ref.shape
    unroll = sub_ref.shape[0]
    start = pl.program_id(0) * slots

    @pl.when(start == 0)
    def _():
        core = core_ref[0]
        for n in range(half):
            base = 4 * (n // 2) + n % 2
            table_ref[base + 2 * core] = own_ref[n]
            table_ref[base + 2 * (1 - core)] = other_ref[n]

    def group(turn, carry):
        for u in range(unroll):
            s = turn * unroll + u
            for k in range(LIST):
                for l in range(LIST):
                    sub_ref[u, k * block : (k + 1) * block, l * block : (l + 1) * block] = table_ref[
                        pairs_ref[(start + s) * LIST * LIST + k * LIST + l]
                    ]
        for u in range(unroll):
            s = turn * unroll + u
            basis = basis_ref[s]
            inner = jnp.dot(sub_ref[u], basis, preferred_element_type=f32)
            rho_ref[pl.ds(start + s, 1), :] = jnp.sum(inner * basis.astype(f32), axis=0, keepdims=True)
        return carry

    lax.fori_loop(0, slots // unroll, group, 0)


def matrix_kernel(
    pairs_ref, plan_ref, basis_ref, rho_ref, hartree_ref, weights_ref,
    out_ref, lists_ref, sums_ref, factor_ref,
):
    slots = basis_ref.shape[0]
    total = rho_ref.shape[0]
    entries, block, _ = sums_ref.shape
    stride = hartree_ref.shape[0] // lists_ref.shape[0]
    unroll = 2
    start = pl.program_id(0) * slots

    @pl.when(start == 0)
    def _():
        for r in range(lists_ref.shape[0]):
            at = r * stride + total
            lists_ref[r : r + 1, :] = hartree_ref[at : at + 1, :block]
        for s in range(total):
            at = plan_ref[s]
            factor_ref[s : s + 1, :] = hartree_ref[
                pl.ds(lax.div(at, total) * stride + lax.rem(at, total), 1), :
            ]
        rho = rho_ref[...]
        root = jnp.exp2(jnp.log2(rho * rho + soft_square) * (1.0 / 6.0))
        factor_ref[...] = weights_ref[...] * (factor_ref[...] - xc_scale * root)

        def clear(e, carry):
            sums_ref[e] = jnp.zeros((block, block), f32)
            return carry

        lax.fori_loop(0, entries, clear, 0)

    def group(turn, carry):
        for u in range(unroll):
            s = turn * unroll + u
            basis = basis_ref[s]
            scaled = (basis.astype(f32) * factor_ref[pl.ds(start + s, 1), :]).astype(bf16)
            full = lax.dot_general(
                basis, scaled, (((1,), (1,)), ((), ())), preferred_element_type=f32
            )
            for k in range(LIST):
                for l in range(LIST):
                    e = pairs_ref[(start + s) * LIST * LIST + k * LIST + l]
                    sums_ref[e] += full[
                        k * block : (k + 1) * block, l * block : (l + 1) * block
                    ]
        return carry

    lax.fori_loop(0, slots // unroll, group, 0)

    @pl.when(start == total - slots)
    def _():
        low = lax.broadcasted_iota(jnp.int32, (1, 8, block), 1) < 4
        for c in range(out_ref.shape[2]):
            first = sums_ref[2 * c].reshape(block // 8, 8, block)
            second = sums_ref[2 * c + 1].reshape(block // 8, 8, block)
            out_ref[:, 0, c] = jnp.where(low, first, pltpu.roll(second, 4, 1)).astype(bf16)
            out_ref[:, 1, c] = jnp.where(low, pltpu.roll(first, 4, 1), second).astype(bf16)


def add_kernel(target_ref, received_ref, rho_ref, out_ref):
    block = out_ref.shape[2]
    parts = rho_ref.shape[1] // block
    slots = rho_ref.shape[0]
    rows = out_ref.shape[1] - parts * slots
    length = target_ref.shape[1]
    chosen = lax.broadcasted_iota(jnp.int32, (rows, length), 0) == target_ref[...]
    total = jnp.dot(
        chosen.astype(f32).astype(bf16), received_ref[...], preferred_element_type=f32
    ).astype(bf16)
    rho = rho_ref[...].astype(bf16)
    for h in range(out_ref.shape[0]):
        out_ref[h, :rows, :] = total
        for n in range(parts):
            out_ref[h, rows + n * slots : rows + (n + 1) * slots, :] = rho[
                :, n * block : (n + 1) * block
            ]


def merge_kernel(received_ref, plan_ref, rank_ref, out_ref, density_ref):
    half, _, rows, block = received_ref.shape
    slots = density_ref.shape[0]
    parts = density_ref.shape[1] // block
    rows -= parts * slots
    low = lax.broadcasted_iota(jnp.int32, (1, 8, block), 1) < 4
    for at in range(0, rows, 16):
        even = received_ref[:, 0, at : at + 16, :].astype(f32)
        odd = received_ref[:, 1, at : at + 16, :].astype(f32)
        for q in range(2):
            first = even[:, 8 * q : 8 * q + 8]
            second = odd[:, 8 * q : 8 * q + 8]
            place = at // 4 + 2 * q
            out_ref[place] = jnp.where(low, first, pltpu.roll(second, 4, 1)).reshape(8 * half, block)
            out_ref[place + 1] = jnp.where(low, pltpu.roll(first, 4, 1), second).reshape(
                8 * half, block
            )
    length = plan_ref.shape[1]
    own = lax.broadcasted_iota(jnp.int32, (slots, length), 0) + rank_ref[0] * slots
    chosen = (own == plan_ref[...]).astype(f32).astype(bf16)
    for n in range(parts):
        values = received_ref[:, :, rows + n * slots : rows + (n + 1) * slots, :]
        density_ref[:, n * block : (n + 1) * block] = jnp.dot(
            chosen, values.reshape(length, block), preferred_element_type=f32
        )


def to_all(value, axis):
    copies = jnp.broadcast_to(value[None], (lax.axis_size(axis),) + value.shape)
    return lax.all_to_all(copies, axis, split_axis=0, concat_axis=0, tiled=True)


def on_device(
    points,
    centers,
    exponents,
    angular,
    grid_weights,
    hartree,
    load_plan,
    density_blocks,
    pair_lists,
    batch_pairs,
):
    slots, _, _, grid = points.shape
    ranks = lax.axis_size("batch")
    columns = lax.axis_size(BLK)
    per_owner = pair_lists.shape[3]
    held, block, _ = density_blocks.shape
    entries = columns * per_owner
    width = LIST * block
    piece = block // ranks
    rank = lax.axis_index("batch")
    core = lax.axis_index("core")
    swap = [(0, 1), (1, 0)]
    plan_rows = lax.dynamic_slice_in_dim(load_plan[0], rank * slots, slots)

    near = lax.all_gather(density_blocks, "y", axis=0, tiled=True)
    wanted = pair_lists[0, 0]
    asked = lax.ppermute(wanted, "core", swap)

    listed = jnp.pad(wanted.reshape(1, entries).astype(f32), ((0, 7), (0, grid - entries)))
    stored = to_all(jnp.concatenate([hartree[:, 0], listed]), "batch")
    stride = stored.shape[1]
    stored = stored.reshape(ranks * stride, grid)

    params = jnp.concatenate(
        [centers[:, 0], exponents, angular[:, 0], jnp.zeros((slots, 1, width), f32)], axis=1
    )
    group = min(4, slots)
    steps = (slots // group,)
    basis, done = call(
        basis_kernel,
        (jax.ShapeDtypeStruct((slots, width, grid), bf16), jax.ShapeDtypeStruct((8, block), f32)),
        [rows_of(group, 3, grid), rows_of(group, 8, width)],
        grid=steps,
        out_specs=(rows_of(group, width, grid), VMEM),
        limit=48,
        flops=slots * width * grid * 400,
        moved=slots * width * grid * 2,
    )(points[:, 0], params)

    sides = jnp.stack([asked, wanted]).reshape(2, columns // 2, 2, per_owner)
    sides = lax.dynamic_index_in_dim(sides, core, 2, keepdims=False)
    sides = sides + held * jnp.arange(columns // 2, dtype=jnp.int32)[None, :, None]
    half = jax.ShapeDtypeStruct((entries // 2, block, block), bf16)
    own, other = call(
        pick_kernel,
        (half, half),
        [SMEM, HBM, HBM],
        [pltpu.SemaphoreType.DMA((entries,))],
        limit=60,
        moved=entries * block * block * 4,
    )(sides.reshape(entries), near, done)
    other = lax.ppermute(other, "core", swap)

    pairs = batch_pairs.reshape(slots * LIST * LIST)
    unroll = 2
    rho = call(
        density_kernel,
        jax.ShapeDtypeStruct((slots, grid), f32),
        [SMEM, SMEM, rows_of(group, width, grid), VMEM, VMEM],
        [pltpu.VMEM((entries, block, block), bf16), pltpu.VMEM((unroll, width, width), bf16)],
        grid=steps,
        limit=48,
        flops=slots * width * width * grid * 2,
        moved=slots * width * grid * 2,
    )(pairs, core.reshape(1), basis, own, other)
    partial, lists = call(
        matrix_kernel,
        (
            jax.ShapeDtypeStruct((ranks // 2, 2, columns, per_owner * piece, block), bf16),
            jax.ShapeDtypeStruct((ranks, block), f32),
        ),
        [SMEM, SMEM, rows_of(group, width, grid), VMEM, VMEM, VMEM],
        [pltpu.VMEM((entries, block, block), f32), pltpu.VMEM((slots, grid), f32)],
        grid=steps,
        limit=48,
        flops=slots * width * width * grid * 2,
        moved=slots * width * grid * 2,
    )(pairs, plan_rows, basis, rho, stored, grid_weights[:, 0])

    rows = per_owner * piece
    received = lax.all_to_all(
        partial.reshape(ranks * columns, rows, block),
        ("batch",) + BLK,
        split_axis=0,
        concat_axis=0,
        tiled=True,
    ).reshape(ranks * columns * rows, block)

    asking = lax.all_gather(lists, BLK, axis=0)
    asking = lax.dynamic_slice_in_dim(asking, lax.axis_index(BLK) * per_owner, per_owner, 2)
    asking = asking.astype(jnp.int32).transpose(1, 0, 2).reshape(ranks * entries, 1)
    targets = (asking * piece + jnp.arange(piece, dtype=jnp.int32)[None]).reshape(
        1, ranks * entries * piece
    )

    lines = held * piece + slots * grid // block
    totals = call(
        add_kernel,
        jax.ShapeDtypeStruct((ranks, lines, block), bf16),
        [VMEM, VMEM, VMEM],
        moved=ranks * columns * rows * block * 2,
    )(targets, received, rho)
    gathered = lax.all_to_all(totals, "batch", split_axis=0, concat_axis=0, tiled=True)
    hamiltonian, density = call(
        merge_kernel,
        (
            jax.ShapeDtypeStruct((held, block, block), f32),
            jax.ShapeDtypeStruct((slots, grid), f32),
        ),
        [VMEM, VMEM, SMEM],
        moved=held * block * block * 6,
    )(gathered.reshape(ranks // 2, 2, lines, block), load_plan, rank.reshape(1))
    return (hamiltonian, density[:, None, :])


def solution(mesh):
    ranks, columns = mesh.devices.shape
    fine = jax.sharding.Mesh(mesh.devices.reshape(ranks, columns // 2, 2), ("batch",) + BLK)
    return jax.shard_map(
        on_device,
        mesh=fine,
        in_specs=(
            P("batch", BLK, None, None),
            P("batch", BLK, None, None),
            P("batch", BLK, None),
            P("batch", BLK, None, None),
            P("batch", BLK, None),
            P("batch", BLK, None),
            P(BLK, None),
            P(BLK, None, None),
            P("batch", BLK, None, None),
            P("batch", BLK, None),
        ),
        out_specs=(P(BLK, None, None), P("batch", BLK, None)),
        check_vma=False,
    )
```

time: 216 us -> 200 us (0.926)
  the two profiles are of different devices: /device:TPU:8 before, /device:TPU:2 now
where the time goes in v2:
time: 200 us; the launch traced here: 199 us
  blocking collectives  73.7 us (37%)
  Pallas kernels  46.8 us (23%)
  starting transfers between devices  33 us (16%)
  waiting for transfers between devices  23.6 us (12%)
  between operations  14.4 us (7%)
  local copies, waits for them, and re-layouts  5.76 us (3%)
    all_to_all x1, blocking collectives, on_device(): lax.all_to_all(totals, 'batch', split_axis=0, concat_axis=0, tiled=True)  40.3 us
    all_gather x1, blocking collectives, on_device(): asking = lax.all_gather(lists, BLK, axis=0)  33.3 us
    pallas_call x1, Pallas kernels, on_device(): call(basis_kernel, (jax.ShapeDtypeStruct((slots, width, grid), bf16), jax...  22.8 us
    all_gather x1, waiting for transfers between devices, on_device(): near = lax.all_gather(density_blocks, 'y', axis=0, tiled=True)  21.1 us
    all_to_all x1, starting transfers between devices, on_device(): lax.all_to_all(partial.reshape(ranks * columns, rows, block), ('batch',)...  15.6 us
    all_to_all x1, starting transfers between devices, to_all(): return lax.all_to_all(copies, axis, split_axis=0, concat_axis=0, tiled=True)  13.5 us
    pallas_call x1, Pallas kernels, on_device(): call(matrix_kernel, (jax.ShapeDtypeStruct((ranks // 2, 2, columns, per_ow...  10.4 us
    pallas_call x1, Pallas kernels, on_device(): call(density_kernel, jax.ShapeDtypeStruct((slots, grid), f32), [SMEM, SME...  8.89 us
  transfers between devices with their start and end apart: 5, of which 2 were waited for; matrix products, arithmetic and copies ran while one was open for 3% of the time, Pallas kernels for 17%

profile of v2, /device:TPU:2, one launch (start us, length us, event | category | flops | bytes accessed | tf_op | source)
XLA Modules:
  0.0 198.9 jit_solution(3778749898829667757)
XLA Ops:
  7.3 0.7 all-gather.3.cloned.1.call-update
  8.0 0.8 copy.56
  8.7 0.7 convert_element_type.19
  9.6 1.1 broadcast_in_dim.7
  10.7 13.5 %all-to-all-start = ((f32[32,40,256]{2,1,0:T(8,128)}), f32[32,40,256]{2,1,0:T(8,128)S(1)}, u32[]{:S(2)}, u32[]{:S(2)}) async-start(f32[32,40,256]{2,1,0:T(8,128)} %broadcast_in_dim.7), calls=%async_computation | async-start | bytes 2621440 | tf_op jit(solution)/shard_map/all_to_all | solution.py:214
  24.2 1.9 collective-permute-start
  26.3 0.1 copy.30
  26.5 0.1 copy.31
  26.8 0.1 maximum_maximum_fusion.params_ref
  26.9 22.8 %shard_map.113 = (bf16[32,384,256]{2,1,0:T(8,128)(2,1)}, f32[8,128]{1,0:T(8,128)S(1)}) custom-call(f32[32,3,256]{2,1,0:T(4,128)S(1)} %copy.32.points_ref, f32[32,8,384]{2,1,0:T(8,128)S(1)} %maximum_maximum_fusion.params_ref), custom_call_target="tpu_custom_call" | custom-call | flops 1258291200 | bytes 6291456 | tf_op jit(solution)/shard_map/pallas_call | solution.py:256
  50.1 0.1 copy.35
  50.2 0.1 squeeze.27
  50.3 0.5 add.53.places_ref
  50.8 21.1 %all-gather.3.cloned.1.call-done.blocks_ref = bf16[128,128,128]{2,1,0:T(8,128)(2,1)} async-done(((bf16[16,128,128]{2,1,0:T(8,128)(2,1)}), bf16[128,128,128]{2,1,0:T(8,128)(2,1)}) %all-gather.3.cloned.1.call-update) | async-done | bytes 4194320 | tf_op jit(solution)/shard_map/all_gather | solution.py:242
  71.9 3.1 %shard_map.114 = (bf16[16,128,128]{2,1,0:T(8,128)(2,1)}, bf16[16,128,128]{2,1,0:T(8,128)(2,1)}) custom-call(s32[32]{0:T(128)} %add.53.places_ref, bf16[128,128,128]{2,1,0:T(8,128)(2,1)} %all-gather.3.cloned.1.call-done.blocks_ref, f32[8,128]{1,0:T(8,128)} %copy-done.1), custom_call_target="tpu_custom_call" | custom-call | bytes 2097152 | tf_op jit(solution)/shard_map/pallas_call | solution.py:271
  75.0 1.9 collective-permute-start.1
  77.1 0.1 reshape.86.pairs_ref
  77.3 1.8 collective-permute-done.1.other_ref
  79.1 1.0 copy-done.2
  80.1 8.9 %shard_map.115.rho_ref = f32[32,256]{1,0:T(8,128)S(1)} custom-call(s32[288]{0:T(512)S(1)} %reshape.86.pairs_ref, s32[1]{0:T(128)} %bitcast.4.core_ref, bf16[32,384,256]{2,1,0:T(8,128)(2,1)} %get-tuple-element.10.basis_ref, bf16[16,128,128]{2,1,0:T(8,128)(2,1)S(1)} %copy-done.2, bf16[16,128,128]{2,1,0:T(8,128)(2,1)S(1)} %collective-permute-done.1.other_ref), custom_call_target="tpu_custom_call" | custom-call | flops 2415919104 | bytes 6291456 | tf_op jit(solution)/shard_map/pallas_call | solution.py:283
  89.0 10.4 %shard_map.116 = (bf16[16,2,16,8,128]{4,3,2,1,0:T(8,128)(2,1)}, f32[32,128]{1,0:T(8,128)S(1)}) custom-call(s32[288]{0:T(512)S(1)} %reshape.86.pairs_ref, s32[32]{0:T(128)S(1)} %fusion.3.plan_ref, bf16[32,384,256]{2,1,0:T(8,128)(2,1)} %get-tuple-element.10.basis_ref, f32[32,256]{1,0:T(8,128)S(1)} %shard_map.115.rho_ref, f32[1280,256]{1,0:T(8,128)S(1)} %bitcast.43, ...), custom_call_target="tpu_custom_call" | custom-call | flops 2415919104 | bytes 6291456 | tf_op jit(solution)/shard_map/pallas_call | solution.py:293
  99.4 15.6 %all-to-all-start.1 = ((bf16[512,8,128]{2,1,0:T(8,128)(2,1)}), bf16[512,8,128]{2,1,0:T(8,128)(2,1)S(1)}, u32[]{:S(2)}, u32[]{:S(2)}) async-start(bf16[512,8,128]{2,1,0:T(8,128)(2,1)} %bitcast.9), calls=%async_computation.1 | async-start | bytes 2097152 | tf_op jit(solution)/shard_map/all_to_all | solution.py:308
  115.0 33.3 %all-gather = f32[512,128]{1,0:T(8,128)S(1)} all-gather(f32[32,128]{1,0:T(8,128)S(1)} %get-tuple-element.14), channel_id=2, replica_groups=mesh['batch'=32,'y'=8,'core'=2] {'y','core'}, dimensions={0}, use_global_device_ids=true | all-gather | bytes 278528 | tf_op jit(solution)/shard_map/all_gather | solution.py:316
  148.4 0.1 constant_dynamic-slice_fusion
  148.5 0.2 fusion.1
  148.7 0.2 mul.41
  148.9 0.2 iota_add_fusion
  149.1 0.3 add.59.target_ref
  149.4 0.4 shard_map.117
  149.8 40.3 %all_to_all.15 = bf16[32,128,128]{2,1,0:T(8,128)(2,1)S(1)} all-to-all(bf16[32,128,128]{2,1,0:T(8,128)(2,1)S(1)} %shard_map.117), channel_id=1, replica_groups=mesh['batch'=32,'y'=8,'core'=2] {'batch'}, dimensions={0} | all-to-all | bytes 2097152 | tf_op jit(solution)/shard_map/all_to_all | solution.py:330
  190.1 1.3 shard_map.118
  191.4 0.6 copy.38
  (42 shorter events, 1.1 us)
Async XLA Ops:
  7.2 17.0 %copy-start.9 = (s32[1,1,16,2]{2,3,1,0:T(2,128)S(1)}, s32[1,1,16,2]{2,3,1,0:T(2,128)}, u32[]{:S(2)}) copy-start(s32[1,1,16,2]{2,3,1,0:T(2,128)} %param.18) | copy-start | bytes 388
  7.2 19.1 %copy-start.3 = (f32[32,1,3,384]{3,1,2,0:T(1,128)S(1)}, f32[32,1,3,384]{3,1,2,0:T(1,128)}, u32[]{:S(2)}) copy-start(f32[32,1,3,384]{3,1,2,0:T(1,128)} %param.11) | copy-start | bytes 442372
  7.2 19.3 %copy-start.4 = (f32[32,1,3,384]{3,1,2,0:T(1,128)S(1)}, f32[32,1,3,384]{3,1,2,0:T(1,128)}, u32[]{:S(2)}) copy-start(f32[32,1,3,384]{3,1,2,0:T(1,128)} %param.13) | copy-start | bytes 442372
  7.2 19.4 %copy-start.5 = (f32[32,1,3,256]{3,1,2,0:T(1,128)S(1)}, f32[32,1,3,256]{3,1,2,0:T(1,128)}, u32[]{:S(2)}) copy-start(f32[32,1,3,256]{3,1,2,0:T(1,128)} %param.10) | copy-start | bytes 294916
  7.2 19.6 %copy-start.6 = (f32[32,1,384]{2,1,0:T(1,128)S(1)}, f32[32,1,384]{2,1,0:T(1,128)}, u32[]{:S(2)}) copy-start(f32[32,1,384]{2,1,0:T(1,128)} %param.12) | copy-start | bytes 147460
  7.2 64.7 %all-gather.3.cloned.1.call-start = ((), (), s32[]{:S(2)}) async-start(), calls=%async_computation.3 | async-start | bytes 4718592 | tf_op jit(solution)/shard_map/all_gather | solution.py:242
  10.7 78.3 %all-to-all-start = ((f32[32,40,256]{2,1,0:T(8,128)}), f32[32,40,256]{2,1,0:T(8,128)S(1)}, u32[]{:S(2)}, u32[]{:S(2)}) async-start(f32[32,40,256]{2,1,0:T(8,128)} %broadcast_in_dim.7), calls=%async_computation | async-start | bytes 2621440 | tf_op jit(solution)/shard_map/all_to_all | solution.py:214
  24.2 25.7 %collective-permute-start = (s32[16,2]{0,1:T(2,128)S(1)}, s32[16,2]{0,1:T(2,128)S(1)}, u32[]{:S(2)}, u32[]{:S(2)}) collective-permute-start(s32[16,2]{0,1:T(2,128)S(1)} %bitcast.51), channel_id=1, source_target_pairs={{0,1},{1,0},{2,3},{3,2},{4,5},{5,4},{6,7},{7,6},{8,9},{9,8},{10,11... | collective-permute-start | bytes 392 | tf_op jit(solution)/shard_map/ppermute | solution.py:244
  26.9 50.1 %copy-start.8 = (s32[32,1,9]{0,1,2:T(1,128)S(1)}, s32[32,1,9]{0,1,2:T(1,128)}, u32[]{:S(2)}) copy-start(s32[32,1,9]{0,1,2:T(1,128)} %param.19) | copy-start | bytes 3460
  26.9 50.3 %copy-start.7 = (f32[32,1,256]{2,1,0:T(1,128)S(1)}, f32[32,1,256]{2,1,0:T(1,128)}, u32[]{:S(2)}) copy-start(f32[32,1,256]{2,1,0:T(1,128)} %param.14) | copy-start | bytes 98308
  26.9 50.3 %copy-start = (s32[1,1024]{1,0:T(1,128)S(1)}, s32[1,1024]{1,0:T(1,128)}, u32[]{:S(2)}) copy-start(s32[1,1024]{1,0:T(1,128)} %plan_ref.1) | copy-start | bytes 12292
  49.8 22.2 %copy-start.1 = (f32[8,128]{1,0:T(8,128)}, f32[8,128]{1,0:T(8,128)S(1)}, u32[]{:S(2)}) copy-start(f32[8,128]{1,0:T(8,128)S(1)} %get-tuple-element.11.done_ref) | copy-start | bytes 12292
  75.0 4.0 %collective-permute-start.1 = (bf16[16,128,128]{2,1,0:T(8,128)(2,1)}, bf16[16,128,128]{2,1,0:T(8,128)(2,1)S(1)}, u32[]{:S(2)}, u32[]{:S(2)}) collective-permute-start(bf16[16,128,128]{2,1,0:T(8,128)(2,1)} %get-tuple-element.13), channel_id=1, source_target_pairs={{0,1},{1,0},{2,3},{3,2},{4,5},{5,4},{6,7},{7,6},{8,9},{9,8},{10,11... | collective-permute-start | bytes 1572872 | tf_op jit(solution)/shard_map/ppermute | solution.py:279
  79.1 1.0 copy-start.2
  99.4 50.0 %all-to-all-start.1 = ((bf16[512,8,128]{2,1,0:T(8,128)(2,1)}), bf16[512,8,128]{2,1,0:T(8,128)(2,1)S(1)}, u32[]{:S(2)}, u32[]{:S(2)}) async-start(bf16[512,8,128]{2,1,0:T(8,128)(2,1)} %bitcast.9), calls=%async_computation.1 | async-start | bytes 2097152 | tf_op jit(solution)/shard_map/all_to_all | solution.py:308
Sparse Core Ops, SparseCore 0:
  10.1 61.7 all-gather.2

commit v3 on v2

--- a/solution.py
+++ b/solution.py
@@ -6,7 +6,6 @@
 from jax.sharding import PartitionSpec as P
 
 LIST = 3
-BLK = ("y", "core")
 xc_scale = 0.98474502
 soft_square = 0.01
 log2_e = 1.4426950408889634
@@ -59,32 +58,23 @@
     lax.fori_loop(0, slots, one, 0)
 
 
-def pick_kernel(places_ref, blocks_ref, done_ref, own_ref, other_ref, sems):
+def pick_kernel(asked_ref, blocks_ref, out_ref):
+    for e in range(out_ref.shape[0]):
+        out_ref[e] = blocks_ref[asked_ref[e]]
+
+
+def spread_kernel(hartree_ref, listed_ref, done_ref, out_ref):
     del done_ref
-    half = own_ref.shape[0]
-    copies = []
-    for n in range(2 * half):
-        to = other_ref.at[n] if n < half else own_ref.at[n - half]
-        copies.append(pltpu.make_async_copy(blocks_ref.at[places_ref[n]], to, sems.at[n]))
-    for copy in copies:
-        copy.start()
-    for copy in copies:
-        copy.wait()
-
-
-def density_kernel(pairs_ref, core_ref, basis_ref, own_ref, other_ref, rho_ref, table_ref, sub_ref):
+    slots = hartree_ref.shape[0]
+    out_ref[:slots] = hartree_ref[...]
+    out_ref[slots:] = jnp.broadcast_to(listed_ref[...], (out_ref.shape[0] - slots, out_ref.shape[1]))
+
+
+def density_kernel(pairs_ref, basis_ref, table_ref, rho_ref, sub_ref):
     slots = basis_ref.shape[0]
-    half, block, _ = own_ref.shape
+    block = table_ref.shape[1]
     unroll = sub_ref.shape[0]
     start = pl.program_id(0) * slots
-
-    @pl.when(start == 0)
-    def _():
-        core = core_ref[0]
-        for n in range(half):
-            base = 4 * (n // 2) + n % 2
-            table_ref[base + 2 * core] = own_ref[n]
-            table_ref[base + 2 * (1 - core)] = other_ref[n]
 
     def group(turn, carry):
         for u in range(unroll):
@@ -163,30 +153,27 @@
             out_ref[:, 1, c] = jnp.where(low, pltpu.roll(first, 4, 1), second).astype(bf16)
 
 
-def add_kernel(target_ref, received_ref, rho_ref, out_ref):
-    block = out_ref.shape[2]
-    parts = rho_ref.shape[1] // block
-    slots = rho_ref.shape[0]
-    rows = out_ref.shape[1] - parts * slots
+def add_kernel(target_ref, received_ref, out_ref):
+    rows = out_ref.shape[1]
     length = target_ref.shape[1]
     chosen = lax.broadcasted_iota(jnp.int32, (rows, length), 0) == target_ref[...]
     total = jnp.dot(
         chosen.astype(f32).astype(bf16), received_ref[...], preferred_element_type=f32
     ).astype(bf16)
-    rho = rho_ref[...].astype(bf16)
     for h in range(out_ref.shape[0]):
-        out_ref[h, :rows, :] = total
-        for n in range(parts):
-            out_ref[h, rows + n * slots : rows + (n + 1) * slots, :] = rho[
-                :, n * block : (n + 1) * block
-            ]
-
-
-def merge_kernel(received_ref, plan_ref, rank_ref, out_ref, density_ref):
+        out_ref[h] = total
+
+
+def place_kernel(spread_ref, plan_ref, rank_ref, density_ref):
+    slots = density_ref.shape[0]
+    length = plan_ref.shape[1]
+    own = lax.broadcasted_iota(jnp.int32, (slots, length), 0) + rank_ref[0] * slots
+    chosen = (own == plan_ref[...]).astype(f32).astype(bf16)
+    density_ref[...] = jnp.dot(chosen, spread_ref[...], preferred_element_type=f32)
+
+
+def merge_kernel(received_ref, out_ref):
     half, _, rows, block = received_ref.shape
-    slots = density_ref.shape[0]
-    parts = density_ref.shape[1] // block
-    rows -= parts * slots
     low = lax.broadcasted_iota(jnp.int32, (1, 8, block), 1) < 4
     for at in range(0, rows, 16):
         even = received_ref[:, 0, at : at + 16, :].astype(f32)
@@ -199,14 +186,6 @@
             out_ref[place + 1] = jnp.where(low, pltpu.roll(first, 4, 1), second).reshape(
                 8 * half, block
             )
-    length = plan_ref.shape[1]
-    own = lax.broadcasted_iota(jnp.int32, (slots, length), 0) + rank_ref[0] * slots
-    chosen = (own == plan_ref[...]).astype(f32).astype(bf16)
-    for n in range(parts):
-        values = received_ref[:, :, rows + n * slots : rows + (n + 1) * slots, :]
-        density_ref[:, n * block : (n + 1) * block] = jnp.dot(
-            chosen, values.reshape(length, block), preferred_element_type=f32
-        )
 
 
 def to_all(value, axis):
@@ -228,25 +207,26 @@
 ):
     slots, _, _, grid = points.shape
     ranks = lax.axis_size("batch")
-    columns = lax.axis_size(BLK)
+    columns = lax.axis_size("blk")
     per_owner = pair_lists.shape[3]
     held, block, _ = density_blocks.shape
     entries = columns * per_owner
     width = LIST * block
     piece = block // ranks
     rank = lax.axis_index("batch")
-    core = lax.axis_index("core")
-    swap = [(0, 1), (1, 0)]
     plan_rows = lax.dynamic_slice_in_dim(load_plan[0], rank * slots, slots)
 
-    near = lax.all_gather(density_blocks, "y", axis=0, tiled=True)
     wanted = pair_lists[0, 0]
-    asked = lax.ppermute(wanted, "core", swap)
-
-    listed = jnp.pad(wanted.reshape(1, entries).astype(f32), ((0, 7), (0, grid - entries)))
-    stored = to_all(jnp.concatenate([hartree[:, 0], listed]), "batch")
-    stride = stored.shape[1]
-    stored = stored.reshape(ranks * stride, grid)
+    asked = lax.all_to_all(wanted, "blk", split_axis=0, concat_axis=0, tiled=True).reshape(entries)
+    sent = call(
+        pick_kernel,
+        jax.ShapeDtypeStruct((entries, block, block), bf16),
+        [SMEM, VMEM],
+        moved=entries * block * block * 4,
+    )(asked, density_blocks)
+    table = lax.all_to_all(
+        sent.reshape(columns, per_owner * block, block), "blk", split_axis=0, concat_axis=0, tiled=True
+    ).reshape(entries, block, block)
 
     params = jnp.concatenate(
         [centers[:, 0], exponents, angular[:, 0], jnp.zeros((slots, 1, width), f32)], axis=1
@@ -264,32 +244,33 @@
         moved=slots * width * grid * 2,
     )(points[:, 0], params)
 
-    sides = jnp.stack([asked, wanted]).reshape(2, columns // 2, 2, per_owner)
-    sides = lax.dynamic_index_in_dim(sides, core, 2, keepdims=False)
-    sides = sides + held * jnp.arange(columns // 2, dtype=jnp.int32)[None, :, None]
-    half = jax.ShapeDtypeStruct((entries // 2, block, block), bf16)
-    own, other = call(
-        pick_kernel,
-        (half, half),
-        [SMEM, HBM, HBM],
-        [pltpu.SemaphoreType.DMA((entries,))],
-        limit=60,
-        moved=entries * block * block * 4,
-    )(sides.reshape(entries), near, done)
-    other = lax.ppermute(other, "core", swap)
+    stride = slots + 8
+    stored = to_all(
+        call(
+            spread_kernel,
+            jax.ShapeDtypeStruct((stride, grid), f32),
+            [VMEM, VMEM, HBM],
+        )(
+            hartree[:, 0],
+            jnp.pad(asked.reshape(1, entries).astype(f32), ((0, 0), (0, grid - entries))),
+            done,
+        ),
+        "batch",
+    ).reshape(ranks * stride, grid)
 
     pairs = batch_pairs.reshape(slots * LIST * LIST)
     unroll = 2
     rho = call(
         density_kernel,
         jax.ShapeDtypeStruct((slots, grid), f32),
-        [SMEM, SMEM, rows_of(group, width, grid), VMEM, VMEM],
-        [pltpu.VMEM((entries, block, block), bf16), pltpu.VMEM((unroll, width, width), bf16)],
+        [SMEM, rows_of(group, width, grid), VMEM],
+        [pltpu.VMEM((unroll, width, width), bf16)],
         grid=steps,
         limit=48,
         flops=slots * width * width * grid * 2,
         moved=slots * width * grid * 2,
-    )(pairs, core.reshape(1), basis, own, other)
+    )(pairs, basis, table)
+    spread = to_all(rho.astype(bf16), "batch").reshape(ranks * slots, grid)
     partial, lists = call(
         matrix_kernel,
         (
@@ -305,59 +286,57 @@
     )(pairs, plan_rows, basis, rho, stored, grid_weights[:, 0])
 
     rows = per_owner * piece
+    partial, spread = lax.optimization_barrier((partial, spread))
     received = lax.all_to_all(
         partial.reshape(ranks * columns, rows, block),
-        ("batch",) + BLK,
+        ("batch", "blk"),
         split_axis=0,
         concat_axis=0,
         tiled=True,
     ).reshape(ranks * columns * rows, block)
-
-    asking = lax.all_gather(lists, BLK, axis=0)
-    asking = lax.dynamic_slice_in_dim(asking, lax.axis_index(BLK) * per_owner, per_owner, 2)
-    asking = asking.astype(jnp.int32).transpose(1, 0, 2).reshape(ranks * entries, 1)
-    targets = (asking * piece + jnp.arange(piece, dtype=jnp.int32)[None]).reshape(
+    density = call(
+        place_kernel,
+        jax.ShapeDtypeStruct((slots, grid), f32),
+        [VMEM, VMEM, SMEM],
+        moved=ranks * slots * grid * 2,
+    )(spread, load_plan, rank.reshape(1))
+
+    targets = lists[:, :entries].astype(jnp.int32).reshape(ranks * entries, 1) * piece
+    targets = (targets + jnp.arange(piece, dtype=jnp.int32)[None]).reshape(
         1, ranks * entries * piece
     )
-
-    lines = held * piece + slots * grid // block
     totals = call(
         add_kernel,
-        jax.ShapeDtypeStruct((ranks, lines, block), bf16),
-        [VMEM, VMEM, VMEM],
+        jax.ShapeDtypeStruct((ranks, held * piece, block), bf16),
+        [VMEM, VMEM],
         moved=ranks * columns * rows * block * 2,
-    )(targets, received, rho)
+    )(targets, received)
     gathered = lax.all_to_all(totals, "batch", split_axis=0, concat_axis=0, tiled=True)
-    hamiltonian, density = call(
+    hamiltonian = call(
         merge_kernel,
-        (
-            jax.ShapeDtypeStruct((held, block, block), f32),
-            jax.ShapeDtypeStruct((slots, grid), f32),
-        ),
-        [VMEM, VMEM, SMEM],
+        jax.ShapeDtypeStruct((held, block, block), f32),
+        [VMEM],
         moved=held * block * block * 6,
-    )(gathered.reshape(ranks // 2, 2, lines, block), load_plan, rank.reshape(1))
+    )(gathered.reshape(ranks // 2, 2, held * piece, block))
     return (hamiltonian, density[:, None, :])
 
 
 def solution(mesh):
-    ranks, columns = mesh.devices.shape
-    fine = jax.sharding.Mesh(mesh.devices.reshape(ranks, columns // 2, 2), ("batch",) + BLK)
     return jax.shard_map(
         on_device,
-        mesh=fine,
+        mesh=mesh,
         in_specs=(
-            P("batch", BLK, None, None),
-            P("batch", BLK, None, None),
-            P("batch", BLK, None),
-            P("batch", BLK, None, None),
-            P("batch", BLK, None),
-            P("batch", BLK, None),
-            P(BLK, None),
-            P(BLK, None, None),
-            P("batch", BLK, None, None),
-            P("batch", BLK, None),
+            P("batch", "blk", None, None),
+            P("batch", "blk", None, None),
+            P("batch", "blk", None),
+            P("batch", "blk", None, None),
+            P("batch", "blk", None),
+            P("batch", "blk", None),
+            P("blk", None),
+            P("blk", None, None),
+            P("batch", "blk", None, None),
+            P("batch", "blk", None),
         ),
-        out_specs=(P(BLK, None, None), P("batch", BLK, None)),
+        out_specs=(P("blk", None, None), P("batch", "blk", None)),
         check_vma=False,
     )

time: 200 us -> 192 us (0.960)
  the two profiles are of different devices: /device:TPU:2 before, /device:TPU:8 now
where the time goes in v3:
time: 192 us; the launch traced here: 191 us
  waiting for transfers between devices  81.8 us (43%)
  Pallas kernels  46 us (24%)
  starting transfers between devices  39.8 us (21%)
  blocking collectives  14.5 us (8%)
  local copies, waits for them, and re-layouts  6.61 us (3%)
    all_to_all x1, waiting for transfers between devices, on_device(): lax.all_to_all(partial.reshape(ranks * columns, rows, block), ('batch', '...  32.1 us
    all_to_all x2, waiting for transfers between devices, to_all(): return lax.all_to_all(copies, axis, split_axis=0, concat_axis=0, tiled=True)  31.6 us
    pallas_call x1, Pallas kernels, on_device(): call(basis_kernel, (jax.ShapeDtypeStruct((slots, width, grid), bf16), jax...  22.8 us
    all_to_all x2, starting transfers between devices, to_all(): return lax.all_to_all(copies, axis, split_axis=0, concat_axis=0, tiled=True)  18.1 us
    all_to_all x1, waiting for transfers between devices, on_device(): lax.all_to_all(totals, 'batch', split_axis=0, concat_axis=0, tiled=True)  17.3 us
    all_to_all x1, blocking collectives, on_device(): lax.all_to_all(wanted, 'blk', split_axis=0, concat_axis=0, tiled=True)  14.5 us
    all_to_all x1, starting transfers between devices, on_device(): lax.all_to_all(partial.reshape(ranks * columns, rows, block), ('batch', '...  11.7 us
    pallas_call x1, Pallas kernels, on_device(): call(matrix_kernel, (jax.ShapeDtypeStruct((ranks // 2, 2, columns, per_ow...  10.4 us
  transfers between devices with their start and end apart: 5, of which 5 were waited for; matrix products, arithmetic and copies ran while one was open for 1% of the time, Pallas kernels for 22%

profile of v3, /device:TPU:8, one launch (start us, length us, event | category | flops | bytes accessed | tf_op | source)
XLA Modules:
  0.0 190.6 jit_solution(18108587774633527222)
XLA Ops:
  0.6 0.8 copy.32
  1.4 14.5 %all_to_all.34 = s32[16,1,2]{2,1,0:T(1,128)S(1)} all-to-all(s32[16,1,2]{2,1,0:T(1,128)S(1)} %copy.32), channel_id=1, replica_groups=mesh['batch'=32,'blk'=16] {'blk'}, dimensions={0} | all-to-all | bytes 256 | tf_op jit(solution)/shard_map/all_to_all | solution.py:220
  15.8 0.5 broadcast.23
  16.4 0.7 reduce.7
  17.1 1.0 copy-done
  18.2 1.6 shard_map.114
  19.7 5.1 %all-to-all-start.1 = ((bf16[16,256,128]{2,1,0:T(8,128)(2,1)}), bf16[16,256,128]{2,1,0:T(8,128)(2,1)S(1)}, u32[]{:S(2)}, u32[]{:S(2)}) async-start(bf16[16,256,128]{2,1,0:T(8,128)(2,1)} %bitcast.5), calls=%async_computation.1 | async-start | bytes 2097152 | tf_op jit(solution)/shard_map/all_to_all | solution.py:227
  24.9 0.1 copy.29
  25.0 0.1 copy.30
  25.2 0.4 copy-done.6
  25.6 0.1 maximum_maximum_fusion.params_ref
  25.8 22.8 %shard_map.113 = (bf16[32,384,256]{2,1,0:T(8,128)(2,1)}, f32[8,128]{1,0:T(8,128)S(1)}) custom-call(f32[32,3,256]{2,1,0:T(4,128)S(1)} %copy.31.points_ref, f32[32,8,384]{2,1,0:T(8,128)S(1)} %maximum_maximum_fusion.params_ref), custom_call_target="tpu_custom_call" | custom-call | flops 1258291200 | bytes 6291456 | tf_op jit(solution)/shard_map/pallas_call | solution.py:236
  48.7 0.8 all-to-all-done.1
  49.6 1.1 broadcast_in_dim.9
  50.7 12.4 %all-to-all-start.2 = ((f32[32,40,256]{2,1,0:T(8,128)}), f32[32,40,256]{2,1,0:T(8,128)S(1)}, u32[]{:S(2)}, u32[]{:S(2)}) async-start(f32[32,40,256]{2,1,0:T(8,128)} %broadcast_in_dim.9), calls=%async_computation.2 | async-start | bytes 2621440 | tf_op jit(solution)/shard_map/all_to_all | solution.py:193
  63.2 0.1 reshape.88.pairs_ref
  63.3 8.8 %shard_map.115.rho_ref = f32[32,256]{1,0:T(8,128)S(1)} custom-call(s32[288]{0:T(512)S(1)} %reshape.88.pairs_ref, bf16[32,384,256]{2,1,0:T(8,128)(2,1)} %get-tuple-element.8.basis_ref, bf16[32,128,128]{2,1,0:T(8,128)(2,1)S(1)} %bitcast.34), custom_call_target="tpu_custom_call" | custom-call | flops 2415919104 | bytes 6291456 | tf_op jit(solution)/shard_map/pallas_call | solution.py:263
  72.1 25.0 %all-to-all-done.2 = f32[32,40,256]{2,1,0:T(8,128)S(1)} async-done(((f32[32,40,256]{2,1,0:T(8,128)}), f32[32,40,256]{2,1,0:T(8,128)S(1)}, u32[]{:S(2)}, u32[]{:S(2)}) %all-to-all-start.2) | async-done | bytes 1310752 | tf_op jit(solution)/shard_map/all_to_all | solution.py:193
  97.1 0.9 broadcast_in_dim.10
  98.0 5.7 %all-to-all-start.3 = ((bf16[32,32,256]{2,1,0:T(8,128)(2,1)}), bf16[32,32,256]{2,1,0:T(8,128)(2,1)S(1)}, u32[]{:S(2)}, u32[]{:S(2)}) async-start(bf16[32,32,256]{2,1,0:T(8,128)(2,1)} %broadcast_in_dim.10), calls=%async_computation.3 | async-start | bytes 1048576 | tf_op jit(solution)/shard_map/all_to_all | solution.py:193
  103.8 10.4 %shard_map.117 = (bf16[16,2,16,8,128]{4,3,2,1,0:T(8,128)(2,1)}, f32[32,128]{1,0:T(8,128)S(1)}) custom-call(s32[288]{0:T(512)S(1)} %reshape.88.pairs_ref, s32[32]{0:T(128)S(1)} %dynamic-slice_bitcast_fusion.plan_ref, bf16[32,384,256]{2,1,0:T(8,128)(2,1)} %get-tuple-element.8.basis_ref, f32[32,256]{1,0:T(8,128)S(1)} %shard_map.115.rho_ref, ...), custom_call_target="tpu_custom_call" | custom-call | flops 2415919104 | bytes 6291456 | tf_op jit(solution)/shard_map/pallas_call | solution.py:274
  114.2 6.6 %all-to-all-done.3 = bf16[32,32,256]{2,1,0:T(8,128)(2,1)S(1)} async-done(((bf16[32,32,256]{2,1,0:T(8,128)(2,1)}), bf16[32,32,256]{2,1,0:T(8,128)(2,1)S(1)}, u32[]{:S(2)}, u32[]{:S(2)}) %all-to-all-start.3) | async-done | bytes 524320 | tf_op jit(solution)/shard_map/all_to_all | solution.py:193
  120.8 11.7 %all-to-all-start.4 = ((bf16[512,8,128]{2,1,0:T(8,128)(2,1)}), bf16[512,8,128]{2,1,0:T(8,128)(2,1)S(1)}, u32[]{:S(2)}, u32[]{:S(2)}) async-start(bf16[512,8,128]{2,1,0:T(8,128)(2,1)} %bitcast.9), calls=%async_computation.4 | async-start | bytes 2097152 | tf_op jit(solution)/shard_map/all_to_all | solution.py:290
  132.6 0.2 iota_add_fusion
  132.8 0.3 add.32.target_ref
  133.1 32.1 %all-to-all-done.4 = bf16[512,8,128]{2,1,0:T(8,128)(2,1)S(1)} async-done(((bf16[512,8,128]{2,1,0:T(8,128)(2,1)}), bf16[512,8,128]{2,1,0:T(8,128)(2,1)S(1)}, u32[]{:S(2)}, u32[]{:S(2)}) %all-to-all-start.4) | async-done | bytes 1048608 | tf_op jit(solution)/shard_map/all_to_all | solution.py:290
  165.2 1.2 shard_map.118
  166.3 5.0 %all-to-all-start.5 = ((bf16[32,64,128]{2,1,0:T(8,128)(2,1)}), bf16[32,64,128]{2,1,0:T(8,128)(2,1)S(1)}, u32[]{:S(2)}, u32[]{:S(2)}) async-start(bf16[32,64,128]{2,1,0:T(8,128)(2,1)} %shard_map.118), calls=%async_computation.5 | async-start | bytes 1048576 | tf_op jit(solution)/shard_map/all_to_all | solution.py:314
  171.3 0.2 shard_map.120
  171.5 0.7 copy.33
  172.2 17.3 %all-to-all-done.5 = bf16[32,64,128]{2,1,0:T(8,128)(2,1)S(1)} async-done(((bf16[32,64,128]{2,1,0:T(8,128)(2,1)}), bf16[32,64,128]{2,1,0:T(8,128)(2,1)S(1)}, u32[]{:S(2)}, u32[]{:S(2)}) %all-to-all-start.5) | async-done | bytes 524320 | tf_op jit(solution)/shard_map/all_to_all | solution.py:314
  189.5 1.1 shard_map.119
  (33 shorter events, 0.7 us)
Async XLA Ops:
  17.1 1.0 copy-start
  19.7 5.1 %copy-start.2 = (f32[32,1,3,384]{3,1,2,0:T(1,128)S(1)}, f32[32,1,3,384]{3,1,2,0:T(1,128)}, u32[]{:S(2)}) copy-start(f32[32,1,3,384]{3,1,2,0:T(1,128)} %param.11) | copy-start | bytes 442372
  19.7 5.2 %copy-start.3 = (f32[32,1,3,384]{3,1,2,0:T(1,128)S(1)}, f32[32,1,3,384]{3,1,2,0:T(1,128)}, u32[]{:S(2)}) copy-start(f32[32,1,3,384]{3,1,2,0:T(1,128)} %param.13) | copy-start | bytes 442372
  19.7 5.4 %copy-start.4 = (f32[32,1,3,256]{3,1,2,0:T(1,128)S(1)}, f32[32,1,3,256]{3,1,2,0:T(1,128)}, u32[]{:S(2)}) copy-start(f32[32,1,3,256]{3,1,2,0:T(1,128)} %param.10) | copy-start | bytes 294916
  19.7 29.8 %all-to-all-start.1 = ((bf16[16,256,128]{2,1,0:T(8,128)(2,1)}), bf16[16,256,128]{2,1,0:T(8,128)(2,1)S(1)}, u32[]{:S(2)}, u32[]{:S(2)}) async-start(bf16[16,256,128]{2,1,0:T(8,128)(2,1)} %bitcast.5), calls=%async_computation.1 | async-start | bytes 2097152 | tf_op jit(solution)/shard_map/all_to_all | solution.py:227
  24.8 0.8 copy-start.6
  24.8 0.8 copy-start.5
  50.7 12.4 %copy-start.8 = (s32[32,1,9]{0,1,2:T(1,128)S(1)}, s32[32,1,9]{0,1,2:T(1,128)}, u32[]{:S(2)}) copy-start(s32[32,1,9]{0,1,2:T(1,128)} %param.19) | copy-start | bytes 3460
  50.7 46.4 %all-to-all-start.2 = ((f32[32,40,256]{2,1,0:T(8,128)}), f32[32,40,256]{2,1,0:T(8,128)S(1)}, u32[]{:S(2)}, u32[]{:S(2)}) async-start(f32[32,40,256]{2,1,0:T(8,128)} %broadcast_in_dim.9), calls=%async_computation.2 | async-start | bytes 2621440 | tf_op jit(solution)/shard_map/all_to_all | solution.py:193
  72.1 31.6 %copy-start.7 = (f32[32,1,256]{2,1,0:T(1,128)S(1)}, f32[32,1,256]{2,1,0:T(1,128)}, u32[]{:S(2)}) copy-start(f32[32,1,256]{2,1,0:T(1,128)} %param.14) | copy-start | bytes 98308
  72.1 31.6 %copy-start.1 = (s32[1,1024]{1,0:T(1,128)S(1)}, s32[1,1024]{1,0:T(1,128)}, u32[]{:S(2)}) copy-start(s32[1,1024]{1,0:T(1,128)} %plan_ref.1) | copy-start | bytes 12292
  98.0 22.8 %all-to-all-start.3 = ((bf16[32,32,256]{2,1,0:T(8,128)(2,1)}), bf16[32,32,256]{2,1,0:T(8,128)(2,1)S(1)}, u32[]{:S(2)}, u32[]{:S(2)}) async-start(bf16[32,32,256]{2,1,0:T(8,128)(2,1)} %broadcast_in_dim.10), calls=%async_computation.3 | async-start | bytes 1048576 | tf_op jit(solution)/shard_map/all_to_all | solution.py:193
  120.8 44.4 %all-to-all-start.4 = ((bf16[512,8,128]{2,1,0:T(8,128)(2,1)}), bf16[512,8,128]{2,1,0:T(8,128)(2,1)S(1)}, u32[]{:S(2)}, u32[]{:S(2)}) async-start(bf16[512,8,128]{2,1,0:T(8,128)(2,1)} %bitcast.9), calls=%async_computation.4 | async-start | bytes 2097152 | tf_op jit(solution)/shard_map/all_to_all | solution.py:290
  166.3 23.1 %all-to-all-start.5 = ((bf16[32,64,128]{2,1,0:T(8,128)(2,1)}), bf16[32,64,128]{2,1,0:T(8,128)(2,1)S(1)}, u32[]{:S(2)}, u32[]{:S(2)}) async-start(bf16[32,64,128]{2,1,0:T(8,128)(2,1)} %shard_map.118), calls=%async_computation.5 | async-start | bytes 1048576 | tf_op jit(solution)/shard_map/all_to_all | solution.py:314

commit v4 on v3

--- a/solution.py
+++ b/solution.py
@@ -8,6 +8,7 @@
 LIST = 3
 xc_scale = 0.98474502
 soft_square = 0.01
+zero_exchange = xc_scale * soft_square ** (1.0 / 6.0)
 log2_e = 1.4426950408889634
 
 bf16 = jnp.bfloat16
@@ -65,12 +66,14 @@
 
 def spread_kernel(hartree_ref, listed_ref, done_ref, out_ref):
     del done_ref
-    slots = hartree_ref.shape[0]
-    out_ref[:slots] = hartree_ref[...]
-    out_ref[slots:] = jnp.broadcast_to(listed_ref[...], (out_ref.shape[0] - slots, out_ref.shape[1]))
-
-
-def density_kernel(pairs_ref, basis_ref, table_ref, rho_ref, sub_ref):
+    _, rows, grid = out_ref.shape
+    below = jnp.broadcast_to(listed_ref[...], (rows - hartree_ref.shape[0], grid))
+    lines = jnp.concatenate([hartree_ref[...] - zero_exchange, below]).astype(bf16)
+    for h in range(out_ref.shape[0]):
+        out_ref[h] = lines
+
+
+def density_kernel(pairs_ref, basis_ref, table_ref, rho_ref, copies_ref, sub_ref):
     slots = basis_ref.shape[0]
     block = table_ref.shape[1]
     unroll = sub_ref.shape[0]
@@ -93,31 +96,38 @@
 
     lax.fori_loop(0, slots // unroll, group, 0)
 
+    @pl.when(start == rho_ref.shape[0] - slots)
+    def _():
+        sent = rho_ref[...].astype(bf16)
+        for h in range(copies_ref.shape[0]):
+            copies_ref[h] = sent
+
 
 def matrix_kernel(
     pairs_ref, plan_ref, basis_ref, rho_ref, hartree_ref, weights_ref,
-    out_ref, lists_ref, sums_ref, factor_ref,
+    out_ref, lists_ref, sums_ref, factor_ref, stored_ref,
 ):
     slots = basis_ref.shape[0]
     total = rho_ref.shape[0]
     entries, block, _ = sums_ref.shape
-    stride = hartree_ref.shape[0] // lists_ref.shape[0]
+    stride = hartree_ref.shape[1]
     unroll = 2
     start = pl.program_id(0) * slots
 
     @pl.when(start == 0)
     def _():
         for r in range(lists_ref.shape[0]):
-            at = r * stride + total
-            lists_ref[r : r + 1, :] = hartree_ref[at : at + 1, :block]
+            lines = hartree_ref[r].astype(f32)
+            stored_ref[r * stride : (r + 1) * stride, :] = lines
+            lists_ref[r : r + 1, :] = lines[total : total + 1, :block]
         for s in range(total):
             at = plan_ref[s]
-            factor_ref[s : s + 1, :] = hartree_ref[
+            factor_ref[s : s + 1, :] = stored_ref[
                 pl.ds(lax.div(at, total) * stride + lax.rem(at, total), 1), :
             ]
         rho = rho_ref[...]
         root = jnp.exp2(jnp.log2(rho * rho + soft_square) * (1.0 / 6.0))
-        factor_ref[...] = weights_ref[...] * (factor_ref[...] - xc_scale * root)
+        factor_ref[...] = weights_ref[...] * (factor_ref[...] + (zero_exchange - xc_scale * root))
 
         def clear(e, carry):
             sums_ref[e] = jnp.zeros((block, block), f32)
@@ -186,11 +196,6 @@
             out_ref[place + 1] = jnp.where(low, pltpu.roll(first, 4, 1), second).reshape(
                 8 * half, block
             )
-
-
-def to_all(value, axis):
-    copies = jnp.broadcast_to(value[None], (lax.axis_size(axis),) + value.shape)
-    return lax.all_to_all(copies, axis, split_axis=0, concat_axis=0, tiled=True)
 
 
 def on_device(
@@ -245,24 +250,25 @@
     )(points[:, 0], params)
 
     stride = slots + 8
-    stored = to_all(
-        call(
-            spread_kernel,
-            jax.ShapeDtypeStruct((stride, grid), f32),
-            [VMEM, VMEM, HBM],
-        )(
-            hartree[:, 0],
-            jnp.pad(asked.reshape(1, entries).astype(f32), ((0, 0), (0, grid - entries))),
-            done,
-        ),
-        "batch",
-    ).reshape(ranks * stride, grid)
+    lines = call(
+        spread_kernel,
+        jax.ShapeDtypeStruct((ranks, stride, grid), bf16),
+        [VMEM, VMEM, HBM],
+    )(
+        hartree[:, 0],
+        jnp.pad(asked.reshape(1, entries).astype(f32), ((0, 0), (0, grid - entries))),
+        done,
+    )
+    stored = lax.all_to_all(lines, "batch", split_axis=0, concat_axis=0, tiled=True)
 
     pairs = batch_pairs.reshape(slots * LIST * LIST)
     unroll = 2
-    rho = call(
+    rho, copies = call(
         density_kernel,
-        jax.ShapeDtypeStruct((slots, grid), f32),
+        (
+            jax.ShapeDtypeStruct((slots, grid), f32),
+            jax.ShapeDtypeStruct((ranks, slots, grid), bf16),
+        ),
         [SMEM, rows_of(group, width, grid), VMEM],
         [pltpu.VMEM((unroll, width, width), bf16)],
         grid=steps,
@@ -270,7 +276,9 @@
         flops=slots * width * width * grid * 2,
         moved=slots * width * grid * 2,
     )(pairs, basis, table)
-    spread = to_all(rho.astype(bf16), "batch").reshape(ranks * slots, grid)
+    spread = lax.all_to_all(copies, "batch", split_axis=0, concat_axis=0, tiled=True).reshape(
+        ranks * slots, grid
+    )
     partial, lists = call(
         matrix_kernel,
         (
@@ -278,7 +286,11 @@
             jax.ShapeDtypeStruct((ranks, block), f32),
         ),
         [SMEM, SMEM, rows_of(group, width, grid), VMEM, VMEM, VMEM],
-        [pltpu.VMEM((entries, block, block), f32), pltpu.VMEM((slots, grid), f32)],
+        [
+            pltpu.VMEM((entries, block, block), f32),
+            pltpu.VMEM((slots, grid), f32),
+            pltpu.VMEM((ranks * stride, grid), f32),
+        ],
         grid=steps,
         limit=48,
         flops=slots * width * width * grid * 2,

time: 192 us -> 179 us (0.932)
  waiting for transfers between devices: 81.8 us -> 66.4 us
    all_to_all x2, waiting for transfers between devices: 31.6 us -> 17.2 us  [the longest x1 10.7 us: on_device(): lax.all_to_all(lines, 'batch', split_axis=0, concat_axis=0, tiled=True)]
    unnamed x25 -> x15, local copies, waits for them, and re-layouts: 2.22 us -> 5.3 us
    broadcast_in_dim x2 -> x0, local copies, waits for them, and re-layouts: 2.01 us -> none  [to_all(): copies = jnp.broadcast_to(value[None], (lax.axis_size(axis),) + value.shape)]
  transfers between devices with their start and end apart: 5 -> 5, of which waited for: 5 -> 4; matrix products, arithmetic and copies ran while one was open for 1% -> 4% of each run, Pallas kernels for 22% -> 25%
where the time goes in v4:
time: 179 us; the launch traced here: 178 us
  waiting for transfers between devices  66.4 us (37%)
  Pallas kernels  47.8 us (27%)
  starting transfers between devices  39.3 us (22%)
  blocking collectives  14.5 us (8%)
  local copies, waits for them, and re-layouts  7.68 us (4%)
  other arithmetic  1.84 us (1%)
    all_to_all x1, waiting for transfers between devices, on_device(): lax.all_to_all(partial.reshape(ranks * columns, rows, block), ('batch', '...  32 us
    pallas_call x1, Pallas kernels, on_device(): call(basis_kernel, (jax.ShapeDtypeStruct((slots, width, grid), bf16), jax...  22.8 us
    all_to_all x1, waiting for transfers between devices, on_device(): lax.all_to_all(totals, 'batch', split_axis=0, concat_axis=0, tiled=True)  17.3 us
    all_to_all x1, blocking collectives, on_device(): lax.all_to_all(wanted, 'blk', split_axis=0, concat_axis=0, tiled=True)  14.5 us
    all_to_all x1, starting transfers between devices, on_device(): lax.all_to_all(lines, 'batch', split_axis=0, concat_axis=0, tiled=True)  12.3 us
    all_to_all x1, starting transfers between devices, on_device(): lax.all_to_all(partial.reshape(ranks * columns, rows, block), ('batch', '...  12.2 us
    all_to_all x1, waiting for transfers between devices, on_device(): lax.all_to_all(lines, 'batch', split_axis=0, concat_axis=0, tiled=True)  10.7 us
    pallas_call x1, Pallas kernels, on_device(): call(matrix_kernel, (jax.ShapeDtypeStruct((ranks // 2, 2, columns, per_ow...  10.4 us
  transfers between devices with their start and end apart: 5, of which 4 were waited for; matrix products, arithmetic and copies ran while one was open for 4% of the time, Pallas kernels for 25%

profile of v4, /device:TPU:8, one launch (start us, length us, event | category | flops | bytes accessed | tf_op | source)
XLA Modules:
  0.0 178.3 jit_solution(14163721008735997004)
XLA Ops:
  0.6 0.8 copy.32
  1.4 14.5 %all_to_all.34 = s32[16,1,2]{2,1,0:T(1,128)S(1)} all-to-all(s32[16,1,2]{2,1,0:T(1,128)S(1)} %copy.32), channel_id=1, replica_groups=mesh['batch'=32,'blk'=16] {'blk'}, dimensions={0} | all-to-all | bytes 256 | tf_op jit(solution)/shard_map/all_to_all | solution.py:225
  15.8 0.5 broadcast.21
  16.4 0.7 reduce.7
  17.1 1.0 copy-done
  18.2 1.6 shard_map.114
  19.7 4.9 %all-to-all-start.1 = ((bf16[16,256,128]{2,1,0:T(8,128)(2,1)}), bf16[16,256,128]{2,1,0:T(8,128)(2,1)S(1)}, u32[]{:S(2)}, u32[]{:S(2)}) async-start(bf16[16,256,128]{2,1,0:T(8,128)(2,1)} %bitcast.5), calls=%async_computation.1 | async-start | bytes 2097152 | tf_op jit(solution)/shard_map/all_to_all | solution.py:232
  24.7 0.8 copy.45
  25.4 0.9 copy.43
  26.4 0.9 copy.42
  27.4 0.9 copy.41
  28.4 0.1 copy.30
  28.5 0.9 maximum_maximum_fusion.params_ref
  29.5 22.8 %shard_map.113 = (bf16[32,384,256]{2,1,0:T(8,128)(2,1)}, f32[8,128]{1,0:T(8,128)S(1)}) custom-call(f32[32,3,256]{2,1,0:T(4,128)S(1)} %copy.31.points_ref, f32[32,8,384]{2,1,0:T(8,128)S(1)} %maximum_maximum_fusion.params_ref), custom_call_target="tpu_custom_call" | custom-call | flops 1258291200 | bytes 6291456 | tf_op jit(solution)/shard_map/pallas_call | solution.py:241
  52.4 0.9 shard_map.116
  53.3 12.3 %all-to-all-start.2 = ((bf16[32,40,256]{2,1,0:T(8,128)(2,1)}), bf16[32,40,256]{2,1,0:T(8,128)(2,1)S(1)}, u32[]{:S(2)}, u32[]{:S(2)}) async-start(bf16[32,40,256]{2,1,0:T(8,128)(2,1)} %shard_map.116), calls=%async_computation.2 | async-start | bytes 1310720 | tf_op jit(solution)/shard_map/all_to_all | solution.py:262
  65.7 0.1 reshape.83.pairs_ref
  65.8 9.7 %shard_map.115 = (f32[32,256]{1,0:T(8,128)S(1)}, bf16[32,32,256]{2,1,0:T(8,128)(2,1)}) custom-call(s32[288]{0:T(512)S(1)} %reshape.83.pairs_ref, bf16[32,384,256]{2,1,0:T(8,128)(2,1)} %get-tuple-element.10.basis_ref, bf16[32,128,128]{2,1,0:T(8,128)(2,1)S(1)} %bitcast.32), custom_call_target="tpu_custom_call" | custom-call | flops 2415919104 | bytes 6291456 | tf_op jit(solution)/shard_map/pallas_call | solution.py:266
  75.5 10.7 %all-to-all-done.2.hartree_ref = bf16[32,40,256]{2,1,0:T(8,128)(2,1)S(1)} async-done(((bf16[32,40,256]{2,1,0:T(8,128)(2,1)}), bf16[32,40,256]{2,1,0:T(8,128)(2,1)S(1)}, u32[]{:S(2)}, u32[]{:S(2)}) %all-to-all-start.2) | async-done | bytes 655392 | tf_op jit(solution)/shard_map/all_to_all | solution.py:262
  86.1 5.0 %all-to-all-start.3 = ((bf16[32,32,256]{2,1,0:T(8,128)(2,1)}), bf16[32,32,256]{2,1,0:T(8,128)(2,1)S(1)}, u32[]{:S(2)}, u32[]{:S(2)}) async-start(bf16[32,32,256]{2,1,0:T(8,128)(2,1)} %get-tuple-element.15), calls=%async_computation.3 | async-start | bytes 1048576 | tf_op jit(solution)/shard_map/all_to_all | solution.py:279
  91.2 10.4 %shard_map.117 = (bf16[16,2,16,8,128]{4,3,2,1,0:T(8,128)(2,1)}, f32[32,128]{1,0:T(8,128)S(1)}) custom-call(s32[288]{0:T(512)S(1)} %reshape.83.pairs_ref, s32[32]{0:T(128)S(1)} %dynamic-slice_bitcast_fusion.plan_ref, bf16[32,384,256]{2,1,0:T(8,128)(2,1)} %get-tuple-element.10.basis_ref, f32[32,256]{1,0:T(8,128)S(1)} %get-tuple-element.11.rho_ref, ...), custom_call_target="tpu_custom_call" | custom-call | flops 2415919104 | bytes 6291456 | tf_op jit(solution)/shard_map/pallas_call | solution.py:282
  101.7 6.5 %all-to-all-done.3 = bf16[32,32,256]{2,1,0:T(8,128)(2,1)S(1)} async-done(((bf16[32,32,256]{2,1,0:T(8,128)(2,1)}), bf16[32,32,256]{2,1,0:T(8,128)(2,1)S(1)}, u32[]{:S(2)}, u32[]{:S(2)}) %all-to-all-start.3) | async-done | bytes 524320 | tf_op jit(solution)/shard_map/all_to_all | solution.py:279
  108.1 12.2 %all-to-all-start.4 = ((bf16[512,8,128]{2,1,0:T(8,128)(2,1)}), bf16[512,8,128]{2,1,0:T(8,128)(2,1)S(1)}, u32[]{:S(2)}, u32[]{:S(2)}) async-start(bf16[512,8,128]{2,1,0:T(8,128)(2,1)} %bitcast.8), calls=%async_computation.4 | async-start | bytes 2097152 | tf_op jit(solution)/shard_map/all_to_all | solution.py:302
  120.4 0.2 iota_add_fusion
  120.6 0.3 add.32.target_ref
  121.0 32.0 %all-to-all-done.4 = bf16[512,8,128]{2,1,0:T(8,128)(2,1)S(1)} async-done(((bf16[512,8,128]{2,1,0:T(8,128)(2,1)}), bf16[512,8,128]{2,1,0:T(8,128)(2,1)S(1)}, u32[]{:S(2)}, u32[]{:S(2)}) %all-to-all-start.4) | async-done | bytes 1048608 | tf_op jit(solution)/shard_map/all_to_all | solution.py:302
  152.9 1.2 shard_map.118
  154.1 5.0 %all-to-all-start.5 = ((bf16[32,64,128]{2,1,0:T(8,128)(2,1)}), bf16[32,64,128]{2,1,0:T(8,128)(2,1)S(1)}, u32[]{:S(2)}, u32[]{:S(2)}) async-start(bf16[32,64,128]{2,1,0:T(8,128)(2,1)} %shard_map.118), calls=%async_computation.5 | async-start | bytes 1048576 | tf_op jit(solution)/shard_map/all_to_all | solution.py:326
  159.1 0.2 shard_map.120
  159.3 0.7 copy.33
  159.9 17.3 %all-to-all-done.5 = bf16[32,64,128]{2,1,0:T(8,128)(2,1)S(1)} async-done(((bf16[32,64,128]{2,1,0:T(8,128)(2,1)}), bf16[32,64,128]{2,1,0:T(8,128)(2,1)S(1)}, u32[]{:S(2)}, u32[]{:S(2)}) %all-to-all-start.5) | async-done | bytes 524320 | tf_op jit(solution)/shard_map/all_to_all | solution.py:326
  177.2 1.1 shard_map.119
  (20 shorter events, 0.7 us)
Async XLA Ops:
  17.1 1.0 copy-start
  18.2 47.4 %copy-start.3 = (s32[32,1,9]{0,1,2:T(1,128)S(1)}, s32[32,1,9]{0,1,2:T(1,128)}, u32[]{:S(2)}) copy-start(s32[32,1,9]{0,1,2:T(1,128)} %param.19) | copy-start | bytes 3460
  19.7 33.6 %all-to-all-start.1 = ((bf16[16,256,128]{2,1,0:T(8,128)(2,1)}), bf16[16,256,128]{2,1,0:T(8,128)(2,1)S(1)}, u32[]{:S(2)}, u32[]{:S(2)}) async-start(bf16[16,256,128]{2,1,0:T(8,128)(2,1)} %bitcast.5), calls=%async_computation.1 | async-start | bytes 2097152 | tf_op jit(solution)/shard_map/all_to_all | solution.py:232
  52.3 38.8 %copy-start.2 = (f32[32,1,256]{2,1,0:T(1,128)S(1)}, f32[32,1,256]{2,1,0:T(1,128)}, u32[]{:S(2)}) copy-start(f32[32,1,256]{2,1,0:T(1,128)} %param.14) | copy-start | bytes 98308
  52.3 38.8 %copy-start.1 = (s32[1,1024]{1,0:T(1,128)S(1)}, s32[1,1024]{1,0:T(1,128)}, u32[]{:S(2)}) copy-start(s32[1,1024]{1,0:T(1,128)} %plan_ref.1) | copy-start | bytes 12292
  53.3 32.8 %all-to-all-start.2 = ((bf16[32,40,256]{2,1,0:T(8,128)(2,1)}), bf16[32,40,256]{2,1,0:T(8,128)(2,1)S(1)}, u32[]{:S(2)}, u32[]{:S(2)}) async-start(bf16[32,40,256]{2,1,0:T(8,128)(2,1)} %shard_map.116), calls=%async_computation.2 | async-start | bytes 1310720 | tf_op jit(solution)/shard_map/all_to_all | solution.py:262
  86.1 22.0 %all-to-all-start.3 = ((bf16[32,32,256]{2,1,0:T(8,128)(2,1)}), bf16[32,32,256]{2,1,0:T(8,128)(2,1)S(1)}, u32[]{:S(2)}, u32[]{:S(2)}) async-start(bf16[32,32,256]{2,1,0:T(8,128)(2,1)} %get-tuple-element.15), calls=%async_computation.3 | async-start | bytes 1048576 | tf_op jit(solution)/shard_map/all_to_all | solution.py:279
  108.1 44.8 %all-to-all-start.4 = ((bf16[512,8,128]{2,1,0:T(8,128)(2,1)}), bf16[512,8,128]{2,1,0:T(8,128)(2,1)S(1)}, u32[]{:S(2)}, u32[]{:S(2)}) async-start(bf16[512,8,128]{2,1,0:T(8,128)(2,1)} %bitcast.8), calls=%async_computation.4 | async-start | bytes 2097152 | tf_op jit(solution)/shard_map/all_to_all | solution.py:302
  154.1 23.1 %all-to-all-start.5 = ((bf16[32,64,128]{2,1,0:T(8,128)(2,1)}), bf16[32,64,128]{2,1,0:T(8,128)(2,1)S(1)}, u32[]{:S(2)}, u32[]{:S(2)}) async-start(bf16[32,64,128]{2,1,0:T(8,128)(2,1)} %shard_map.118), calls=%async_computation.5 | async-start | bytes 1048576 | tf_op jit(solution)/shard_map/all_to_all | solution.py:326

commit v5 on v4

--- a/solution.py
+++ b/solution.py
@@ -35,33 +35,90 @@
     )
 
 
-def basis_kernel(points_ref, params_ref, out_ref, done_ref):
-    slots, width, _ = out_ref.shape
-    step = 32
-    done_ref[...] = jnp.zeros_like(done_ref)
-
-    def one(s, carry):
-        columns = jnp.transpose(params_ref[s])
-        for at in range(0, width, step):
-            own = columns[at : at + step]
-            distance = None
-            angular = None
+def in_parts(value):
+    high = value.astype(bf16).astype(f32)
+    rest = value - high
+    middle = rest.astype(bf16).astype(f32)
+    return high, middle, rest - middle
+
+
+LEFT = (0, 1, 2, 0, 1, 0)
+RIGHT = (0, 0, 0, 1, 1, 2)
+TERMS = 32
+
+
+def basis_kernel(
+    points_ref, centers_ref, exponents_ref, angular_ref, out_ref, done_ref, left_ref, right_ref
+):
+    slots = out_ref.shape[0]
+    chunks, total, lanes = left_ref.shape
+    total //= TERMS
+    chunks //= 2
+    halves = right_ref.shape[0]
+
+    @pl.when(pl.program_id(0) == 0)
+    def _():
+        done_ref[...] = jnp.zeros_like(done_ref)
+        none = jnp.zeros((total, lanes), f32)
+
+        def put(ref, at, row, value):
+            ref[at, pl.ds(row, total, TERMS), :] = value
+
+        for j in range(chunks):
+            scale = exponents_ref[pl.ds(j, total, chunks), :] * -log2_e
+            center, slope = [], []
             for a in range(3):
-                delta = points_ref[s, a : a + 1, :] - own[:, a : a + 1]
-                square = delta * delta
-                slope = own[:, 4 + a : 5 + a] * delta
-                distance = square if a == 0 else distance + square
-                angular = slope + 1.0 if a == 0 else angular + slope
-            value = jnp.exp2((own[:, 3:4] * -log2_e) * distance) * angular
-            out_ref[s, at : at + step, :] = value.astype(bf16)
-        return carry
-
-    lax.fori_loop(0, slots, one, 0)
-
-
-def pick_kernel(asked_ref, blocks_ref, out_ref):
+                center.append(centers_ref[pl.ds(a * chunks + j, total, 3 * chunks), :])
+                slope.append(angular_ref[pl.ds(a * chunks + j, total, 3 * chunks), :])
+            square = center[0] * center[0] + center[1] * center[1] + center[2] * center[2]
+            offset = slope[0] * center[0] + slope[1] * center[1] + slope[2] * center[2]
+            logarithm = [scale] + [(-2.0 * scale) * c for c in center] + [scale * square]
+            factor = [None] + slope + [1.0 - offset]
+            for at, values in ((j, logarithm), (chunks + j, factor)):
+                for n in range(5):
+                    parts = (none, none, none) if values[n] is None else in_parts(values[n])
+                    for i in range(6 if n < 4 else 3):
+                        put(left_ref, at, 6 * n + i, parts[LEFT[i]])
+                for row in range(27, TERMS):
+                    put(left_ref, at, row, none)
+        for j in range(halves):
+            point = [points_ref[pl.ds(a * halves + j, total, 3 * halves), :] for a in range(3)]
+            square = point[0] * point[0] + point[1] * point[1] + point[2] * point[2]
+            for n, value in enumerate([square] + point):
+                parts = in_parts(value)
+                for i in range(6):
+                    put(right_ref, j, 6 * n + i, parts[RIGHT[i]])
+            for row in range(24, TERMS):
+                put(right_ref, j, row, none + 1.0 if row < 27 else none)
+
+    start = pl.program_id(0) * slots
+    for s in range(slots):
+        rows = pl.ds((start + s) * TERMS, TERMS)
+        right = jnp.concatenate([right_ref[j, rows, :] for j in range(halves)], axis=1).astype(bf16)
+        for j in range(chunks):
+            found = [
+                lax.dot_general(
+                    left_ref[at, rows, :].astype(bf16),
+                    right,
+                    (((0,), (0,)), ((), ())),
+                    preferred_element_type=f32,
+                )
+                for at in (j, chunks + j)
+            ]
+            value = jnp.exp2(found[0]) * found[1]
+            out_ref[s, j * lanes : (j + 1) * lanes, :] = value.astype(bf16)
+
+
+def pick_kernel(asked_ref, blocks_ref, out_ref, sems):
+    per_owner = asked_ref.shape[2]
+    copies = []
     for e in range(out_ref.shape[0]):
-        out_ref[e] = blocks_ref[asked_ref[e]]
+        place = asked_ref[e // per_owner, 0, e % per_owner]
+        copies.append(pltpu.make_async_copy(blocks_ref.at[place], out_ref.at[e], sems.at[e]))
+    for copy in copies:
+        copy.start()
+    for copy in copies:
+        copy.wait()
 
 
 def spread_kernel(hartree_ref, listed_ref, done_ref, out_ref):
@@ -221,33 +278,42 @@
     rank = lax.axis_index("batch")
     plan_rows = lax.dynamic_slice_in_dim(load_plan[0], rank * slots, slots)
 
-    wanted = pair_lists[0, 0]
-    asked = lax.all_to_all(wanted, "blk", split_axis=0, concat_axis=0, tiled=True).reshape(entries)
+    wanted = pair_lists.reshape(columns, 1, per_owner)
+    asked = lax.all_to_all(wanted, "blk", split_axis=0, concat_axis=0, tiled=True)
     sent = call(
         pick_kernel,
         jax.ShapeDtypeStruct((entries, block, block), bf16),
-        [SMEM, VMEM],
+        [SMEM, HBM],
+        [pltpu.SemaphoreType.DMA((entries,))],
+        out_specs=HBM,
+        limit=60,
         moved=entries * block * block * 4,
     )(asked, density_blocks)
     table = lax.all_to_all(
         sent.reshape(columns, per_owner * block, block), "blk", split_axis=0, concat_axis=0, tiled=True
     ).reshape(entries, block, block)
 
-    params = jnp.concatenate(
-        [centers[:, 0], exponents, angular[:, 0], jnp.zeros((slots, 1, width), f32)], axis=1
-    )
     group = min(4, slots)
     steps = (slots // group,)
     basis, done = call(
         basis_kernel,
         (jax.ShapeDtypeStruct((slots, width, grid), bf16), jax.ShapeDtypeStruct((8, block), f32)),
-        [rows_of(group, 3, grid), rows_of(group, 8, width)],
+        [VMEM, VMEM, VMEM, VMEM],
+        [
+            pltpu.VMEM((2 * LIST, slots * TERMS, block), f32),
+            pltpu.VMEM((grid // block, slots * TERMS, block), f32),
+        ],
         grid=steps,
         out_specs=(rows_of(group, width, grid), VMEM),
         limit=48,
         flops=slots * width * grid * 400,
         moved=slots * width * grid * 2,
-    )(points[:, 0], params)
+    )(
+        points.reshape(-1, block),
+        centers.reshape(-1, block),
+        exponents.reshape(-1, block),
+        angular.reshape(-1, block),
+    )
 
     stride = slots + 8
     lines = call(

time: 179 us -> 206 us (1.15)
  Pallas kernels: 47.8 us -> 67.4 us
  waiting for transfers between devices: 66.4 us -> 76.4 us
    pallas_call x1, Pallas kernels: 1.58 us -> 34.1 us  [on_device(): call(pick_kernel, jax.ShapeDtypeStruct((entries, block, block), bf16), [S...]
    pallas_call x1, Pallas kernels: 22.8 us -> 9.83 us  [on_device(): call(basis_kernel, (jax.ShapeDtypeStruct((slots, width, grid), bf16), jax...]
    all_to_all x1, waiting for transfers between devices: 0.01 us -> 9.61 us  [on_device(): lax.all_to_all(sent.reshape(columns, per_owner * block, block), 'blk', sp...]
    unnamed x15 -> x20, local copies, waits for them, and re-layouts: 5.3 us -> 5.03 us
  transfers between devices with their start and end apart: 5 -> 5, of which waited for: 4 -> 5; matrix products, arithmetic and copies ran while one was open for 4% -> 1% of each run, Pallas kernels for 25% -> 15%
where the time goes in v5:
time: 206 us; the launch traced here: 205 us
  waiting for transfers between devices  76.4 us (37%)
  Pallas kernels  67.4 us (33%)
  starting transfers between devices  38.4 us (19%)
  blocking collectives  15.1 us (7%)
  local copies, waits for them, and re-layouts  6.47 us (3%)
    pallas_call x1, Pallas kernels, on_device(): call(pick_kernel, jax.ShapeDtypeStruct((entries, block, block), bf16), [S...  34.1 us
    all_to_all x1, waiting for transfers between devices, on_device(): lax.all_to_all(partial.reshape(ranks * columns, rows, block), ('batch', '...  32.1 us
    all_to_all x1, waiting for transfers between devices, on_device(): lax.all_to_all(totals, 'batch', split_axis=0, concat_axis=0, tiled=True)  17.3 us
    all_to_all x1, blocking collectives, on_device(): lax.all_to_all(wanted, 'blk', split_axis=0, concat_axis=0, tiled=True)  15.1 us
    all_to_all x1, starting transfers between devices, on_device(): lax.all_to_all(partial.reshape(ranks * columns, rows, block), ('batch', '...  11.9 us
    all_to_all x1, starting transfers between devices, on_device(): lax.all_to_all(lines, 'batch', split_axis=0, concat_axis=0, tiled=True)  11.7 us
    all_to_all x1, waiting for transfers between devices, on_device(): lax.all_to_all(lines, 'batch', split_axis=0, concat_axis=0, tiled=True)  10.8 us
    pallas_call x1, Pallas kernels, on_device(): call(matrix_kernel, (jax.ShapeDtypeStruct((ranks // 2, 2, columns, per_ow...  10.4 us
  transfers between devices with their start and end apart: 5, of which 5 were waited for; matrix products, arithmetic and copies ran while one was open for 1% of the time, Pallas kernels for 15%

profile of v5, /device:TPU:8, one launch (start us, length us, event | category | flops | bytes accessed | tf_op | source)
XLA Modules:
  0.0 204.8 jit_solution(13070364734579839402)
XLA Ops:
  0.6 0.8 copy.15
  1.4 15.1 %all_to_all.30.asked_ref = s32[16,1,2]{2,1,0:T(1,128)} all-to-all(s32[16,1,2]{2,1,0:T(1,128)S(1)} %copy.15), channel_id=1, replica_groups=mesh['batch'=32,'blk'=16] {'blk'}, dimensions={0} | all-to-all | bytes 256 | tf_op jit(solution)/shard_map/all_to_all | solution.py:282
  16.5 34.1 %shard_map.114 = bf16[32,128,128]{2,1,0:T(8,128)(2,1)} custom-call(s32[16,1,2]{2,1,0:T(1,128)} %all_to_all.30.asked_ref, bf16[16,128,128]{2,1,0:T(8,128)(2,1)} %blocks_ref.1), custom_call_target="tpu_custom_call" | custom-call | bytes 2097152 | tf_op jit(solution)/shard_map/pallas_call | solution.py:283
  50.6 4.9 %all-to-all-start.1 = ((bf16[16,256,128]{2,1,0:T(8,128)(2,1)}), bf16[16,256,128]{2,1,0:T(8,128)(2,1)S(1)}, u32[]{:S(2)}, u32[]{:S(2)}) async-start(bf16[16,256,128]{2,1,0:T(8,128)(2,1)} %bitcast.34), calls=%async_computation.1 | async-start | bytes 2097152 | tf_op jit(solution)/shard_map/all_to_all | solution.py:292
  55.5 0.8 copy.22
  56.3 0.9 copy-done.1
  57.2 0.9 copy-done.2
  58.1 0.9 copy-done.3
  59.0 0.8 copy-done.4
  59.8 9.8 %shard_map.113 = (bf16[32,384,256]{2,1,0:T(8,128)(2,1)}, f32[8,128]{1,0:T(8,128)S(1)}) custom-call(f32[192,128]{1,0:T(8,128)S(1)} %bitcast.32, f32[288,128]{1,0:T(8,128)S(1)} %bitcast.30, f32[96,128]{1,0:T(8,128)S(1)} %bitcast.33, f32[288,128]{1,0:T(8,128)S(1)} %bitcast.31), custom_call_target="tpu_custom_call" | custom-call | flops 1258291200 | bytes 6291456 | tf_op jit(solution)/shard_map/pallas_call | solution.py:298
  69.7 0.1 convert_element_type.20
  69.8 0.9 shard_map.116
  70.7 9.6 %all-to-all-done.1 = bf16[16,256,128]{2,1,0:T(8,128)(2,1)S(1)} async-done(((bf16[16,256,128]{2,1,0:T(8,128)(2,1)}), bf16[16,256,128]{2,1,0:T(8,128)(2,1)S(1)}, u32[]{:S(2)}, u32[]{:S(2)}) %all-to-all-start.1) | async-done | bytes 1048608 | tf_op jit(solution)/shard_map/all_to_all | solution.py:292
  80.3 11.7 %all-to-all-start.2 = ((bf16[32,40,256]{2,1,0:T(8,128)(2,1)}), bf16[32,40,256]{2,1,0:T(8,128)(2,1)S(1)}, u32[]{:S(2)}, u32[]{:S(2)}) async-start(bf16[32,40,256]{2,1,0:T(8,128)(2,1)} %shard_map.116), calls=%async_computation.2 | async-start | bytes 1310720 | tf_op jit(solution)/shard_map/all_to_all | solution.py:328
  92.0 0.1 copy.14
  92.1 0.1 reshape.91.pairs_ref
  92.2 9.7 %shard_map.115 = (f32[32,256]{1,0:T(8,128)S(1)}, bf16[32,32,256]{2,1,0:T(8,128)(2,1)}) custom-call(s32[288]{0:T(512)S(1)} %reshape.91.pairs_ref, bf16[32,384,256]{2,1,0:T(8,128)(2,1)} %get-tuple-element.10.basis_ref, bf16[32,128,128]{2,1,0:T(8,128)(2,1)S(1)} %bitcast.26), custom_call_target="tpu_custom_call" | custom-call | flops 2415919104 | bytes 6291456 | tf_op jit(solution)/shard_map/pallas_call | solution.py:332
  102.0 10.8 %all-to-all-done.2.hartree_ref = bf16[32,40,256]{2,1,0:T(8,128)(2,1)S(1)} async-done(((bf16[32,40,256]{2,1,0:T(8,128)(2,1)}), bf16[32,40,256]{2,1,0:T(8,128)(2,1)S(1)}, u32[]{:S(2)}, u32[]{:S(2)}) %all-to-all-start.2) | async-done | bytes 655392 | tf_op jit(solution)/shard_map/all_to_all | solution.py:328
  112.8 4.9 %all-to-all-start.3 = ((bf16[32,32,256]{2,1,0:T(8,128)(2,1)}), bf16[32,32,256]{2,1,0:T(8,128)(2,1)S(1)}, u32[]{:S(2)}, u32[]{:S(2)}) async-start(bf16[32,32,256]{2,1,0:T(8,128)(2,1)} %get-tuple-element.15), calls=%async_computation.3 | async-start | bytes 1048576 | tf_op jit(solution)/shard_map/all_to_all | solution.py:345
  117.7 0.1 dynamic-slice_bitcast_fusion.plan_ref
  117.8 10.4 %shard_map.117 = (bf16[16,2,16,8,128]{4,3,2,1,0:T(8,128)(2,1)}, f32[32,128]{1,0:T(8,128)S(1)}) custom-call(s32[288]{0:T(512)S(1)} %reshape.91.pairs_ref, s32[32]{0:T(128)S(1)} %dynamic-slice_bitcast_fusion.plan_ref, bf16[32,384,256]{2,1,0:T(8,128)(2,1)} %get-tuple-element.10.basis_ref, f32[32,256]{1,0:T(8,128)S(1)} %get-tuple-element.11.rho_ref, ...), custom_call_target="tpu_custom_call" | custom-call | flops 2415919104 | bytes 6291456 | tf_op jit(solution)/shard_map/pallas_call | solution.py:348
  128.2 6.5 %all-to-all-done.3 = bf16[32,32,256]{2,1,0:T(8,128)(2,1)S(1)} async-done(((bf16[32,32,256]{2,1,0:T(8,128)(2,1)}), bf16[32,32,256]{2,1,0:T(8,128)(2,1)S(1)}, u32[]{:S(2)}, u32[]{:S(2)}) %all-to-all-start.3) | async-done | bytes 524320 | tf_op jit(solution)/shard_map/all_to_all | solution.py:345
  134.8 11.9 %all-to-all-start.4 = ((bf16[512,8,128]{2,1,0:T(8,128)(2,1)}), bf16[512,8,128]{2,1,0:T(8,128)(2,1)S(1)}, u32[]{:S(2)}, u32[]{:S(2)}) async-start(bf16[512,8,128]{2,1,0:T(8,128)(2,1)} %bitcast.9), calls=%async_computation.4 | async-start | bytes 2097152 | tf_op jit(solution)/shard_map/all_to_all | solution.py:368
  146.8 0.2 iota_add_fusion
  147.0 0.3 add.32.target_ref
  147.3 32.1 %all-to-all-done.4 = bf16[512,8,128]{2,1,0:T(8,128)(2,1)S(1)} async-done(((bf16[512,8,128]{2,1,0:T(8,128)(2,1)}), bf16[512,8,128]{2,1,0:T(8,128)(2,1)S(1)}, u32[]{:S(2)}, u32[]{:S(2)}) %all-to-all-start.4) | async-done | bytes 1048608 | tf_op jit(solution)/shard_map/all_to_all | solution.py:368
  179.4 1.2 shard_map.118
  180.6 5.0 %all-to-all-start.5 = ((bf16[32,64,128]{2,1,0:T(8,128)(2,1)}), bf16[32,64,128]{2,1,0:T(8,128)(2,1)S(1)}, u32[]{:S(2)}, u32[]{:S(2)}) async-start(bf16[32,64,128]{2,1,0:T(8,128)(2,1)} %shard_map.118), calls=%async_computation.5 | async-start | bytes 1048576 | tf_op jit(solution)/shard_map/all_to_all | solution.py:392
  185.5 0.2 shard_map.120
  185.7 0.7 copy.16
  186.4 17.3 %all-to-all-done.5 = bf16[32,64,128]{2,1,0:T(8,128)(2,1)S(1)} async-done(((bf16[32,64,128]{2,1,0:T(8,128)(2,1)}), bf16[32,64,128]{2,1,0:T(8,128)(2,1)S(1)}, u32[]{:S(2)}, u32[]{:S(2)}) %all-to-all-start.5) | async-done | bytes 524320 | tf_op jit(solution)/shard_map/all_to_all | solution.py:392
  203.7 1.1 shard_map.119
  (17 shorter events, 0.1 us)
Async XLA Ops:
  0.6 91.4 %copy-start.7 = (s32[32,1,9]{0,1,2:T(1,128)S(1)}, s32[32,1,9]{0,1,2:T(1,128)}, u32[]{:S(2)}) copy-start(s32[32,1,9]{0,1,2:T(1,128)} %param.19) | copy-start | bytes 3460
  16.5 53.1 %copy-start.5 = (s32[16,1,2]{2,1,0:T(1,128)S(1)}, s32[16,1,2]{2,1,0:T(1,128)}, u32[]{:S(2)}) copy-start(s32[16,1,2]{2,1,0:T(1,128)} %all_to_all.30.asked_ref) | copy-start | bytes 388
  50.6 29.7 %all-to-all-start.1 = ((bf16[16,256,128]{2,1,0:T(8,128)(2,1)}), bf16[16,256,128]{2,1,0:T(8,128)(2,1)S(1)}, u32[]{:S(2)}, u32[]{:S(2)}) async-start(bf16[16,256,128]{2,1,0:T(8,128)(2,1)} %bitcast.34), calls=%async_computation.1 | async-start | bytes 2097152 | tf_op jit(solution)/shard_map/all_to_all | solution.py:292
  56.3 0.9 copy-start.1
  57.2 0.9 copy-start.2
  58.1 0.9 copy-start.3
  59.0 0.8 copy-start.4
  69.6 48.1 %copy-start.6 = (f32[32,1,256]{2,1,0:T(1,128)S(1)}, f32[32,1,256]{2,1,0:T(1,128)}, u32[]{:S(2)}) copy-start(f32[32,1,256]{2,1,0:T(1,128)} %param.14) | copy-start | bytes 98308
  69.6 48.1 %copy-start = (s32[1,1024]{1,0:T(1,128)S(1)}, s32[1,1024]{1,0:T(1,128)}, u32[]{:S(2)}) copy-start(s32[1,1024]{1,0:T(1,128)} %plan_ref.1) | copy-start | bytes 12292
  80.3 32.5 %all-to-all-start.2 = ((bf16[32,40,256]{2,1,0:T(8,128)(2,1)}), bf16[32,40,256]{2,1,0:T(8,128)(2,1)S(1)}, u32[]{:S(2)}, u32[]{:S(2)}) async-start(bf16[32,40,256]{2,1,0:T(8,128)(2,1)} %shard_map.116), calls=%async_computation.2 | async-start | bytes 1310720 | tf_op jit(solution)/shard_map/all_to_all | solution.py:328
  112.8 21.9 %all-to-all-start.3 = ((bf16[32,32,256]{2,1,0:T(8,128)(2,1)}), bf16[32,32,256]{2,1,0:T(8,128)(2,1)S(1)}, u32[]{:S(2)}, u32[]{:S(2)}) async-start(bf16[32,32,256]{2,1,0:T(8,128)(2,1)} %get-tuple-element.15), calls=%async_computation.3 | async-start | bytes 1048576 | tf_op jit(solution)/shard_map/all_to_all | solution.py:345
  134.8 44.7 %all-to-all-start.4 = ((bf16[512,8,128]{2,1,0:T(8,128)(2,1)}), bf16[512,8,128]{2,1,0:T(8,128)(2,1)S(1)}, u32[]{:S(2)}, u32[]{:S(2)}) async-start(bf16[512,8,128]{2,1,0:T(8,128)(2,1)} %bitcast.9), calls=%async_computation.4 | async-start | bytes 2097152 | tf_op jit(solution)/shard_map/all_to_all | solution.py:368
  180.6 23.1 %all-to-all-start.5 = ((bf16[32,64,128]{2,1,0:T(8,128)(2,1)}), bf16[32,64,128]{2,1,0:T(8,128)(2,1)S(1)}, u32[]{:S(2)}, u32[]{:S(2)}) async-start(bf16[32,64,128]{2,1,0:T(8,128)(2,1)} %shard_map.118), calls=%async_computation.5 | async-start | bytes 1048576 | tf_op jit(solution)/shard_map/all_to_all | solution.py:392

commit v6 on v5

--- a/solution.py
+++ b/solution.py
@@ -6,6 +6,7 @@
 from jax.sharding import PartitionSpec as P
 
 LIST = 3
+BATCH = ("z", "x")
 xc_scale = 0.98474502
 soft_square = 0.01
 zero_exchange = xc_scale * soft_square ** (1.0 / 6.0)
@@ -109,16 +110,10 @@
             out_ref[s, j * lanes : (j + 1) * lanes, :] = value.astype(bf16)
 
 
-def pick_kernel(asked_ref, blocks_ref, out_ref, sems):
+def pick_kernel(asked_ref, blocks_ref, out_ref):
     per_owner = asked_ref.shape[2]
-    copies = []
     for e in range(out_ref.shape[0]):
-        place = asked_ref[e // per_owner, 0, e % per_owner]
-        copies.append(pltpu.make_async_copy(blocks_ref.at[place], out_ref.at[e], sems.at[e]))
-    for copy in copies:
-        copy.start()
-    for copy in copies:
-        copy.wait()
+        out_ref[e] = blocks_ref[asked_ref[e // per_owner, 0, e % per_owner]]
 
 
 def spread_kernel(hartree_ref, listed_ref, done_ref, out_ref):
@@ -220,7 +215,8 @@
             out_ref[:, 1, c] = jnp.where(low, pltpu.roll(first, 4, 1), second).astype(bf16)
 
 
-def add_kernel(target_ref, received_ref, out_ref):
+def add_kernel(target_ref, received_ref, density_ref, out_ref):
+    del density_ref
     rows = out_ref.shape[1]
     length = target_ref.shape[1]
     chosen = lax.broadcasted_iota(jnp.int32, (rows, length), 0) == target_ref[...]
@@ -231,12 +227,17 @@
         out_ref[h] = total
 
 
-def place_kernel(spread_ref, plan_ref, rank_ref, density_ref):
+def place_kernel(plan_ref, place_ref, *refs):
+    density_ref = refs[-1]
     slots = density_ref.shape[0]
-    length = plan_ref.shape[1]
-    own = lax.broadcasted_iota(jnp.int32, (slots, length), 0) + rank_ref[0] * slots
-    chosen = (own == plan_ref[...]).astype(f32).astype(bf16)
-    density_ref[...] = jnp.dot(chosen, spread_ref[...], preferred_element_type=f32)
+    planes, length = plan_ref.shape
+    own = lax.broadcasted_iota(jnp.int32, (slots, length), 0) + place_ref[1] * slots
+    total = jnp.zeros(density_ref.shape, f32)
+    for k in range(planes):
+        plane = lax.rem(place_ref[0] + (planes - k), planes)
+        chosen = (own == plan_ref[pl.ds(plane, 1), :]).astype(f32).astype(bf16)
+        total += jnp.dot(chosen, refs[k][...], preferred_element_type=f32)
+    density_ref[...] = total
 
 
 def merge_kernel(received_ref, out_ref):
@@ -268,14 +269,14 @@
     batch_pairs,
 ):
     slots, _, _, grid = points.shape
-    ranks = lax.axis_size("batch")
+    ranks = lax.axis_size(BATCH)
     columns = lax.axis_size("blk")
     per_owner = pair_lists.shape[3]
     held, block, _ = density_blocks.shape
     entries = columns * per_owner
     width = LIST * block
     piece = block // ranks
-    rank = lax.axis_index("batch")
+    rank = lax.axis_index(BATCH)
     plan_rows = lax.dynamic_slice_in_dim(load_plan[0], rank * slots, slots)
 
     wanted = pair_lists.reshape(columns, 1, per_owner)
@@ -283,10 +284,7 @@
     sent = call(
         pick_kernel,
         jax.ShapeDtypeStruct((entries, block, block), bf16),
-        [SMEM, HBM],
-        [pltpu.SemaphoreType.DMA((entries,))],
-        out_specs=HBM,
-        limit=60,
+        [SMEM, VMEM],
         moved=entries * block * block * 4,
     )(asked, density_blocks)
     table = lax.all_to_all(
@@ -325,7 +323,7 @@
         jnp.pad(asked.reshape(1, entries).astype(f32), ((0, 0), (0, grid - entries))),
         done,
     )
-    stored = lax.all_to_all(lines, "batch", split_axis=0, concat_axis=0, tiled=True)
+    stored = lax.all_to_all(lines, BATCH, split_axis=0, concat_axis=0, tiled=True)
 
     pairs = batch_pairs.reshape(slots * LIST * LIST)
     unroll = 2
@@ -333,7 +331,7 @@
         density_kernel,
         (
             jax.ShapeDtypeStruct((slots, grid), f32),
-            jax.ShapeDtypeStruct((ranks, slots, grid), bf16),
+            jax.ShapeDtypeStruct((lax.axis_size("x"), slots, grid), bf16),
         ),
         [SMEM, rows_of(group, width, grid), VMEM],
         [pltpu.VMEM((unroll, width, width), bf16)],
@@ -342,9 +340,7 @@
         flops=slots * width * width * grid * 2,
         moved=slots * width * grid * 2,
     )(pairs, basis, table)
-    spread = lax.all_to_all(copies, "batch", split_axis=0, concat_axis=0, tiled=True).reshape(
-        ranks * slots, grid
-    )
+    near = lax.all_to_all(copies, "x", split_axis=0, concat_axis=0, tiled=True).reshape(-1, grid)
     partial, lists = call(
         matrix_kernel,
         (
@@ -364,20 +360,25 @@
     )(pairs, plan_rows, basis, rho, stored, grid_weights[:, 0])
 
     rows = per_owner * piece
-    partial, spread = lax.optimization_barrier((partial, spread))
+    partial, near = lax.optimization_barrier((partial, near))
     received = lax.all_to_all(
         partial.reshape(ranks * columns, rows, block),
-        ("batch", "blk"),
+        BATCH + ("blk",),
         split_axis=0,
         concat_axis=0,
         tiled=True,
     ).reshape(ranks * columns * rows, block)
+    planes = lax.axis_size("z")
+    spread = [near] + [
+        lax.ppermute(near, "z", [(n, (n + k) % planes) for n in range(planes)])
+        for k in range(1, planes)
+    ]
     density = call(
         place_kernel,
         jax.ShapeDtypeStruct((slots, grid), f32),
-        [VMEM, VMEM, SMEM],
+        [VMEM, SMEM] + [VMEM] * planes,
         moved=ranks * slots * grid * 2,
-    )(spread, load_plan, rank.reshape(1))
+    )(load_plan.reshape(planes, -1), jnp.stack([lax.axis_index("z"), rank]), *spread)
 
     targets = lists[:, :entries].astype(jnp.int32).reshape(ranks * entries, 1) * piece
     targets = (targets + jnp.arange(piece, dtype=jnp.int32)[None]).reshape(
@@ -386,10 +387,10 @@
     totals = call(
         add_kernel,
         jax.ShapeDtypeStruct((ranks, held * piece, block), bf16),
-        [VMEM, VMEM],
+        [VMEM, VMEM, HBM],
         moved=ranks * columns * rows * block * 2,
-    )(targets, received)
-    gathered = lax.all_to_all(totals, "batch", split_axis=0, concat_axis=0, tiled=True)
+    )(targets, received, density)
+    gathered = lax.all_to_all(totals, BATCH, split_axis=0, concat_axis=0, tiled=True)
     hamiltonian = call(
         merge_kernel,
         jax.ShapeDtypeStruct((held, block, block), f32),
@@ -400,21 +401,23 @@
 
 
 def solution(mesh):
+    ranks, columns = mesh.devices.shape
+    fine = jax.sharding.Mesh(mesh.devices.reshape(ranks // 4, 4, columns), BATCH + ("blk",))
     return jax.shard_map(
         on_device,
-        mesh=mesh,
+        mesh=fine,
         in_specs=(
-            P("batch", "blk", None, None),
-            P("batch", "blk", None, None),
-            P("batch", "blk", None),
-            P("batch", "blk", None, None),
-            P("batch", "blk", None),
-            P("batch", "blk", None),
+            P(BATCH, "blk", None, None),
+            P(BATCH, "blk", None, None),
+            P(BATCH, "blk", None),
+            P(BATCH, "blk", None, None),
+            P(BATCH, "blk", None),
+            P(BATCH, "blk", None),
             P("blk", None),
             P("blk", None, None),
-            P("batch", "blk", None, None),
-            P("batch", "blk", None),
+            P(BATCH, "blk", None, None),
+            P(BATCH, "blk", None),
         ),
-        out_specs=(P("blk", None, None), P("batch", "blk", None)),
+        out_specs=(P("blk", None, None), P(BATCH, "blk", None)),
         check_vma=False,
     )

time: 206 us -> 175 us (0.85)
  starting transfers between devices: 38.4 us -> 71.7 us
  waiting for transfers between devices: 76.4 us -> 43.7 us
  Pallas kernels: 67.4 us -> 35.3 us
    all_to_all x4, waiting for transfers between devices: 66.7 us -> 27.7 us  [the longest x1 16.7 us: on_device(): lax.all_to_all(totals, BATCH, split_axis=0, concat_axis=0, tiled=True)]
    pallas_call x1, Pallas kernels: 34.1 us -> 1.71 us  [on_device(): call(pick_kernel, jax.ShapeDtypeStruct((entries, block, block), bf16), [S...]
    ppermute x0 -> x7, starting transfers between devices: none -> 31.2 us  [on_device(): lax.ppermute(near, 'z', [(n, (n + k) % planes) for n in range(planes)])]
    ppermute x0 -> x7, waiting for transfers between devices: none -> 6.41 us  [on_device(): lax.ppermute(near, 'z', [(n, (n + k) % planes) for n in range(planes)])]
    all_to_all x4, starting transfers between devices: 33.5 us -> 35.6 us  [the longest x1 13.1 us: on_device(): lax.all_to_all(partial.reshape(ranks * columns, rows, block), BATCH + ('b...]
  transfers between devices with their start and end apart: 5 -> 12, of which waited for: 5 -> 7; matrix products, arithmetic and copies ran while one was open for 1% -> 1% of each run, Pallas kernels for 15% -> 18%
where the time goes in v6:
time: 175 us; the launch traced here: 174 us
  starting transfers between devices  71.7 us (41%)
  waiting for transfers between devices  43.7 us (25%)
  Pallas kernels  35.3 us (20%)
  blocking collectives  14.5 us (8%)
  local copies, waits for them, and re-layouts  7.51 us (4%)
    ppermute x7, starting transfers between devices, on_device(): lax.ppermute(near, 'z', [(n, (n + k) % planes) for n in range(planes)])  31.2 us
    all_to_all x1, waiting for transfers between devices, on_device(): lax.all_to_all(totals, BATCH, split_axis=0, concat_axis=0, tiled=True)  16.7 us
    all_to_all x1, blocking collectives, on_device(): lax.all_to_all(wanted, 'blk', split_axis=0, concat_axis=0, tiled=True)  14.5 us
    all_to_all x1, starting transfers between devices, on_device(): lax.all_to_all(partial.reshape(ranks * columns, rows, block), BATCH + ('b...  13.1 us
    all_to_all x1, starting transfers between devices, on_device(): lax.all_to_all(lines, BATCH, split_axis=0, concat_axis=0, tiled=True)  12.3 us
    all_to_all x1, waiting for transfers between devices, on_device(): lax.all_to_all(lines, BATCH, split_axis=0, concat_axis=0, tiled=True)  11 us
    pallas_call x1, Pallas kernels, on_device(): call(matrix_kernel, (jax.ShapeDtypeStruct((ranks // 2, 2, columns, per_ow...  10.4 us
    pallas_call x1, Pallas kernels, on_device(): call(basis_kernel, (jax.ShapeDtypeStruct((slots, width, grid), bf16), jax...  9.87 us
  transfers between devices with their start and end apart: 12, of which 7 were waited for; matrix products, arithmetic and copies ran while one was open for 1% of the time, Pallas kernels for 18%

profile of v6, /device:TPU:8, one launch (start us, length us, event | category | flops | bytes accessed | tf_op | source)
XLA Modules:
  0.0 173.9 jit_solution(7788238854321829309)
XLA Ops:
  1.4 14.5 %all_to_all.30.asked_ref = s32[16,1,2]{2,1,0:T(1,128)S(1)} all-to-all(s32[16,1,2]{2,1,0:T(1,128)S(1)} %copy.15), channel_id=1, replica_groups=mesh['z'=8,'x'=4,'blk'=16] {'blk'}, dimensions={0} | all-to-all | bytes 256 | tf_op jit(solution)/shard_map/all_to_all | solution.py:283
  15.9 1.0 copy-done
  16.9 1.7 shard_map.114
  18.6 4.9 %all-to-all-start.1 = ((bf16[16,256,128]{2,1,0:T(8,128)(2,1)}), bf16[16,256,128]{2,1,0:T(8,128)(2,1)S(1)}, u32[]{:S(2)}, u32[]{:S(2)}) async-start(bf16[16,256,128]{2,1,0:T(8,128)(2,1)} %bitcast.6), calls=%async_computation.1 | async-start | bytes 2097152 | tf_op jit(solution)/shard_map/all_to_all | solution.py:290
  24.3 0.9 copy-done.2
  25.2 0.9 copy-done.3
  26.1 0.9 copy-done.4
  27.0 0.8 copy-done.5
  27.8 9.9 %shard_map.113 = (bf16[32,384,256]{2,1,0:T(8,128)(2,1)}, f32[8,128]{1,0:T(8,128)S(1)}) custom-call(f32[192,128]{1,0:T(8,128)S(1)} %bitcast.42, f32[288,128]{1,0:T(8,128)S(1)} %bitcast.40, f32[96,128]{1,0:T(8,128)S(1)} %bitcast.43, f32[288,128]{1,0:T(8,128)S(1)} %bitcast.41), custom_call_target="tpu_custom_call" | custom-call | flops 1258291200 | bytes 6291456 | tf_op jit(solution)/shard_map/pallas_call | solution.py:296
  37.8 0.9 shard_map.116
  38.7 9.6 %all-to-all-done.1 = bf16[16,256,128]{2,1,0:T(8,128)(2,1)S(1)} async-done(((bf16[16,256,128]{2,1,0:T(8,128)(2,1)}), bf16[16,256,128]{2,1,0:T(8,128)(2,1)S(1)}, u32[]{:S(2)}, u32[]{:S(2)}) %all-to-all-start.1) | async-done | bytes 1048608 | tf_op jit(solution)/shard_map/all_to_all | solution.py:290
  48.3 12.3 %all-to-all-start.2 = ((bf16[32,40,256]{2,1,0:T(8,128)(2,1)}), bf16[32,40,256]{2,1,0:T(8,128)(2,1)S(1)}, u32[]{:S(2)}, u32[]{:S(2)}) async-start(bf16[32,40,256]{2,1,0:T(8,128)(2,1)} %shard_map.116), calls=%async_computation.2 | async-start | bytes 1310720 | tf_op jit(solution)/shard_map/all_to_all | solution.py:326
  60.9 9.4 %shard_map.115 = (f32[32,256]{1,0:T(8,128)S(1)}, bf16[4,32,256]{2,1,0:T(8,128)(2,1)}) custom-call(s32[288]{0:T(512)S(1)} %reshape.91.pairs_ref, bf16[32,384,256]{2,1,0:T(8,128)(2,1)} %get-tuple-element.10.basis_ref, bf16[32,128,128]{2,1,0:T(8,128)(2,1)S(1)} %bitcast.27), custom_call_target="tpu_custom_call" | custom-call | flops 2415919104 | bytes 6291456 | tf_op jit(solution)/shard_map/pallas_call | solution.py:330
  70.3 11.0 %all-to-all-done.2.hartree_ref = bf16[32,40,256]{2,1,0:T(8,128)(2,1)S(1)} async-done(((bf16[32,40,256]{2,1,0:T(8,128)(2,1)}), bf16[32,40,256]{2,1,0:T(8,128)(2,1)S(1)}, u32[]{:S(2)}, u32[]{:S(2)}) %all-to-all-start.2) | async-done | bytes 655392 | tf_op jit(solution)/shard_map/all_to_all | solution.py:326
  81.4 3.9 %all-to-all-start.3 = ((bf16[4,32,256]{2,1,0:T(8,128)(2,1)}), bf16[4,32,256]{2,1,0:T(8,128)(2,1)S(1)}, u32[]{:S(2)}, u32[]{:S(2)}) async-start(bf16[4,32,256]{2,1,0:T(8,128)(2,1)} %get-tuple-element.15), calls=%async_computation.3 | async-start | bytes 131072 | tf_op jit(solution)/shard_map/all_to_all | solution.py:343
  85.2 10.4 %shard_map.117 = (bf16[16,2,16,8,128]{4,3,2,1,0:T(8,128)(2,1)}, f32[32,128]{1,0:T(8,128)S(1)}) custom-call(s32[288]{0:T(512)S(1)} %reshape.91.pairs_ref, s32[32]{0:T(128)S(1)} %dynamic-slice_bitcast_fusion.plan_ref, bf16[32,384,256]{2,1,0:T(8,128)(2,1)} %get-tuple-element.10.basis_ref, f32[32,256]{1,0:T(8,128)S(1)} %get-tuple-element.11.rho_ref, ...), custom_call_target="tpu_custom_call" | custom-call | flops 2415919104 | bytes 6291456 | tf_op jit(solution)/shard_map/pallas_call | solution.py:344
  95.6 13.1 %all-to-all-start.4 = ((bf16[512,8,128]{2,1,0:T(8,128)(2,1)}), bf16[512,8,128]{2,1,0:T(8,128)(2,1)S(1)}, u32[]{:S(2)}, u32[]{:S(2)}) async-start(bf16[512,8,128]{2,1,0:T(8,128)(2,1)} %bitcast.9), calls=%async_computation.4 | async-start | bytes 2097152 | tf_op jit(solution)/shard_map/all_to_all | solution.py:364
  108.8 8.3 %collective-permute-start.6 = (bf16[128,256]{1,0:T(8,128)(2,1)S(1)}, bf16[128,256]{1,0:T(8,128)(2,1)S(1)}, u32[]{:S(2)}, u32[]{:S(2)}) collective-permute-start(bf16[128,256]{1,0:T(8,128)(2,1)S(1)} %bitcast.29), channel_id=1, source_target_pairs={{0,448},{64,0},{128,64},{192,128},{256,192},{320,256},{384,320},{4... | collective-permute-start | bytes 196616 | tf_op jit(solution)/shard_map/ppermute | solution.py:373
  117.1 3.2 %collective-permute-start.5 = (bf16[128,256]{1,0:T(8,128)(2,1)S(1)}, bf16[128,256]{1,0:T(8,128)(2,1)S(1)}, u32[]{:S(2)}, u32[]{:S(2)}) collective-permute-start(bf16[128,256]{1,0:T(8,128)(2,1)S(1)} %bitcast.30), channel_id=1, source_target_pairs={{0,384},{64,448},{128,0},{192,64},{256,128},{320,192},{384,256},{4... | collective-permute-start | bytes 196616 | tf_op jit(solution)/shard_map/ppermute | solution.py:373
  120.3 2.3 %collective-permute-start.4 = (bf16[128,256]{1,0:T(8,128)(2,1)S(1)}, bf16[128,256]{1,0:T(8,128)(2,1)S(1)}, u32[]{:S(2)}, u32[]{:S(2)}) collective-permute-start(bf16[128,256]{1,0:T(8,128)(2,1)S(1)} %bitcast.31), channel_id=1, source_target_pairs={{0,320},{64,384},{128,448},{192,0},{256,64},{320,128},{384,192},{4... | collective-permute-start | bytes 196616 | tf_op jit(solution)/shard_map/ppermute | solution.py:373
  122.6 7.1 %collective-permute-start.3 = (bf16[128,256]{1,0:T(8,128)(2,1)S(1)}, bf16[128,256]{1,0:T(8,128)(2,1)S(1)}, u32[]{:S(2)}, u32[]{:S(2)}) collective-permute-start(bf16[128,256]{1,0:T(8,128)(2,1)S(1)} %bitcast.32), channel_id=1, source_target_pairs={{0,256},{64,320},{128,384},{192,448},{256,0},{320,64},{384,128},{4... | collective-permute-start | bytes 196616 | tf_op jit(solution)/shard_map/ppermute | solution.py:373
  129.7 1.9 %collective-permute-start.2 = (bf16[128,256]{1,0:T(8,128)(2,1)S(1)}, bf16[128,256]{1,0:T(8,128)(2,1)S(1)}, u32[]{:S(2)}, u32[]{:S(2)}) collective-permute-start(bf16[128,256]{1,0:T(8,128)(2,1)S(1)} %bitcast.33), channel_id=1, source_target_pairs={{0,192},{64,256},{128,320},{192,384},{256,448},{320,0},{384,64},{4... | collective-permute-start | bytes 196616 | tf_op jit(solution)/shard_map/ppermute | solution.py:373
  131.7 4.1 %collective-permute-start.1 = (bf16[128,256]{1,0:T(8,128)(2,1)S(1)}, bf16[128,256]{1,0:T(8,128)(2,1)S(1)}, u32[]{:S(2)}, u32[]{:S(2)}) collective-permute-start(bf16[128,256]{1,0:T(8,128)(2,1)S(1)} %bitcast.34), channel_id=1, source_target_pairs={{0,128},{64,192},{128,256},{192,320},{256,384},{320,448},{384,0},{... | collective-permute-start | bytes 196616 | tf_op jit(solution)/shard_map/ppermute | solution.py:373
  135.8 1.1 collective-permute-done.5.refs_6_
  136.9 4.4 %collective-permute-start = (bf16[128,256]{1,0:T(8,128)(2,1)S(1)}, bf16[128,256]{1,0:T(8,128)(2,1)S(1)}, u32[]{:S(2)}, u32[]{:S(2)}) collective-permute-start(bf16[128,256]{1,0:T(8,128)(2,1)S(1)} %bitcast.35), channel_id=1, source_target_pairs={{0,64},{64,128},{128,192},{192,256},{256,320},{320,384},{384,448},... | collective-permute-start | bytes 196616 | tf_op jit(solution)/shard_map/ppermute | solution.py:373
  141.9 0.9 collective-permute-done.2.refs_3_
  142.7 3.3 %collective-permute-done.1.refs_2_ = bf16[128,256]{1,0:T(8,128)(2,1)S(1)} collective-permute-done((bf16[128,256]{1,0:T(8,128)(2,1)S(1)}, bf16[128,256]{1,0:T(8,128)(2,1)S(1)}, u32[]{:S(2)}, u32[]{:S(2)}) %collective-permute-start.1) | collective-permute-done | bytes 65568 | tf_op jit(solution)/shard_map/ppermute | solution.py:373
  146.0 1.1 collective-permute-done.refs_1_
  147.9 1.2 shard_map.119
  149.0 6.4 %all-to-all-start.5 = ((bf16[32,64,128]{2,1,0:T(8,128)(2,1)}), bf16[32,64,128]{2,1,0:T(8,128)(2,1)S(1)}, u32[]{:S(2)}, u32[]{:S(2)}) async-start(bf16[32,64,128]{2,1,0:T(8,128)(2,1)} %shard_map.119), calls=%async_computation.5 | async-start | bytes 1048576 | tf_op jit(solution)/shard_map/all_to_all | solution.py:393
  156.1 16.7 %all-to-all-done.5 = bf16[32,64,128]{2,1,0:T(8,128)(2,1)S(1)} async-done(((bf16[32,64,128]{2,1,0:T(8,128)(2,1)}), bf16[32,64,128]{2,1,0:T(8,128)(2,1)S(1)}, u32[]{:S(2)}, u32[]{:S(2)}) %all-to-all-start.5) | async-done | bytes 524320 | tf_op jit(solution)/shard_map/all_to_all | solution.py:393
  172.8 1.1 shard_map.120
  (32 shorter events, 4.0 us)
Async XLA Ops:
  0.6 60.0 %copy-start.7 = (s32[32,1,9]{0,1,2:T(1,128)S(1)}, s32[32,1,9]{0,1,2:T(1,128)}, u32[]{:S(2)}) copy-start(s32[32,1,9]{0,1,2:T(1,128)} %param.19) | copy-start | bytes 3460
  0.6 60.2 %copy-start.1 = (s32[1,1024]{1,0:T(1,128)S(1)}, s32[1,1024]{1,0:T(1,128)}, u32[]{:S(2)}) copy-start(s32[1,1024]{1,0:T(1,128)} %param.16) | copy-start | bytes 12292
  15.9 1.0 copy-start
  16.9 43.9 %copy-start.6 = (f32[32,1,256]{2,1,0:T(1,128)S(1)}, f32[32,1,256]{2,1,0:T(1,128)}, u32[]{:S(2)}) copy-start(f32[32,1,256]{2,1,0:T(1,128)} %param.14) | copy-start | bytes 98308
  18.6 29.7 %all-to-all-start.1 = ((bf16[16,256,128]{2,1,0:T(8,128)(2,1)}), bf16[16,256,128]{2,1,0:T(8,128)(2,1)S(1)}, u32[]{:S(2)}, u32[]{:S(2)}) async-start(bf16[16,256,128]{2,1,0:T(8,128)(2,1)} %bitcast.6), calls=%async_computation.1 | async-start | bytes 2097152 | tf_op jit(solution)/shard_map/all_to_all | solution.py:290
  24.3 0.9 copy-start.2
  25.2 0.9 copy-start.3
  26.1 0.9 copy-start.4
  27.0 0.8 copy-start.5
  48.3 33.1 %all-to-all-start.2 = ((bf16[32,40,256]{2,1,0:T(8,128)(2,1)}), bf16[32,40,256]{2,1,0:T(8,128)(2,1)S(1)}, u32[]{:S(2)}, u32[]{:S(2)}) async-start(bf16[32,40,256]{2,1,0:T(8,128)(2,1)} %shard_map.116), calls=%async_computation.2 | async-start | bytes 1310720 | tf_op jit(solution)/shard_map/all_to_all | solution.py:326
  81.4 14.3 %all-to-all-start.3 = ((bf16[4,32,256]{2,1,0:T(8,128)(2,1)}), bf16[4,32,256]{2,1,0:T(8,128)(2,1)S(1)}, u32[]{:S(2)}, u32[]{:S(2)}) async-start(bf16[4,32,256]{2,1,0:T(8,128)(2,1)} %get-tuple-element.15), calls=%async_computation.3 | async-start | bytes 131072 | tf_op jit(solution)/shard_map/all_to_all | solution.py:343
  95.6 52.2 %all-to-all-start.4 = ((bf16[512,8,128]{2,1,0:T(8,128)(2,1)}), bf16[512,8,128]{2,1,0:T(8,128)(2,1)S(1)}, u32[]{:S(2)}, u32[]{:S(2)}) async-start(bf16[512,8,128]{2,1,0:T(8,128)(2,1)} %bitcast.9), calls=%async_computation.4 | async-start | bytes 2097152 | tf_op jit(solution)/shard_map/all_to_all | solution.py:364
  108.8 22.9 %collective-permute-start.6 = (bf16[128,256]{1,0:T(8,128)(2,1)S(1)}, bf16[128,256]{1,0:T(8,128)(2,1)S(1)}, u32[]{:S(2)}, u32[]{:S(2)}) collective-permute-start(bf16[128,256]{1,0:T(8,128)(2,1)S(1)} %bitcast.29), channel_id=1, source_target_pairs={{0,448},{64,0},{128,64},{192,128},{256,192},{320,256},{384,320},{4... | collective-permute-start | bytes 196616 | tf_op jit(solution)/shard_map/ppermute | solution.py:373
  117.1 19.9 %collective-permute-start.5 = (bf16[128,256]{1,0:T(8,128)(2,1)S(1)}, bf16[128,256]{1,0:T(8,128)(2,1)S(1)}, u32[]{:S(2)}, u32[]{:S(2)}) collective-permute-start(bf16[128,256]{1,0:T(8,128)(2,1)S(1)} %bitcast.30), channel_id=1, source_target_pairs={{0,384},{64,448},{128,0},{192,64},{256,128},{320,192},{384,256},{4... | collective-permute-start | bytes 196616 | tf_op jit(solution)/shard_map/ppermute | solution.py:373
  120.3 21.5 %collective-permute-start.4 = (bf16[128,256]{1,0:T(8,128)(2,1)S(1)}, bf16[128,256]{1,0:T(8,128)(2,1)S(1)}, u32[]{:S(2)}, u32[]{:S(2)}) collective-permute-start(bf16[128,256]{1,0:T(8,128)(2,1)S(1)} %bitcast.31), channel_id=1, source_target_pairs={{0,320},{64,384},{128,448},{192,0},{256,64},{320,128},{384,192},{4... | collective-permute-start | bytes 196616 | tf_op jit(solution)/shard_map/ppermute | solution.py:373
  122.6 19.2 %collective-permute-start.3 = (bf16[128,256]{1,0:T(8,128)(2,1)S(1)}, bf16[128,256]{1,0:T(8,128)(2,1)S(1)}, u32[]{:S(2)}, u32[]{:S(2)}) collective-permute-start(bf16[128,256]{1,0:T(8,128)(2,1)S(1)} %bitcast.32), channel_id=1, source_target_pairs={{0,256},{64,320},{128,384},{192,448},{256,0},{320,64},{384,128},{4... | collective-permute-start | bytes 196616 | tf_op jit(solution)/shard_map/ppermute | solution.py:373
  129.7 13.0 %collective-permute-start.2 = (bf16[128,256]{1,0:T(8,128)(2,1)S(1)}, bf16[128,256]{1,0:T(8,128)(2,1)S(1)}, u32[]{:S(2)}, u32[]{:S(2)}) collective-permute-start(bf16[128,256]{1,0:T(8,128)(2,1)S(1)} %bitcast.33), channel_id=1, source_target_pairs={{0,192},{64,256},{128,320},{192,384},{256,448},{320,0},{384,64},{4... | collective-permute-start | bytes 196616 | tf_op jit(solution)/shard_map/ppermute | solution.py:373
  131.7 14.4 %collective-permute-start.1 = (bf16[128,256]{1,0:T(8,128)(2,1)S(1)}, bf16[128,256]{1,0:T(8,128)(2,1)S(1)}, u32[]{:S(2)}, u32[]{:S(2)}) collective-permute-start(bf16[128,256]{1,0:T(8,128)(2,1)S(1)} %bitcast.34), channel_id=1, source_target_pairs={{0,128},{64,192},{128,256},{192,320},{256,384},{320,448},{384,0},{... | collective-permute-start | bytes 196616 | tf_op jit(solution)/shard_map/ppermute | solution.py:373
  136.9 10.2 %collective-permute-start = (bf16[128,256]{1,0:T(8,128)(2,1)S(1)}, bf16[128,256]{1,0:T(8,128)(2,1)S(1)}, u32[]{:S(2)}, u32[]{:S(2)}) collective-permute-start(bf16[128,256]{1,0:T(8,128)(2,1)S(1)} %bitcast.35), channel_id=1, source_target_pairs={{0,64},{64,128},{128,192},{192,256},{256,320},{320,384},{384,448},... | collective-permute-start | bytes 196616 | tf_op jit(solution)/shard_map/ppermute | solution.py:373
  149.0 23.7 %all-to-all-start.5 = ((bf16[32,64,128]{2,1,0:T(8,128)(2,1)}), bf16[32,64,128]{2,1,0:T(8,128)(2,1)S(1)}, u32[]{:S(2)}, u32[]{:S(2)}) async-start(bf16[32,64,128]{2,1,0:T(8,128)(2,1)} %shard_map.119), calls=%async_computation.5 | async-start | bytes 1048576 | tf_op jit(solution)/shard_map/all_to_all | solution.py:393

commit v7 on v6

--- a/solution.py
+++ b/solution.py
@@ -1,3 +1,5 @@
+import functools
+
 import jax
 import jax.numpy as jnp
 from jax import lax
@@ -163,7 +165,7 @@
     total = rho_ref.shape[0]
     entries, block, _ = sums_ref.shape
     stride = hartree_ref.shape[1]
-    unroll = 2
+    unroll = slots
     start = pl.program_id(0) * slots
 
     @pl.when(start == 0)
@@ -227,16 +229,16 @@
         out_ref[h] = total
 
 
-def place_kernel(plan_ref, place_ref, *refs):
-    density_ref = refs[-1]
+def place_kernel(first, plan_ref, place_ref, *refs):
+    before_ref, density_ref = refs[0], refs[-1]
     slots = density_ref.shape[0]
     planes, length = plan_ref.shape
     own = lax.broadcasted_iota(jnp.int32, (slots, length), 0) + place_ref[1] * slots
-    total = jnp.zeros(density_ref.shape, f32)
-    for k in range(planes):
+    total = before_ref[...]
+    for k, plane_ref in enumerate(refs[1:-1], first):
         plane = lax.rem(place_ref[0] + (planes - k), planes)
         chosen = (own == plan_ref[pl.ds(plane, 1), :]).astype(f32).astype(bf16)
-        total += jnp.dot(chosen, refs[k][...], preferred_element_type=f32)
+        total += jnp.dot(chosen, plane_ref[...], preferred_element_type=f32)
     density_ref[...] = total
 
 
@@ -341,19 +343,20 @@
         moved=slots * width * grid * 2,
     )(pairs, basis, table)
     near = lax.all_to_all(copies, "x", split_axis=0, concat_axis=0, tiled=True).reshape(-1, grid)
+    wide = min(8, slots)
     partial, lists = call(
         matrix_kernel,
         (
             jax.ShapeDtypeStruct((ranks // 2, 2, columns, per_owner * piece, block), bf16),
             jax.ShapeDtypeStruct((ranks, block), f32),
         ),
-        [SMEM, SMEM, rows_of(group, width, grid), VMEM, VMEM, VMEM],
+        [SMEM, SMEM, rows_of(wide, width, grid), VMEM, VMEM, VMEM],
         [
             pltpu.VMEM((entries, block, block), f32),
             pltpu.VMEM((slots, grid), f32),
             pltpu.VMEM((ranks * stride, grid), f32),
         ],
-        grid=steps,
+        grid=(slots // wide,),
         limit=48,
         flops=slots * width * width * grid * 2,
         moved=slots * width * grid * 2,
@@ -373,12 +376,19 @@
         lax.ppermute(near, "z", [(n, (n + k) % planes) for n in range(planes)])
         for k in range(1, planes)
     ]
-    density = call(
-        place_kernel,
-        jax.ShapeDtypeStruct((slots, grid), f32),
-        [VMEM, SMEM] + [VMEM] * planes,
-        moved=ranks * slots * grid * 2,
-    )(load_plan.reshape(planes, -1), jnp.stack([lax.axis_index("z"), rank]), *spread)
+    place = jnp.stack([lax.axis_index("z"), rank])
+
+    def placed(before, first, last):
+        count = last - first
+        return call(
+            functools.partial(place_kernel, first),
+            jax.ShapeDtypeStruct((slots, grid), f32),
+            [VMEM, SMEM] + [VMEM] * (1 + count),
+            moved=ranks * slots * grid * 2,
+        )(load_plan.reshape(planes, -1), place, before, *spread[first:last])
+
+    cut = planes // 2 + 1
+    density = placed(jnp.zeros((slots, grid), f32), 0, cut)
 
     targets = lists[:, :entries].astype(jnp.int32).reshape(ranks * entries, 1) * piece
     targets = (targets + jnp.arange(piece, dtype=jnp.int32)[None]).reshape(
@@ -390,6 +400,7 @@
         [VMEM, VMEM, HBM],
         moved=ranks * columns * rows * block * 2,
     )(targets, received, density)
+    density = placed(density, cut, planes)
     gathered = lax.all_to_all(totals, BATCH, split_axis=0, concat_axis=0, tiled=True)
     hamiltonian = call(
         merge_kernel,

time: 175 us -> 179 us (1.023)
  the two profiles are of different devices: /device:TPU:8 before, /device:TPU:66 now
where the time goes in v7:
time: 179 us; the launch traced here: 177 us
  starting transfers between devices  70 us (39%)
  waiting for transfers between devices  50.9 us (28%)
  Pallas kernels  33.3 us (19%)
  blocking collectives  14.6 us (8%)
  local copies, waits for them, and re-layouts  7.53 us (4%)
    ppermute x7, starting transfers between devices, on_device(): lax.ppermute(near, 'z', [(n, (n + k) % planes) for n in range(planes)])  29.8 us
    ppermute x7, waiting for transfers between devices, on_device(): lax.ppermute(near, 'z', [(n, (n + k) % planes) for n in range(planes)])  29.6 us
    all_to_all x1, blocking collectives, on_device(): lax.all_to_all(wanted, 'blk', split_axis=0, concat_axis=0, tiled=True)  14.6 us
    all_to_all x1, starting transfers between devices, on_device(): lax.all_to_all(lines, BATCH, split_axis=0, concat_axis=0, tiled=True)  12.6 us
    all_to_all x1, starting transfers between devices, on_device(): lax.all_to_all(partial.reshape(ranks * columns, rows, block), BATCH + ('b...  11.7 us
    all_to_all x1, waiting for transfers between devices, on_device(): lax.all_to_all(sent.reshape(columns, per_owner * block, block), 'blk', sp...  11.4 us
    pallas_call x1, Pallas kernels, on_device(): call(basis_kernel, (jax.ShapeDtypeStruct((slots, width, grid), bf16), jax...  9.86 us
    all_to_all x1, waiting for transfers between devices, on_device(): lax.all_to_all(lines, BATCH, split_axis=0, concat_axis=0, tiled=True)  9.86 us
  transfers between devices with their start and end apart: 12, of which 8 were waited for; matrix products, arithmetic and copies ran while one was open for 1% of the time, Pallas kernels for 17%

profile of v7, /device:TPU:66, one launch (start us, length us, event | category | flops | bytes accessed | tf_op | source)
XLA Modules:
  0.0 177.4 jit_solution(12372529658266793675)
XLA Ops:
  1.4 14.6 %all_to_all.30.asked_ref = s32[16,1,2]{2,1,0:T(1,128)S(1)} all-to-all(s32[16,1,2]{2,1,0:T(1,128)S(1)} %copy.15), channel_id=1, replica_groups=mesh['z'=8,'x'=4,'blk'=16] {'blk'}, dimensions={0} | all-to-all | bytes 256 | tf_op jit(solution)/shard_map/all_to_all | solution.py:285
  16.0 1.0 copy-done
  17.0 1.7 shard_map.114
  18.7 3.7 %all-to-all-start.1 = ((bf16[16,256,128]{2,1,0:T(8,128)(2,1)}), bf16[16,256,128]{2,1,0:T(8,128)(2,1)S(1)}, u32[]{:S(2)}, u32[]{:S(2)}) async-start(bf16[16,256,128]{2,1,0:T(8,128)(2,1)} %bitcast.6), calls=%async_computation.1 | async-start | bytes 2097152 | tf_op jit(solution)/shard_map/all_to_all | solution.py:292
  23.2 0.9 copy-done.2
  24.1 0.9 copy-done.3
  25.0 0.9 copy-done.4
  25.9 0.8 copy-done.5
  26.7 9.9 %shard_map.113 = (bf16[32,384,256]{2,1,0:T(8,128)(2,1)}, f32[8,128]{1,0:T(8,128)S(1)}) custom-call(f32[192,128]{1,0:T(8,128)S(1)} %bitcast.43, f32[288,128]{1,0:T(8,128)S(1)} %bitcast.41, f32[96,128]{1,0:T(8,128)S(1)} %bitcast.44, f32[288,128]{1,0:T(8,128)S(1)} %bitcast.42), custom_call_target="tpu_custom_call" | custom-call | flops 1258291200 | bytes 6291456 | tf_op jit(solution)/shard_map/pallas_call | solution.py:298
  36.7 0.9 shard_map.116
  37.6 11.4 %all-to-all-done.1 = bf16[16,256,128]{2,1,0:T(8,128)(2,1)S(1)} async-done(((bf16[16,256,128]{2,1,0:T(8,128)(2,1)}), bf16[16,256,128]{2,1,0:T(8,128)(2,1)S(1)}, u32[]{:S(2)}, u32[]{:S(2)}) %all-to-all-start.1) | async-done | bytes 1048608 | tf_op jit(solution)/shard_map/all_to_all | solution.py:292
  49.0 12.6 %all-to-all-start.2 = ((bf16[32,40,256]{2,1,0:T(8,128)(2,1)}), bf16[32,40,256]{2,1,0:T(8,128)(2,1)S(1)}, u32[]{:S(2)}, u32[]{:S(2)}) async-start(bf16[32,40,256]{2,1,0:T(8,128)(2,1)} %shard_map.116), calls=%async_computation.2 | async-start | bytes 1310720 | tf_op jit(solution)/shard_map/all_to_all | solution.py:328
  61.9 9.4 %shard_map.115 = (f32[32,256]{1,0:T(8,128)S(1)}, bf16[4,32,256]{2,1,0:T(8,128)(2,1)}) custom-call(s32[288]{0:T(512)S(1)} %reshape.92.pairs_ref, bf16[32,384,256]{2,1,0:T(8,128)(2,1)} %get-tuple-element.10.basis_ref, bf16[32,128,128]{2,1,0:T(8,128)(2,1)S(1)} %bitcast.27), custom_call_target="tpu_custom_call" | custom-call | flops 2415919104 | bytes 6291456 | tf_op jit(solution)/shard_map/pallas_call | solution.py:332
  71.3 9.9 %all-to-all-done.2.hartree_ref = bf16[32,40,256]{2,1,0:T(8,128)(2,1)S(1)} async-done(((bf16[32,40,256]{2,1,0:T(8,128)(2,1)}), bf16[32,40,256]{2,1,0:T(8,128)(2,1)S(1)}, u32[]{:S(2)}, u32[]{:S(2)}) %all-to-all-start.2) | async-done | bytes 655392 | tf_op jit(solution)/shard_map/all_to_all | solution.py:328
  81.2 4.9 %all-to-all-start.3 = ((bf16[4,32,256]{2,1,0:T(8,128)(2,1)}), bf16[4,32,256]{2,1,0:T(8,128)(2,1)S(1)}, u32[]{:S(2)}, u32[]{:S(2)}) async-start(bf16[4,32,256]{2,1,0:T(8,128)(2,1)} %get-tuple-element.15), calls=%async_computation.3 | async-start | bytes 131072 | tf_op jit(solution)/shard_map/all_to_all | solution.py:345
  86.1 7.7 %shard_map.117 = (bf16[16,2,16,8,128]{4,3,2,1,0:T(8,128)(2,1)}, f32[32,128]{1,0:T(8,128)S(1)}) custom-call(s32[288]{0:T(512)S(1)} %reshape.92.pairs_ref, s32[32]{0:T(128)S(1)} %dynamic-slice_bitcast_fusion.plan_ref, bf16[32,384,256]{2,1,0:T(8,128)(2,1)} %get-tuple-element.10.basis_ref, f32[32,256]{1,0:T(8,128)S(1)} %get-tuple-element.11.rho_ref, ...), custom_call_target="tpu_custom_call" | custom-call | flops 2415919104 | bytes 6291456 | tf_op jit(solution)/shard_map/pallas_call | solution.py:347
  93.9 11.7 %all-to-all-start.4 = ((bf16[512,8,128]{2,1,0:T(8,128)(2,1)}), bf16[512,8,128]{2,1,0:T(8,128)(2,1)S(1)}, u32[]{:S(2)}, u32[]{:S(2)}) async-start(bf16[512,8,128]{2,1,0:T(8,128)(2,1)} %bitcast.9), calls=%async_computation.4 | async-start | bytes 2097152 | tf_op jit(solution)/shard_map/all_to_all | solution.py:367
  105.8 8.5 %collective-permute-start.3 = (bf16[128,256]{1,0:T(8,128)(2,1)S(1)}, bf16[128,256]{1,0:T(8,128)(2,1)S(1)}, u32[]{:S(2)}, u32[]{:S(2)}) collective-permute-start(bf16[128,256]{1,0:T(8,128)(2,1)S(1)} %bitcast.28), channel_id=1, source_target_pairs={{0,256},{64,320},{128,384},{192,448},{256,0},{320,64},{384,128},{4... | collective-permute-start | bytes 196616 | tf_op jit(solution)/shard_map/ppermute | solution.py:376
  114.3 1.9 %collective-permute-start.2 = (bf16[128,256]{1,0:T(8,128)(2,1)S(1)}, bf16[128,256]{1,0:T(8,128)(2,1)S(1)}, u32[]{:S(2)}, u32[]{:S(2)}) collective-permute-start(bf16[128,256]{1,0:T(8,128)(2,1)S(1)} %bitcast.29), channel_id=1, source_target_pairs={{0,192},{64,256},{128,320},{192,384},{256,448},{320,0},{384,64},{4... | collective-permute-start | bytes 196616 | tf_op jit(solution)/shard_map/ppermute | solution.py:376
  116.2 3.5 %collective-permute-start.1 = (bf16[128,256]{1,0:T(8,128)(2,1)S(1)}, bf16[128,256]{1,0:T(8,128)(2,1)S(1)}, u32[]{:S(2)}, u32[]{:S(2)}) collective-permute-start(bf16[128,256]{1,0:T(8,128)(2,1)S(1)} %bitcast.30), channel_id=1, source_target_pairs={{0,128},{64,192},{128,256},{192,320},{256,384},{320,448},{384,0},{... | collective-permute-start | bytes 196616 | tf_op jit(solution)/shard_map/ppermute | solution.py:376
  119.8 3.6 %collective-permute-start = (bf16[128,256]{1,0:T(8,128)(2,1)S(1)}, bf16[128,256]{1,0:T(8,128)(2,1)S(1)}, u32[]{:S(2)}, u32[]{:S(2)}) collective-permute-start(bf16[128,256]{1,0:T(8,128)(2,1)S(1)} %bitcast.31), channel_id=1, source_target_pairs={{0,64},{64,128},{128,192},{192,256},{256,320},{320,384},{384,448},... | collective-permute-start | bytes 196616 | tf_op jit(solution)/shard_map/ppermute | solution.py:376
  123.9 11.4 %collective-permute-done.3.refs_5_ = bf16[128,256]{1,0:T(8,128)(2,1)S(1)} collective-permute-done((bf16[128,256]{1,0:T(8,128)(2,1)S(1)}, bf16[128,256]{1,0:T(8,128)(2,1)S(1)}, u32[]{:S(2)}, u32[]{:S(2)}) %collective-permute-start.3) | collective-permute-done | bytes 65568 | tf_op jit(solution)/shard_map/ppermute | solution.py:376
  135.3 4.2 %collective-permute-done.2.refs_4_ = bf16[128,256]{1,0:T(8,128)(2,1)S(1)} collective-permute-done((bf16[128,256]{1,0:T(8,128)(2,1)S(1)}, bf16[128,256]{1,0:T(8,128)(2,1)S(1)}, u32[]{:S(2)}, u32[]{:S(2)}) %collective-permute-start.2) | collective-permute-done | bytes 65568 | tf_op jit(solution)/shard_map/ppermute | solution.py:376
  139.5 2.0 %collective-permute-done.1.refs_3_ = bf16[128,256]{1,0:T(8,128)(2,1)S(1)} collective-permute-done((bf16[128,256]{1,0:T(8,128)(2,1)S(1)}, bf16[128,256]{1,0:T(8,128)(2,1)S(1)}, u32[]{:S(2)}, u32[]{:S(2)}) %collective-permute-start.1) | collective-permute-done | bytes 65568 | tf_op jit(solution)/shard_map/ppermute | solution.py:376
  142.3 1.2 shard_map.119
  143.5 7.3 %all-to-all-start.5 = ((bf16[32,64,128]{2,1,0:T(8,128)(2,1)}), bf16[32,64,128]{2,1,0:T(8,128)(2,1)S(1)}, u32[]{:S(2)}, u32[]{:S(2)}) async-start(bf16[32,64,128]{2,1,0:T(8,128)(2,1)} %shard_map.119), calls=%async_computation.5 | async-start | bytes 1048576 | tf_op jit(solution)/shard_map/all_to_all | solution.py:404
  150.8 2.5 %collective-permute-start.6 = (bf16[128,256]{1,0:T(8,128)(2,1)S(1)}, bf16[128,256]{1,0:T(8,128)(2,1)S(1)}, u32[]{:S(2)}, u32[]{:S(2)}) collective-permute-start(bf16[128,256]{1,0:T(8,128)(2,1)S(1)} %bitcast.33), channel_id=1, source_target_pairs={{0,448},{64,0},{128,64},{192,128},{256,192},{320,256},{384,320},{4... | collective-permute-start | bytes 196616 | tf_op jit(solution)/shard_map/ppermute | solution.py:376
  153.3 5.5 %collective-permute-start.5 = (bf16[128,256]{1,0:T(8,128)(2,1)S(1)}, bf16[128,256]{1,0:T(8,128)(2,1)S(1)}, u32[]{:S(2)}, u32[]{:S(2)}) collective-permute-start(bf16[128,256]{1,0:T(8,128)(2,1)S(1)} %bitcast.34), channel_id=1, source_target_pairs={{0,384},{64,448},{128,0},{192,64},{256,128},{320,192},{384,256},{4... | collective-permute-start | bytes 196616 | tf_op jit(solution)/shard_map/ppermute | solution.py:376
  158.8 4.2 %collective-permute-start.4 = (bf16[128,256]{1,0:T(8,128)(2,1)S(1)}, bf16[128,256]{1,0:T(8,128)(2,1)S(1)}, u32[]{:S(2)}, u32[]{:S(2)}) collective-permute-start(bf16[128,256]{1,0:T(8,128)(2,1)S(1)} %bitcast.35), channel_id=1, source_target_pairs={{0,320},{64,384},{128,448},{192,0},{256,64},{320,128},{384,192},{4... | collective-permute-start | bytes 196616 | tf_op jit(solution)/shard_map/ppermute | solution.py:376
  163.0 5.4 %collective-permute-done.6.refs_3_ = bf16[128,256]{1,0:T(8,128)(2,1)S(1)} collective-permute-done((bf16[128,256]{1,0:T(8,128)(2,1)S(1)}, bf16[128,256]{1,0:T(8,128)(2,1)S(1)}, u32[]{:S(2)}, u32[]{:S(2)}) %collective-permute-start.6) | collective-permute-done | bytes 65568 | tf_op jit(solution)/shard_map/ppermute | solution.py:376
  168.7 6.2 %collective-permute-done.4.refs_1_ = bf16[128,256]{1,0:T(8,128)(2,1)S(1)} collective-permute-done((bf16[128,256]{1,0:T(8,128)(2,1)S(1)}, bf16[128,256]{1,0:T(8,128)(2,1)S(1)}, u32[]{:S(2)}, u32[]{:S(2)}) %collective-permute-start.4) | collective-permute-done | bytes 65568 | tf_op jit(solution)/shard_map/ppermute | solution.py:376
  176.3 1.1 shard_map.120
  (34 shorter events, 5.0 us)
Async XLA Ops:
  0.6 61.0 %copy-start.7 = (s32[32,1,9]{0,1,2:T(1,128)S(1)}, s32[32,1,9]{0,1,2:T(1,128)}, u32[]{:S(2)}) copy-start(s32[32,1,9]{0,1,2:T(1,128)} %param.19) | copy-start | bytes 3460
  0.6 61.2 %copy-start.1 = (s32[1,1024]{1,0:T(1,128)S(1)}, s32[1,1024]{1,0:T(1,128)}, u32[]{:S(2)}) copy-start(s32[1,1024]{1,0:T(1,128)} %param.16) | copy-start | bytes 12292
  16.0 1.0 copy-start
  17.0 44.8 %copy-start.6 = (f32[32,1,256]{2,1,0:T(1,128)S(1)}, f32[32,1,256]{2,1,0:T(1,128)}, u32[]{:S(2)}) copy-start(f32[32,1,256]{2,1,0:T(1,128)} %param.14) | copy-start | bytes 98308
  18.7 30.3 %all-to-all-start.1 = ((bf16[16,256,128]{2,1,0:T(8,128)(2,1)}), bf16[16,256,128]{2,1,0:T(8,128)(2,1)S(1)}, u32[]{:S(2)}, u32[]{:S(2)}) async-start(bf16[16,256,128]{2,1,0:T(8,128)(2,1)} %bitcast.6), calls=%async_computation.1 | async-start | bytes 2097152 | tf_op jit(solution)/shard_map/all_to_all | solution.py:292
  23.2 0.9 copy-start.2
  24.1 0.9 copy-start.3
  25.0 0.9 copy-start.4
  25.9 0.8 copy-start.5
  49.0 32.2 %all-to-all-start.2 = ((bf16[32,40,256]{2,1,0:T(8,128)(2,1)}), bf16[32,40,256]{2,1,0:T(8,128)(2,1)S(1)}, u32[]{:S(2)}, u32[]{:S(2)}) async-start(bf16[32,40,256]{2,1,0:T(8,128)(2,1)} %shard_map.116), calls=%async_computation.2 | async-start | bytes 1310720 | tf_op jit(solution)/shard_map/all_to_all | solution.py:328
  81.2 12.7 %all-to-all-start.3 = ((bf16[4,32,256]{2,1,0:T(8,128)(2,1)}), bf16[4,32,256]{2,1,0:T(8,128)(2,1)S(1)}, u32[]{:S(2)}, u32[]{:S(2)}) async-start(bf16[4,32,256]{2,1,0:T(8,128)(2,1)} %get-tuple-element.15), calls=%async_computation.3 | async-start | bytes 131072 | tf_op jit(solution)/shard_map/all_to_all | solution.py:345
  93.9 48.5 %all-to-all-start.4 = ((bf16[512,8,128]{2,1,0:T(8,128)(2,1)}), bf16[512,8,128]{2,1,0:T(8,128)(2,1)S(1)}, u32[]{:S(2)}, u32[]{:S(2)}) async-start(bf16[512,8,128]{2,1,0:T(8,128)(2,1)} %bitcast.9), calls=%async_computation.4 | async-start | bytes 2097152 | tf_op jit(solution)/shard_map/all_to_all | solution.py:367
  105.8 29.6 %collective-permute-start.3 = (bf16[128,256]{1,0:T(8,128)(2,1)S(1)}, bf16[128,256]{1,0:T(8,128)(2,1)S(1)}, u32[]{:S(2)}, u32[]{:S(2)}) collective-permute-start(bf16[128,256]{1,0:T(8,128)(2,1)S(1)} %bitcast.28), channel_id=1, source_target_pairs={{0,256},{64,320},{128,384},{192,448},{256,0},{320,64},{384,128},{4... | collective-permute-start | bytes 196616 | tf_op jit(solution)/shard_map/ppermute | solution.py:376
  114.3 25.2 %collective-permute-start.2 = (bf16[128,256]{1,0:T(8,128)(2,1)S(1)}, bf16[128,256]{1,0:T(8,128)(2,1)S(1)}, u32[]{:S(2)}, u32[]{:S(2)}) collective-permute-start(bf16[128,256]{1,0:T(8,128)(2,1)S(1)} %bitcast.29), channel_id=1, source_target_pairs={{0,192},{64,256},{128,320},{192,384},{256,448},{320,0},{384,64},{4... | collective-permute-start | bytes 196616 | tf_op jit(solution)/shard_map/ppermute | solution.py:376
  116.2 25.4 %collective-permute-start.1 = (bf16[128,256]{1,0:T(8,128)(2,1)S(1)}, bf16[128,256]{1,0:T(8,128)(2,1)S(1)}, u32[]{:S(2)}, u32[]{:S(2)}) collective-permute-start(bf16[128,256]{1,0:T(8,128)(2,1)S(1)} %bitcast.30), channel_id=1, source_target_pairs={{0,128},{64,192},{128,256},{192,320},{256,384},{320,448},{384,0},{... | collective-permute-start | bytes 196616 | tf_op jit(solution)/shard_map/ppermute | solution.py:376
  119.8 21.8 %collective-permute-start = (bf16[128,256]{1,0:T(8,128)(2,1)S(1)}, bf16[128,256]{1,0:T(8,128)(2,1)S(1)}, u32[]{:S(2)}, u32[]{:S(2)}) collective-permute-start(bf16[128,256]{1,0:T(8,128)(2,1)S(1)} %bitcast.31), channel_id=1, source_target_pairs={{0,64},{64,128},{128,192},{192,256},{256,320},{320,384},{384,448},... | collective-permute-start | bytes 196616 | tf_op jit(solution)/shard_map/ppermute | solution.py:376
  143.5 32.9 %all-to-all-start.5 = ((bf16[32,64,128]{2,1,0:T(8,128)(2,1)}), bf16[32,64,128]{2,1,0:T(8,128)(2,1)S(1)}, u32[]{:S(2)}, u32[]{:S(2)}) async-start(bf16[32,64,128]{2,1,0:T(8,128)(2,1)} %shard_map.119), calls=%async_computation.5 | async-start | bytes 1048576 | tf_op jit(solution)/shard_map/all_to_all | solution.py:404
  150.8 17.6 %collective-permute-start.6 = (bf16[128,256]{1,0:T(8,128)(2,1)S(1)}, bf16[128,256]{1,0:T(8,128)(2,1)S(1)}, u32[]{:S(2)}, u32[]{:S(2)}) collective-permute-start(bf16[128,256]{1,0:T(8,128)(2,1)S(1)} %bitcast.33), channel_id=1, source_target_pairs={{0,448},{64,0},{128,64},{192,128},{256,192},{320,256},{384,320},{4... | collective-permute-start | bytes 196616 | tf_op jit(solution)/shard_map/ppermute | solution.py:376
  153.3 15.5 %collective-permute-start.5 = (bf16[128,256]{1,0:T(8,128)(2,1)S(1)}, bf16[128,256]{1,0:T(8,128)(2,1)S(1)}, u32[]{:S(2)}, u32[]{:S(2)}) collective-permute-start(bf16[128,256]{1,0:T(8,128)(2,1)S(1)} %bitcast.34), channel_id=1, source_target_pairs={{0,384},{64,448},{128,0},{192,64},{256,128},{320,192},{384,256},{4... | collective-permute-start | bytes 196616 | tf_op jit(solution)/shard_map/ppermute | solution.py:376
  158.8 16.2 %collective-permute-start.4 = (bf16[128,256]{1,0:T(8,128)(2,1)S(1)}, bf16[128,256]{1,0:T(8,128)(2,1)S(1)}, u32[]{:S(2)}, u32[]{:S(2)}) collective-permute-start(bf16[128,256]{1,0:T(8,128)(2,1)S(1)} %bitcast.35), channel_id=1, source_target_pairs={{0,320},{64,384},{128,448},{192,0},{256,64},{320,128},{384,192},{4... | collective-permute-start | bytes 196616 | tf_op jit(solution)/shard_map/ppermute | solution.py:376

commit v8 on v6

--- a/solution.py
+++ b/solution.py
@@ -163,7 +163,7 @@
     total = rho_ref.shape[0]
     entries, block, _ = sums_ref.shape
     stride = hartree_ref.shape[1]
-    unroll = 2
+    unroll = slots
     start = pl.program_id(0) * slots
 
     @pl.when(start == 0)
@@ -227,17 +227,12 @@
         out_ref[h] = total
 
 
-def place_kernel(plan_ref, place_ref, *refs):
-    density_ref = refs[-1]
+def place_kernel(spread_ref, plan_ref, rank_ref, density_ref):
     slots = density_ref.shape[0]
-    planes, length = plan_ref.shape
-    own = lax.broadcasted_iota(jnp.int32, (slots, length), 0) + place_ref[1] * slots
-    total = jnp.zeros(density_ref.shape, f32)
-    for k in range(planes):
-        plane = lax.rem(place_ref[0] + (planes - k), planes)
-        chosen = (own == plan_ref[pl.ds(plane, 1), :]).astype(f32).astype(bf16)
-        total += jnp.dot(chosen, refs[k][...], preferred_element_type=f32)
-    density_ref[...] = total
+    length = plan_ref.shape[1]
+    own = lax.broadcasted_iota(jnp.int32, (slots, length), 0) + rank_ref[0] * slots
+    chosen = (own == plan_ref[...]).astype(f32).astype(bf16)
+    density_ref[...] = jnp.dot(chosen, spread_ref[...], preferred_element_type=f32)
 
 
 def merge_kernel(received_ref, out_ref):
@@ -341,19 +336,20 @@
         moved=slots * width * grid * 2,
     )(pairs, basis, table)
     near = lax.all_to_all(copies, "x", split_axis=0, concat_axis=0, tiled=True).reshape(-1, grid)
+    wide = min(8, slots)
     partial, lists = call(
         matrix_kernel,
         (
             jax.ShapeDtypeStruct((ranks // 2, 2, columns, per_owner * piece, block), bf16),
             jax.ShapeDtypeStruct((ranks, block), f32),
         ),
-        [SMEM, SMEM, rows_of(group, width, grid), VMEM, VMEM, VMEM],
+        [SMEM, SMEM, rows_of(wide, width, grid), VMEM, VMEM, VMEM],
         [
             pltpu.VMEM((entries, block, block), f32),
             pltpu.VMEM((slots, grid), f32),
             pltpu.VMEM((ranks * stride, grid), f32),
         ],
-        grid=steps,
+        grid=(slots // wide,),
         limit=48,
         flops=slots * width * width * grid * 2,
         moved=slots * width * grid * 2,
@@ -368,17 +364,13 @@
         concat_axis=0,
         tiled=True,
     ).reshape(ranks * columns * rows, block)
-    planes = lax.axis_size("z")
-    spread = [near] + [
-        lax.ppermute(near, "z", [(n, (n + k) % planes) for n in range(planes)])
-        for k in range(1, planes)
-    ]
+    spread = lax.all_gather(near, "z", axis=0, tiled=True)
     density = call(
         place_kernel,
         jax.ShapeDtypeStruct((slots, grid), f32),
-        [VMEM, SMEM] + [VMEM] * planes,
+        [VMEM, VMEM, SMEM],
         moved=ranks * slots * grid * 2,
-    )(load_plan.reshape(planes, -1), jnp.stack([lax.axis_index("z"), rank]), *spread)
+    )(spread, load_plan, rank.reshape(1))
 
     targets = lists[:, :entries].astype(jnp.int32).reshape(ranks * entries, 1) * piece
     targets = (targets + jnp.arange(piece, dtype=jnp.int32)[None]).reshape(

time: 175 us -> 176 us (level)
  the two profiles are of different devices: /device:TPU:8 before, /device:TPU:32 now
where the time goes in v8:
time: 176 us; the launch traced here: 175 us
  blocking collectives  56.2 us (32%)
  starting transfers between devices  45.2 us (26%)
  waiting for transfers between devices  33.2 us (19%)
  Pallas kernels  32.1 us (18%)
  local copies, waits for them, and re-layouts  7.51 us (4%)
    all_gather x1, blocking collectives, on_device(): spread = lax.all_gather(near, 'z', axis=0, tiled=True)  45.9 us
    all_to_all x1, starting transfers between devices, on_device(): lax.all_to_all(partial.reshape(ranks * columns, rows, block), BATCH + ('b...  13.9 us
    all_to_all x1, waiting for transfers between devices, on_device(): lax.all_to_all(totals, BATCH, split_axis=0, concat_axis=0, tiled=True)  13.4 us
    all_to_all x1, starting transfers between devices, on_device(): lax.all_to_all(lines, BATCH, split_axis=0, concat_axis=0, tiled=True)  12.3 us
    all_to_all x1, waiting for transfers between devices, on_device(): lax.all_to_all(lines, BATCH, split_axis=0, concat_axis=0, tiled=True)  10.8 us
    all_to_all x1, blocking collectives, on_device(): lax.all_to_all(wanted, 'blk', split_axis=0, concat_axis=0, tiled=True)  10.3 us
    pallas_call x1, Pallas kernels, on_device(): call(basis_kernel, (jax.ShapeDtypeStruct((slots, width, grid), bf16), jax...  9.84 us
    pallas_call x1, Pallas kernels, on_device(): call(density_kernel, (jax.ShapeDtypeStruct((slots, grid), f32), jax.Shape...  9.43 us
  transfers between devices with their start and end apart: 5, of which 3 were waited for; matrix products, arithmetic and copies ran while one was open for 1% of the time, Pallas kernels for 16%

profile of v8, /device:TPU:32, one launch (start us, length us, event | category | flops | bytes accessed | tf_op | source)
XLA Modules:
  0.0 175.1 jit_solution(3557716621945677591)
XLA Ops:
  0.7 0.8 copy.15
  1.4 10.3 %all_to_all.30.asked_ref = s32[16,1,2]{2,1,0:T(1,128)S(1)} all-to-all(s32[16,1,2]{2,1,0:T(1,128)S(1)} %copy.15), channel_id=1, replica_groups=mesh['z'=8,'x'=4,'blk'=16] {'blk'}, dimensions={0} | all-to-all | bytes 256 | tf_op jit(solution)/shard_map/all_to_all | solution.py:278
  11.7 1.0 copy-done
  12.7 1.7 shard_map.114
  14.4 8.8 %all-to-all-start.1 = ((bf16[16,256,128]{2,1,0:T(8,128)(2,1)}), bf16[16,256,128]{2,1,0:T(8,128)(2,1)S(1)}, u32[]{:S(2)}, u32[]{:S(2)}) async-start(bf16[16,256,128]{2,1,0:T(8,128)(2,1)} %bitcast.6), calls=%async_computation.1 | async-start | bytes 2097152 | tf_op jit(solution)/shard_map/all_to_all | solution.py:285
  23.2 0.8 copy.22
  24.0 0.9 copy-done.2
  24.9 0.9 copy-done.3
  25.8 0.9 copy-done.4
  26.7 0.8 copy-done.5
  27.5 9.8 %shard_map.113 = (bf16[32,384,256]{2,1,0:T(8,128)(2,1)}, f32[8,128]{1,0:T(8,128)S(1)}) custom-call(f32[192,128]{1,0:T(8,128)S(1)} %bitcast.31, f32[288,128]{1,0:T(8,128)S(1)} %bitcast.29, f32[96,128]{1,0:T(8,128)S(1)} %bitcast.32, f32[288,128]{1,0:T(8,128)S(1)} %bitcast.30), custom_call_target="tpu_custom_call" | custom-call | flops 1258291200 | bytes 6291456 | tf_op jit(solution)/shard_map/pallas_call | solution.py:291
  37.4 0.1 convert_element_type.20
  37.5 0.9 shard_map.116
  38.4 9.1 %all-to-all-done.1 = bf16[16,256,128]{2,1,0:T(8,128)(2,1)S(1)} async-done(((bf16[16,256,128]{2,1,0:T(8,128)(2,1)}), bf16[16,256,128]{2,1,0:T(8,128)(2,1)S(1)}, u32[]{:S(2)}, u32[]{:S(2)}) %all-to-all-start.1) | async-done | bytes 1048608 | tf_op jit(solution)/shard_map/all_to_all | solution.py:285
  47.5 12.3 %all-to-all-start.2 = ((bf16[32,40,256]{2,1,0:T(8,128)(2,1)}), bf16[32,40,256]{2,1,0:T(8,128)(2,1)S(1)}, u32[]{:S(2)}, u32[]{:S(2)}) async-start(bf16[32,40,256]{2,1,0:T(8,128)(2,1)} %shard_map.116), calls=%async_computation.2 | async-start | bytes 1310720 | tf_op jit(solution)/shard_map/all_to_all | solution.py:321
  59.7 0.1 copy.14
  59.8 0.1 reshape.91.pairs_ref
  60.0 0.1 dynamic-slice_bitcast_fusion.plan_ref
  60.0 9.4 %shard_map.115 = (f32[32,256]{1,0:T(8,128)S(1)}, bf16[4,32,256]{2,1,0:T(8,128)(2,1)}) custom-call(s32[288]{0:T(512)S(1)} %reshape.91.pairs_ref, bf16[32,384,256]{2,1,0:T(8,128)(2,1)} %get-tuple-element.10.basis_ref, bf16[32,128,128]{2,1,0:T(8,128)(2,1)S(1)} %bitcast.25), custom_call_target="tpu_custom_call" | custom-call | flops 2415919104 | bytes 6291456 | tf_op jit(solution)/shard_map/pallas_call | solution.py:325
  69.5 10.8 %all-to-all-done.2.hartree_ref = bf16[32,40,256]{2,1,0:T(8,128)(2,1)S(1)} async-done(((bf16[32,40,256]{2,1,0:T(8,128)(2,1)}), bf16[32,40,256]{2,1,0:T(8,128)(2,1)S(1)}, u32[]{:S(2)}, u32[]{:S(2)}) %all-to-all-start.2) | async-done | bytes 655392 | tf_op jit(solution)/shard_map/all_to_all | solution.py:321
  80.2 4.0 %all-to-all-start.3 = ((bf16[4,32,256]{2,1,0:T(8,128)(2,1)}), bf16[4,32,256]{2,1,0:T(8,128)(2,1)S(1)}, u32[]{:S(2)}, u32[]{:S(2)}) async-start(bf16[4,32,256]{2,1,0:T(8,128)(2,1)} %get-tuple-element.15), calls=%async_computation.3 | async-start | bytes 131072 | tf_op jit(solution)/shard_map/all_to_all | solution.py:338
  84.2 7.7 %shard_map.117 = (bf16[16,2,16,8,128]{4,3,2,1,0:T(8,128)(2,1)}, f32[32,128]{1,0:T(8,128)S(1)}) custom-call(s32[288]{0:T(512)S(1)} %reshape.91.pairs_ref, s32[32]{0:T(128)S(1)} %dynamic-slice_bitcast_fusion.plan_ref, bf16[32,384,256]{2,1,0:T(8,128)(2,1)} %get-tuple-element.10.basis_ref, f32[32,256]{1,0:T(8,128)S(1)} %get-tuple-element.11.rho_ref, ...), custom_call_target="tpu_custom_call" | custom-call | flops 2415919104 | bytes 6291456 | tf_op jit(solution)/shard_map/pallas_call | solution.py:340
  91.9 13.9 %all-to-all-start.4 = ((bf16[512,8,128]{2,1,0:T(8,128)(2,1)}), bf16[512,8,128]{2,1,0:T(8,128)(2,1)S(1)}, u32[]{:S(2)}, u32[]{:S(2)}) async-start(bf16[512,8,128]{2,1,0:T(8,128)(2,1)} %bitcast.9), calls=%async_computation.4 | async-start | bytes 2097152 | tf_op jit(solution)/shard_map/all_to_all | solution.py:360
  105.9 0.2 iota_add_fusion
  106.1 0.3 add.36.target_ref
  106.4 45.9 %all_gather.3.spread_ref = bf16[1024,256]{1,0:T(8,128)(2,1)S(1)} all-gather(bf16[128,256]{1,0:T(8,128)(2,1)S(1)} %bitcast.33), channel_id=1, replica_groups=mesh['z'=8,'x'=4,'blk'=16] {'z'}, dimensions={0}, use_global_device_ids=true | all-gather | bytes 589824 | tf_op jit(solution)/shard_map/all_gather | solution.py:367
  152.4 0.2 shard_map.118.density_ref
  152.6 1.2 shard_map.119
  153.7 6.3 %all-to-all-start.5 = ((bf16[32,64,128]{2,1,0:T(8,128)(2,1)}), bf16[32,64,128]{2,1,0:T(8,128)(2,1)S(1)}, u32[]{:S(2)}, u32[]{:S(2)}) async-start(bf16[32,64,128]{2,1,0:T(8,128)(2,1)} %shard_map.119), calls=%async_computation.5 | async-start | bytes 1048576 | tf_op jit(solution)/shard_map/all_to_all | solution.py:385
  160.0 0.6 copy.16
  160.7 13.4 %all-to-all-done.5 = bf16[32,64,128]{2,1,0:T(8,128)(2,1)S(1)} async-done(((bf16[32,64,128]{2,1,0:T(8,128)(2,1)}), bf16[32,64,128]{2,1,0:T(8,128)(2,1)S(1)}, u32[]{:S(2)}, u32[]{:S(2)}) %all-to-all-start.5) | async-done | bytes 524320 | tf_op jit(solution)/shard_map/all_to_all | solution.py:385
  174.1 1.1 shard_map.120
  (18 shorter events, 0.1 us)
Async XLA Ops:
  0.6 59.1 %copy-start.7 = (s32[32,1,9]{0,1,2:T(1,128)S(1)}, s32[32,1,9]{0,1,2:T(1,128)}, u32[]{:S(2)}) copy-start(s32[32,1,9]{0,1,2:T(1,128)} %param.19) | copy-start | bytes 3460
  0.6 59.3 %copy-start.1 = (s32[1,1024]{1,0:T(1,128)S(1)}, s32[1,1024]{1,0:T(1,128)}, u32[]{:S(2)}) copy-start(s32[1,1024]{1,0:T(1,128)} %plan_ref.1) | copy-start | bytes 12292
  11.7 1.0 copy-start
  12.7 47.2 %copy-start.6 = (f32[32,1,256]{2,1,0:T(1,128)S(1)}, f32[32,1,256]{2,1,0:T(1,128)}, u32[]{:S(2)}) copy-start(f32[32,1,256]{2,1,0:T(1,128)} %param.14) | copy-start | bytes 98308
  14.4 33.0 %all-to-all-start.1 = ((bf16[16,256,128]{2,1,0:T(8,128)(2,1)}), bf16[16,256,128]{2,1,0:T(8,128)(2,1)S(1)}, u32[]{:S(2)}, u32[]{:S(2)}) async-start(bf16[16,256,128]{2,1,0:T(8,128)(2,1)} %bitcast.6), calls=%async_computation.1 | async-start | bytes 2097152 | tf_op jit(solution)/shard_map/all_to_all | solution.py:285
  24.0 0.9 copy-start.2
  24.9 0.9 copy-start.3
  25.8 0.9 copy-start.4
  26.7 0.8 copy-start.5
  47.5 32.8 %all-to-all-start.2 = ((bf16[32,40,256]{2,1,0:T(8,128)(2,1)}), bf16[32,40,256]{2,1,0:T(8,128)(2,1)S(1)}, u32[]{:S(2)}, u32[]{:S(2)}) async-start(bf16[32,40,256]{2,1,0:T(8,128)(2,1)} %shard_map.116), calls=%async_computation.2 | async-start | bytes 1310720 | tf_op jit(solution)/shard_map/all_to_all | solution.py:321
  80.2 11.7 %all-to-all-start.3 = ((bf16[4,32,256]{2,1,0:T(8,128)(2,1)}), bf16[4,32,256]{2,1,0:T(8,128)(2,1)S(1)}, u32[]{:S(2)}, u32[]{:S(2)}) async-start(bf16[4,32,256]{2,1,0:T(8,128)(2,1)} %get-tuple-element.15), calls=%async_computation.3 | async-start | bytes 131072 | tf_op jit(solution)/shard_map/all_to_all | solution.py:338
  91.9 60.6 %all-to-all-start.4 = ((bf16[512,8,128]{2,1,0:T(8,128)(2,1)}), bf16[512,8,128]{2,1,0:T(8,128)(2,1)S(1)}, u32[]{:S(2)}, u32[]{:S(2)}) async-start(bf16[512,8,128]{2,1,0:T(8,128)(2,1)} %bitcast.9), calls=%async_computation.4 | async-start | bytes 2097152 | tf_op jit(solution)/shard_map/all_to_all | solution.py:360
  153.7 20.3 %all-to-all-start.5 = ((bf16[32,64,128]{2,1,0:T(8,128)(2,1)}), bf16[32,64,128]{2,1,0:T(8,128)(2,1)S(1)}, u32[]{:S(2)}, u32[]{:S(2)}) async-start(bf16[32,64,128]{2,1,0:T(8,128)(2,1)} %shard_map.119), calls=%async_computation.5 | async-start | bytes 1048576 | tf_op jit(solution)/shard_map/all_to_all | solution.py:385

commit v9 on v5

--- a/solution.py
+++ b/solution.py
@@ -109,16 +109,10 @@
             out_ref[s, j * lanes : (j + 1) * lanes, :] = value.astype(bf16)
 
 
-def pick_kernel(asked_ref, blocks_ref, out_ref, sems):
+def pick_kernel(asked_ref, blocks_ref, out_ref):
     per_owner = asked_ref.shape[2]
-    copies = []
     for e in range(out_ref.shape[0]):
-        place = asked_ref[e // per_owner, 0, e % per_owner]
-        copies.append(pltpu.make_async_copy(blocks_ref.at[place], out_ref.at[e], sems.at[e]))
-    for copy in copies:
-        copy.start()
-    for copy in copies:
-        copy.wait()
+        out_ref[e] = blocks_ref[asked_ref[e // per_owner, 0, e % per_owner]]
 
 
 def spread_kernel(hartree_ref, listed_ref, done_ref, out_ref):
@@ -168,7 +162,7 @@
     total = rho_ref.shape[0]
     entries, block, _ = sums_ref.shape
     stride = hartree_ref.shape[1]
-    unroll = 2
+    unroll = slots
     start = pl.program_id(0) * slots
 
     @pl.when(start == 0)
@@ -283,10 +277,7 @@
     sent = call(
         pick_kernel,
         jax.ShapeDtypeStruct((entries, block, block), bf16),
-        [SMEM, HBM],
-        [pltpu.SemaphoreType.DMA((entries,))],
-        out_specs=HBM,
-        limit=60,
+        [SMEM, VMEM],
         moved=entries * block * block * 4,
     )(asked, density_blocks)
     table = lax.all_to_all(
@@ -345,19 +336,20 @@
     spread = lax.all_to_all(copies, "batch", split_axis=0, concat_axis=0, tiled=True).reshape(
         ranks * slots, grid
     )
+    wide = min(8, slots)
     partial, lists = call(
         matrix_kernel,
         (
             jax.ShapeDtypeStruct((ranks // 2, 2, columns, per_owner * piece, block), bf16),
             jax.ShapeDtypeStruct((ranks, block), f32),
         ),
-        [SMEM, SMEM, rows_of(group, width, grid), VMEM, VMEM, VMEM],
+        [SMEM, SMEM, rows_of(wide, width, grid), VMEM, VMEM, VMEM],
         [
             pltpu.VMEM((entries, block, block), f32),
             pltpu.VMEM((slots, grid), f32),
             pltpu.VMEM((ranks * stride, grid), f32),
         ],
-        grid=steps,
+        grid=(slots // wide,),
         limit=48,
         flops=slots * width * width * grid * 2,
         moved=slots * width * grid * 2,

time: 206 us -> 174 us (0.84)
  Pallas kernels: 67.4 us -> 32.3 us
  waiting for transfers between devices: 76.4 us -> 79.1 us
    pallas_call x1, Pallas kernels: 34.1 us -> 1.71 us  [on_device(): call(pick_kernel, jax.ShapeDtypeStruct((entries, block, block), bf16), [S...]
    pallas_call x1, Pallas kernels: 10.4 us -> 7.73 us  [on_device(): call(matrix_kernel, (jax.ShapeDtypeStruct((ranks // 2, 2, columns, per_ow...]
    all_to_all x1, waiting for transfers between devices: 6.53 us -> 9.22 us  [on_device(): lax.all_to_all(copies, 'batch', split_axis=0, concat_axis=0, tiled=True)]
  transfers between devices with their start and end apart: 5 -> 5, of which waited for: 5 -> 5; matrix products, arithmetic and copies ran while one was open for 1% -> 1% of each run, Pallas kernels for 15% -> 16%
where the time goes in v9:
time: 174 us; the launch traced here: 173 us
  waiting for transfers between devices  79.1 us (45%)
  starting transfers between devices  39 us (22%)
  Pallas kernels  32.3 us (19%)
  blocking collectives  14.5 us (8%)
  local copies, waits for them, and re-layouts  7.51 us (4%)
    all_to_all x1, waiting for transfers between devices, on_device(): lax.all_to_all(partial.reshape(ranks * columns, rows, block), ('batch', '...  32.1 us
    all_to_all x1, waiting for transfers between devices, on_device(): lax.all_to_all(totals, 'batch', split_axis=0, concat_axis=0, tiled=True)  17.3 us
    all_to_all x1, blocking collectives, on_device(): lax.all_to_all(wanted, 'blk', split_axis=0, concat_axis=0, tiled=True)  14.5 us
    all_to_all x1, starting transfers between devices, on_device(): lax.all_to_all(lines, 'batch', split_axis=0, concat_axis=0, tiled=True)  12.3 us
    all_to_all x1, starting transfers between devices, on_device(): lax.all_to_all(partial.reshape(ranks * columns, rows, block), ('batch', '...  11.9 us
    all_to_all x1, waiting for transfers between devices, on_device(): lax.all_to_all(lines, 'batch', split_axis=0, concat_axis=0, tiled=True)  10.9 us
    pallas_call x1, Pallas kernels, on_device(): call(basis_kernel, (jax.ShapeDtypeStruct((slots, width, grid), bf16), jax...  9.83 us
    pallas_call x1, Pallas kernels, on_device(): call(density_kernel, (jax.ShapeDtypeStruct((slots, grid), f32), jax.Shape...  9.67 us
  transfers between devices with their start and end apart: 5, of which 5 were waited for; matrix products, arithmetic and copies ran while one was open for 1% of the time, Pallas kernels for 16%

profile of v9, /device:TPU:8, one launch (start us, length us, event | category | flops | bytes accessed | tf_op | source)
XLA Modules:
  0.0 173.3 jit_solution(8642457975201184633)
XLA Ops:
  0.6 0.8 copy.15
  1.4 14.5 %all_to_all.30.asked_ref = s32[16,1,2]{2,1,0:T(1,128)S(1)} all-to-all(s32[16,1,2]{2,1,0:T(1,128)S(1)} %copy.15), channel_id=1, replica_groups=mesh['batch'=32,'blk'=16] {'blk'}, dimensions={0} | all-to-all | bytes 256 | tf_op jit(solution)/shard_map/all_to_all | solution.py:276
  15.9 1.0 copy-done
  16.9 1.7 shard_map.114
  18.6 4.9 %all-to-all-start.1 = ((bf16[16,256,128]{2,1,0:T(8,128)(2,1)}), bf16[16,256,128]{2,1,0:T(8,128)(2,1)S(1)}, u32[]{:S(2)}, u32[]{:S(2)}) async-start(bf16[16,256,128]{2,1,0:T(8,128)(2,1)} %bitcast.6), calls=%async_computation.1 | async-start | bytes 2097152 | tf_op jit(solution)/shard_map/all_to_all | solution.py:283
  23.5 0.8 copy.22
  24.3 0.9 copy-done.2
  25.2 0.9 copy-done.3
  26.1 0.9 copy-done.4
  27.0 0.8 copy-done.5
  27.8 9.8 %shard_map.113 = (bf16[32,384,256]{2,1,0:T(8,128)(2,1)}, f32[8,128]{1,0:T(8,128)S(1)}) custom-call(f32[192,128]{1,0:T(8,128)S(1)} %bitcast.32, f32[288,128]{1,0:T(8,128)S(1)} %bitcast.30, f32[96,128]{1,0:T(8,128)S(1)} %bitcast.33, f32[288,128]{1,0:T(8,128)S(1)} %bitcast.31), custom_call_target="tpu_custom_call" | custom-call | flops 1258291200 | bytes 6291456 | tf_op jit(solution)/shard_map/pallas_call | solution.py:289
  37.7 0.1 convert_element_type.20
  37.8 0.9 shard_map.116
  38.7 9.6 %all-to-all-done.1 = bf16[16,256,128]{2,1,0:T(8,128)(2,1)S(1)} async-done(((bf16[16,256,128]{2,1,0:T(8,128)(2,1)}), bf16[16,256,128]{2,1,0:T(8,128)(2,1)S(1)}, u32[]{:S(2)}, u32[]{:S(2)}) %all-to-all-start.1) | async-done | bytes 1048608 | tf_op jit(solution)/shard_map/all_to_all | solution.py:283
  48.3 12.3 %all-to-all-start.2 = ((bf16[32,40,256]{2,1,0:T(8,128)(2,1)}), bf16[32,40,256]{2,1,0:T(8,128)(2,1)S(1)}, u32[]{:S(2)}, u32[]{:S(2)}) async-start(bf16[32,40,256]{2,1,0:T(8,128)(2,1)} %shard_map.116), calls=%async_computation.2 | async-start | bytes 1310720 | tf_op jit(solution)/shard_map/all_to_all | solution.py:319
  60.6 0.1 copy.14
  60.7 0.1 reshape.91.pairs_ref
  60.8 9.7 %shard_map.115 = (f32[32,256]{1,0:T(8,128)S(1)}, bf16[32,32,256]{2,1,0:T(8,128)(2,1)}) custom-call(s32[288]{0:T(512)S(1)} %reshape.91.pairs_ref, bf16[32,384,256]{2,1,0:T(8,128)(2,1)} %get-tuple-element.10.basis_ref, bf16[32,128,128]{2,1,0:T(8,128)(2,1)S(1)} %bitcast.26), custom_call_target="tpu_custom_call" | custom-call | flops 2415919104 | bytes 6291456 | tf_op jit(solution)/shard_map/pallas_call | solution.py:323
  70.4 10.9 %all-to-all-done.2.hartree_ref = bf16[32,40,256]{2,1,0:T(8,128)(2,1)S(1)} async-done(((bf16[32,40,256]{2,1,0:T(8,128)(2,1)}), bf16[32,40,256]{2,1,0:T(8,128)(2,1)S(1)}, u32[]{:S(2)}, u32[]{:S(2)}) %all-to-all-start.2) | async-done | bytes 655392 | tf_op jit(solution)/shard_map/all_to_all | solution.py:319
  81.3 4.9 %all-to-all-start.3 = ((bf16[32,32,256]{2,1,0:T(8,128)(2,1)}), bf16[32,32,256]{2,1,0:T(8,128)(2,1)S(1)}, u32[]{:S(2)}, u32[]{:S(2)}) async-start(bf16[32,32,256]{2,1,0:T(8,128)(2,1)} %get-tuple-element.15), calls=%async_computation.3 | async-start | bytes 1048576 | tf_op jit(solution)/shard_map/all_to_all | solution.py:336
  86.4 7.7 %shard_map.117 = (bf16[16,2,16,8,128]{4,3,2,1,0:T(8,128)(2,1)}, f32[32,128]{1,0:T(8,128)S(1)}) custom-call(s32[288]{0:T(512)S(1)} %reshape.91.pairs_ref, s32[32]{0:T(128)S(1)} %dynamic-slice_bitcast_fusion.plan_ref, bf16[32,384,256]{2,1,0:T(8,128)(2,1)} %get-tuple-element.10.basis_ref, f32[32,256]{1,0:T(8,128)S(1)} %get-tuple-element.11.rho_ref, ...), custom_call_target="tpu_custom_call" | custom-call | flops 2415919104 | bytes 6291456 | tf_op jit(solution)/shard_map/pallas_call | solution.py:340
  94.1 9.2 %all-to-all-done.3 = bf16[32,32,256]{2,1,0:T(8,128)(2,1)S(1)} async-done(((bf16[32,32,256]{2,1,0:T(8,128)(2,1)}), bf16[32,32,256]{2,1,0:T(8,128)(2,1)S(1)}, u32[]{:S(2)}, u32[]{:S(2)}) %all-to-all-start.3) | async-done | bytes 524320 | tf_op jit(solution)/shard_map/all_to_all | solution.py:336
  103.3 11.9 %all-to-all-start.4 = ((bf16[512,8,128]{2,1,0:T(8,128)(2,1)}), bf16[512,8,128]{2,1,0:T(8,128)(2,1)S(1)}, u32[]{:S(2)}, u32[]{:S(2)}) async-start(bf16[512,8,128]{2,1,0:T(8,128)(2,1)} %bitcast.9), calls=%async_computation.4 | async-start | bytes 2097152 | tf_op jit(solution)/shard_map/all_to_all | solution.py:360
  115.3 0.2 iota_add_fusion
  115.5 0.3 add.32.target_ref
  115.9 32.1 %all-to-all-done.4 = bf16[512,8,128]{2,1,0:T(8,128)(2,1)S(1)} async-done(((bf16[512,8,128]{2,1,0:T(8,128)(2,1)}), bf16[512,8,128]{2,1,0:T(8,128)(2,1)S(1)}, u32[]{:S(2)}, u32[]{:S(2)}) %all-to-all-start.4) | async-done | bytes 1048608 | tf_op jit(solution)/shard_map/all_to_all | solution.py:360
  148.0 1.2 shard_map.118
  149.1 5.0 %all-to-all-start.5 = ((bf16[32,64,128]{2,1,0:T(8,128)(2,1)}), bf16[32,64,128]{2,1,0:T(8,128)(2,1)S(1)}, u32[]{:S(2)}, u32[]{:S(2)}) async-start(bf16[32,64,128]{2,1,0:T(8,128)(2,1)} %shard_map.118), calls=%async_computation.5 | async-start | bytes 1048576 | tf_op jit(solution)/shard_map/all_to_all | solution.py:384
  154.1 0.2 shard_map.120
  154.3 0.7 copy.16
  154.9 17.3 %all-to-all-done.5 = bf16[32,64,128]{2,1,0:T(8,128)(2,1)S(1)} async-done(((bf16[32,64,128]{2,1,0:T(8,128)(2,1)}), bf16[32,64,128]{2,1,0:T(8,128)(2,1)S(1)}, u32[]{:S(2)}, u32[]{:S(2)}) %all-to-all-start.5) | async-done | bytes 524320 | tf_op jit(solution)/shard_map/all_to_all | solution.py:384
  172.2 1.1 shard_map.119
  (17 shorter events, 0.2 us)
Async XLA Ops:
  0.6 59.9 %copy-start.7 = (s32[32,1,9]{0,1,2:T(1,128)S(1)}, s32[32,1,9]{0,1,2:T(1,128)}, u32[]{:S(2)}) copy-start(s32[32,1,9]{0,1,2:T(1,128)} %param.19) | copy-start | bytes 3460
  15.9 1.0 copy-start
  18.6 29.7 %all-to-all-start.1 = ((bf16[16,256,128]{2,1,0:T(8,128)(2,1)}), bf16[16,256,128]{2,1,0:T(8,128)(2,1)S(1)}, u32[]{:S(2)}, u32[]{:S(2)}) async-start(bf16[16,256,128]{2,1,0:T(8,128)(2,1)} %bitcast.6), calls=%async_computation.1 | async-start | bytes 2097152 | tf_op jit(solution)/shard_map/all_to_all | solution.py:283
  24.3 0.9 copy-start.2
  25.2 0.9 copy-start.3
  26.1 0.9 copy-start.4
  27.0 0.8 copy-start.5
  37.6 48.6 %copy-start.6 = (f32[32,1,256]{2,1,0:T(1,128)S(1)}, f32[32,1,256]{2,1,0:T(1,128)}, u32[]{:S(2)}) copy-start(f32[32,1,256]{2,1,0:T(1,128)} %param.14) | copy-start | bytes 98308
  37.6 48.6 %copy-start.1 = (s32[1,1024]{1,0:T(1,128)S(1)}, s32[1,1024]{1,0:T(1,128)}, u32[]{:S(2)}) copy-start(s32[1,1024]{1,0:T(1,128)} %plan_ref.1) | copy-start | bytes 12292
  48.3 33.1 %all-to-all-start.2 = ((bf16[32,40,256]{2,1,0:T(8,128)(2,1)}), bf16[32,40,256]{2,1,0:T(8,128)(2,1)S(1)}, u32[]{:S(2)}, u32[]{:S(2)}) async-start(bf16[32,40,256]{2,1,0:T(8,128)(2,1)} %shard_map.116), calls=%async_computation.2 | async-start | bytes 1310720 | tf_op jit(solution)/shard_map/all_to_all | solution.py:319
  81.3 21.9 %all-to-all-start.3 = ((bf16[32,32,256]{2,1,0:T(8,128)(2,1)}), bf16[32,32,256]{2,1,0:T(8,128)(2,1)S(1)}, u32[]{:S(2)}, u32[]{:S(2)}) async-start(bf16[32,32,256]{2,1,0:T(8,128)(2,1)} %get-tuple-element.15), calls=%async_computation.3 | async-start | bytes 1048576 | tf_op jit(solution)/shard_map/all_to_all | solution.py:336
  103.3 44.7 %all-to-all-start.4 = ((bf16[512,8,128]{2,1,0:T(8,128)(2,1)}), bf16[512,8,128]{2,1,0:T(8,128)(2,1)S(1)}, u32[]{:S(2)}, u32[]{:S(2)}) async-start(bf16[512,8,128]{2,1,0:T(8,128)(2,1)} %bitcast.9), calls=%async_computation.4 | async-start | bytes 2097152 | tf_op jit(solution)/shard_map/all_to_all | solution.py:360
  149.1 23.1 %all-to-all-start.5 = ((bf16[32,64,128]{2,1,0:T(8,128)(2,1)}), bf16[32,64,128]{2,1,0:T(8,128)(2,1)S(1)}, u32[]{:S(2)}, u32[]{:S(2)}) async-start(bf16[32,64,128]{2,1,0:T(8,128)(2,1)} %shard_map.118), calls=%async_computation.5 | async-start | bytes 1048576 | tf_op jit(solution)/shard_map/all_to_all | solution.py:384

commit v10 on v8

--- a/solution.py
+++ b/solution.py
@@ -118,11 +118,9 @@
 
 def spread_kernel(hartree_ref, listed_ref, done_ref, out_ref):
     del done_ref
-    _, rows, grid = out_ref.shape
+    rows, grid = out_ref.shape
     below = jnp.broadcast_to(listed_ref[...], (rows - hartree_ref.shape[0], grid))
-    lines = jnp.concatenate([hartree_ref[...] - zero_exchange, below]).astype(bf16)
-    for h in range(out_ref.shape[0]):
-        out_ref[h] = lines
+    out_ref[...] = jnp.concatenate([hartree_ref[...] - zero_exchange, below]).astype(bf16)
 
 
 def density_kernel(pairs_ref, basis_ref, table_ref, rho_ref, copies_ref, sub_ref):
@@ -215,8 +213,7 @@
             out_ref[:, 1, c] = jnp.where(low, pltpu.roll(first, 4, 1), second).astype(bf16)
 
 
-def add_kernel(target_ref, received_ref, density_ref, out_ref):
-    del density_ref
+def add_kernel(target_ref, received_ref, out_ref):
     rows = out_ref.shape[1]
     length = target_ref.shape[1]
     chosen = lax.broadcasted_iota(jnp.int32, (rows, length), 0) == target_ref[...]
@@ -311,14 +308,18 @@
     stride = slots + 8
     lines = call(
         spread_kernel,
-        jax.ShapeDtypeStruct((ranks, stride, grid), bf16),
+        jax.ShapeDtypeStruct((stride, grid), bf16),
         [VMEM, VMEM, HBM],
     )(
         hartree[:, 0],
         jnp.pad(asked.reshape(1, entries).astype(f32), ((0, 0), (0, grid - entries))),
         done,
     )
-    stored = lax.all_to_all(lines, BATCH, split_axis=0, concat_axis=0, tiled=True)
+    lines = lax.all_gather(lines, "x", axis=0, tiled=True)
+    planes = lax.axis_size("z")
+    stored = lax.all_to_all(
+        jnp.broadcast_to(lines[None], (planes,) + lines.shape), "z", split_axis=0, concat_axis=0, tiled=True
+    ).reshape(ranks, stride, grid)
 
     pairs = batch_pairs.reshape(slots * LIST * LIST)
     unroll = 2
@@ -326,7 +327,7 @@
         density_kernel,
         (
             jax.ShapeDtypeStruct((slots, grid), f32),
-            jax.ShapeDtypeStruct((lax.axis_size("x"), slots, grid), bf16),
+            jax.ShapeDtypeStruct((ranks, slots, grid), bf16),
         ),
         [SMEM, rows_of(group, width, grid), VMEM],
         [pltpu.VMEM((unroll, width, width), bf16)],
@@ -335,7 +336,9 @@
         flops=slots * width * width * grid * 2,
         moved=slots * width * grid * 2,
     )(pairs, basis, table)
-    near = lax.all_to_all(copies, "x", split_axis=0, concat_axis=0, tiled=True).reshape(-1, grid)
+    spread = lax.all_to_all(copies, BATCH, split_axis=0, concat_axis=0, tiled=True).reshape(
+        ranks * slots, grid
+    )
     wide = min(8, slots)
     partial, lists = call(
         matrix_kernel,
@@ -356,7 +359,7 @@
     )(pairs, plan_rows, basis, rho, stored, grid_weights[:, 0])
 
     rows = per_owner * piece
-    partial, near = lax.optimization_barrier((partial, near))
+    partial, spread = lax.optimization_barrier((partial, spread))
     received = lax.all_to_all(
         partial.reshape(ranks * columns, rows, block),
         BATCH + ("blk",),
@@ -364,7 +367,6 @@
         concat_axis=0,
         tiled=True,
     ).reshape(ranks * columns * rows, block)
-    spread = lax.all_gather(near, "z", axis=0, tiled=True)
     density = call(
         place_kernel,
         jax.ShapeDtypeStruct((slots, grid), f32),
@@ -379,9 +381,9 @@
     totals = call(
         add_kernel,
         jax.ShapeDtypeStruct((ranks, held * piece, block), bf16),
-        [VMEM, VMEM, HBM],
+        [VMEM, VMEM],
         moved=ranks * columns * rows * block * 2,
-    )(targets, received, density)
+    )(targets, received)
     gathered = lax.all_to_all(totals, BATCH, split_axis=0, concat_axis=0, tiled=True)
     hamiltonian = call(
         merge_kernel,

time: 176 us -> 173 us (0.983)
  the two profiles are of different devices: /device:TPU:32 before, /device:TPU:8 now
where the time goes in v10:
time: 173 us; the launch traced here: 172 us
  waiting for transfers between devices  68.9 us (40%)
  starting transfers between devices  35.6 us (21%)
  Pallas kernels  31.4 us (18%)
  blocking collectives  26.4 us (15%)
  local copies, waits for them, and re-layouts  8.39 us (5%)
    all_to_all x1, waiting for transfers between devices, on_device(): lax.all_to_all(partial.reshape(ranks * columns, rows, block), BATCH + ('b...  32 us
    all_to_all x1, waiting for transfers between devices, on_device(): lax.all_to_all(totals, BATCH, split_axis=0, concat_axis=0, tiled=True)  17.3 us
    all_to_all x1, blocking collectives, on_device(): lax.all_to_all(wanted, 'blk', split_axis=0, concat_axis=0, tiled=True)  14.5 us
    all_gather x1, blocking collectives, on_device(): lines = lax.all_gather(lines, 'x', axis=0, tiled=True)  11.9 us
    all_to_all x1, starting transfers between devices, on_device(): lax.all_to_all(partial.reshape(ranks * columns, rows, block), BATCH + ('b...  11.6 us
    all_to_all x1, waiting for transfers between devices, on_device(): lax.all_to_all(copies, BATCH, split_axis=0, concat_axis=0, tiled=True)  10.1 us
    pallas_call x1, Pallas kernels, on_device(): call(basis_kernel, (jax.ShapeDtypeStruct((slots, width, grid), bf16), jax...  9.83 us
    all_to_all x1, starting transfers between devices, on_device(): lax.all_to_all(jnp.broadcast_to(lines[None], (planes,) + lines.shape), 'z...  9.76 us
  transfers between devices with their start and end apart: 5, of which 4 were waited for; matrix products, arithmetic and copies ran while one was open for 1% of the time, Pallas kernels for 16%

profile of v10, /device:TPU:8, one launch (start us, length us, event | category | flops | bytes accessed | tf_op | source)
XLA Modules:
  0.0 171.6 jit_solution(6423919888467698724)
XLA Ops:
  0.6 0.8 copy.15
  1.4 14.5 %all_to_all.30.asked_ref = s32[16,1,2]{2,1,0:T(1,128)S(1)} all-to-all(s32[16,1,2]{2,1,0:T(1,128)S(1)} %copy.15), channel_id=1, replica_groups=mesh['z'=8,'x'=4,'blk'=16] {'blk'}, dimensions={0} | all-to-all | bytes 256 | tf_op jit(solution)/shard_map/all_to_all | solution.py:275
  15.9 1.0 copy-done
  16.9 1.7 shard_map.114
  18.6 4.9 %all-to-all-start.1 = ((bf16[16,256,128]{2,1,0:T(8,128)(2,1)}), bf16[16,256,128]{2,1,0:T(8,128)(2,1)S(1)}, u32[]{:S(2)}, u32[]{:S(2)}) async-start(bf16[16,256,128]{2,1,0:T(8,128)(2,1)} %bitcast.6), calls=%async_computation.1 | async-start | bytes 2097152 | tf_op jit(solution)/shard_map/all_to_all | solution.py:282
  23.5 0.8 copy.22
  24.3 0.9 copy-done.2
  25.2 0.9 copy-done.3
  26.1 0.9 copy-done.4
  27.0 0.8 copy-done.5
  27.8 9.8 %shard_map.113 = (bf16[32,384,256]{2,1,0:T(8,128)(2,1)}, f32[8,128]{1,0:T(8,128)S(1)}) custom-call(f32[192,128]{1,0:T(8,128)S(1)} %bitcast.34, f32[288,128]{1,0:T(8,128)S(1)} %bitcast.32, f32[96,128]{1,0:T(8,128)S(1)} %bitcast.35, f32[288,128]{1,0:T(8,128)S(1)} %bitcast.33), custom_call_target="tpu_custom_call" | custom-call | flops 1258291200 | bytes 6291456 | tf_op jit(solution)/shard_map/pallas_call | solution.py:288
  37.7 0.1 convert_element_type.20
  37.8 11.9 %all_gather.3 = bf16[160,256]{1,0:T(8,128)(2,1)S(1)} all-gather(bf16[40,256]{1,0:T(8,128)(2,1)S(1)} %shard_map.116), channel_id=1, replica_groups=mesh['z'=8,'x'=4,'blk'=16] {'x'}, dimensions={0}, use_global_device_ids=true | all-gather | bytes 102400 | tf_op jit(solution)/shard_map/all_gather | solution.py:318
  49.7 0.9 broadcast_in_dim.4
  50.6 9.8 %all-to-all-start.2 = ((bf16[8,160,256]{2,1,0:T(8,128)(2,1)}), bf16[8,160,256]{2,1,0:T(8,128)(2,1)S(1)}, u32[]{:S(2)}, u32[]{:S(2)}) async-start(bf16[8,160,256]{2,1,0:T(8,128)(2,1)} %broadcast_in_dim.4), calls=%async_computation.2 | async-start | bytes 1310720 | tf_op jit(solution)/shard_map/all_to_all | solution.py:320
  60.3 0.1 copy.14
  60.4 0.1 reshape.95.pairs_ref
  60.5 9.7 %shard_map.115 = (f32[32,256]{1,0:T(8,128)S(1)}, bf16[32,32,256]{2,1,0:T(8,128)(2,1)}) custom-call(s32[288]{0:T(512)S(1)} %reshape.95.pairs_ref, bf16[32,384,256]{2,1,0:T(8,128)(2,1)} %get-tuple-element.10.basis_ref, bf16[32,128,128]{2,1,0:T(8,128)(2,1)S(1)} %bitcast.27), custom_call_target="tpu_custom_call" | custom-call | flops 2415919104 | bytes 6291456 | tf_op jit(solution)/shard_map/pallas_call | solution.py:326
  70.2 9.4 %all-to-all-done.2 = bf16[8,160,256]{2,1,0:T(8,128)(2,1)S(1)} async-done(((bf16[8,160,256]{2,1,0:T(8,128)(2,1)}), bf16[8,160,256]{2,1,0:T(8,128)(2,1)S(1)}, u32[]{:S(2)}, u32[]{:S(2)}) %all-to-all-start.2) | async-done | bytes 655392 | tf_op jit(solution)/shard_map/all_to_all | solution.py:320
  79.6 4.4 %all-to-all-start.3 = ((bf16[32,32,256]{2,1,0:T(8,128)(2,1)}), bf16[32,32,256]{2,1,0:T(8,128)(2,1)S(1)}, u32[]{:S(2)}, u32[]{:S(2)}) async-start(bf16[32,32,256]{2,1,0:T(8,128)(2,1)} %get-tuple-element.15), calls=%async_computation.3 | async-start | bytes 1048576 | tf_op jit(solution)/shard_map/all_to_all | solution.py:339
  84.2 7.7 %shard_map.117 = (bf16[16,2,16,8,128]{4,3,2,1,0:T(8,128)(2,1)}, f32[32,128]{1,0:T(8,128)S(1)}) custom-call(s32[288]{0:T(512)S(1)} %reshape.95.pairs_ref, s32[32]{0:T(128)S(1)} %dynamic-slice_bitcast_fusion.plan_ref, bf16[32,384,256]{2,1,0:T(8,128)(2,1)} %get-tuple-element.10.basis_ref, f32[32,256]{1,0:T(8,128)S(1)} %get-tuple-element.11.rho_ref, ...), custom_call_target="tpu_custom_call" | custom-call | flops 2415919104 | bytes 6291456 | tf_op jit(solution)/shard_map/pallas_call | solution.py:343
  91.9 10.1 %all-to-all-done.3 = bf16[32,32,256]{2,1,0:T(8,128)(2,1)S(1)} async-done(((bf16[32,32,256]{2,1,0:T(8,128)(2,1)}), bf16[32,32,256]{2,1,0:T(8,128)(2,1)S(1)}, u32[]{:S(2)}, u32[]{:S(2)}) %all-to-all-start.3) | async-done | bytes 524320 | tf_op jit(solution)/shard_map/all_to_all | solution.py:339
  102.0 11.6 %all-to-all-start.4 = ((bf16[512,8,128]{2,1,0:T(8,128)(2,1)}), bf16[512,8,128]{2,1,0:T(8,128)(2,1)S(1)}, u32[]{:S(2)}, u32[]{:S(2)}) async-start(bf16[512,8,128]{2,1,0:T(8,128)(2,1)} %bitcast.10), calls=%async_computation.4 | async-start | bytes 2097152 | tf_op jit(solution)/shard_map/all_to_all | solution.py:363
  113.7 0.2 iota_add_fusion
  113.9 0.3 add.36.target_ref
  114.3 32.0 %all-to-all-done.4 = bf16[512,8,128]{2,1,0:T(8,128)(2,1)S(1)} async-done(((bf16[512,8,128]{2,1,0:T(8,128)(2,1)}), bf16[512,8,128]{2,1,0:T(8,128)(2,1)S(1)}, u32[]{:S(2)}, u32[]{:S(2)}) %all-to-all-start.4) | async-done | bytes 1048608 | tf_op jit(solution)/shard_map/all_to_all | solution.py:363
  146.2 1.2 shard_map.118
  147.4 5.0 %all-to-all-start.5 = ((bf16[32,64,128]{2,1,0:T(8,128)(2,1)}), bf16[32,64,128]{2,1,0:T(8,128)(2,1)S(1)}, u32[]{:S(2)}, u32[]{:S(2)}) async-start(bf16[32,64,128]{2,1,0:T(8,128)(2,1)} %shard_map.118), calls=%async_computation.5 | async-start | bytes 1048576 | tf_op jit(solution)/shard_map/all_to_all | solution.py:387
  152.4 0.2 shard_map.120
  152.6 0.7 copy.16
  153.2 17.3 %all-to-all-done.5 = bf16[32,64,128]{2,1,0:T(8,128)(2,1)S(1)} async-done(((bf16[32,64,128]{2,1,0:T(8,128)(2,1)}), bf16[32,64,128]{2,1,0:T(8,128)(2,1)S(1)}, u32[]{:S(2)}, u32[]{:S(2)}) %all-to-all-start.5) | async-done | bytes 524320 | tf_op jit(solution)/shard_map/all_to_all | solution.py:387
  170.5 1.1 shard_map.119
  (19 shorter events, 0.2 us)
Async XLA Ops:
  0.6 59.7 %copy-start.7 = (s32[32,1,9]{0,1,2:T(1,128)S(1)}, s32[32,1,9]{0,1,2:T(1,128)}, u32[]{:S(2)}) copy-start(s32[32,1,9]{0,1,2:T(1,128)} %param.19) | copy-start | bytes 3460
  15.9 1.0 copy-start
  18.6 31.1 %all-to-all-start.1 = ((bf16[16,256,128]{2,1,0:T(8,128)(2,1)}), bf16[16,256,128]{2,1,0:T(8,128)(2,1)S(1)}, u32[]{:S(2)}, u32[]{:S(2)}) async-start(bf16[16,256,128]{2,1,0:T(8,128)(2,1)} %bitcast.6), calls=%async_computation.1 | async-start | bytes 2097152 | tf_op jit(solution)/shard_map/all_to_all | solution.py:282
  24.3 0.9 copy-start.2
  25.2 0.9 copy-start.3
  26.1 0.9 copy-start.4
  27.0 0.8 copy-start.5
  37.6 46.4 %copy-start.6 = (f32[32,1,256]{2,1,0:T(1,128)S(1)}, f32[32,1,256]{2,1,0:T(1,128)}, u32[]{:S(2)}) copy-start(f32[32,1,256]{2,1,0:T(1,128)} %param.14) | copy-start | bytes 98308
  37.6 46.4 %copy-start.1 = (s32[1,1024]{1,0:T(1,128)S(1)}, s32[1,1024]{1,0:T(1,128)}, u32[]{:S(2)}) copy-start(s32[1,1024]{1,0:T(1,128)} %plan_ref.1) | copy-start | bytes 12292
  50.6 29.1 %all-to-all-start.2 = ((bf16[8,160,256]{2,1,0:T(8,128)(2,1)}), bf16[8,160,256]{2,1,0:T(8,128)(2,1)S(1)}, u32[]{:S(2)}, u32[]{:S(2)}) async-start(bf16[8,160,256]{2,1,0:T(8,128)(2,1)} %broadcast_in_dim.4), calls=%async_computation.2 | async-start | bytes 1310720 | tf_op jit(solution)/shard_map/all_to_all | solution.py:320
  79.6 22.4 %all-to-all-start.3 = ((bf16[32,32,256]{2,1,0:T(8,128)(2,1)}), bf16[32,32,256]{2,1,0:T(8,128)(2,1)S(1)}, u32[]{:S(2)}, u32[]{:S(2)}) async-start(bf16[32,32,256]{2,1,0:T(8,128)(2,1)} %get-tuple-element.15), calls=%async_computation.3 | async-start | bytes 1048576 | tf_op jit(solution)/shard_map/all_to_all | solution.py:339
  102.0 44.2 %all-to-all-start.4 = ((bf16[512,8,128]{2,1,0:T(8,128)(2,1)}), bf16[512,8,128]{2,1,0:T(8,128)(2,1)S(1)}, u32[]{:S(2)}, u32[]{:S(2)}) async-start(bf16[512,8,128]{2,1,0:T(8,128)(2,1)} %bitcast.10), calls=%async_computation.4 | async-start | bytes 2097152 | tf_op jit(solution)/shard_map/all_to_all | solution.py:363
  147.4 23.1 %all-to-all-start.5 = ((bf16[32,64,128]{2,1,0:T(8,128)(2,1)}), bf16[32,64,128]{2,1,0:T(8,128)(2,1)S(1)}, u32[]{:S(2)}, u32[]{:S(2)}) async-start(bf16[32,64,128]{2,1,0:T(8,128)(2,1)} %shard_map.118), calls=%async_computation.5 | async-start | bytes 1048576 | tf_op jit(solution)/shard_map/all_to_all | solution.py:387
